TPU v7x, 32 devices: a whole 2x2x4 slice. The times are simulated.
32 devices in a mesh: expert: 8 (over z, y), tensor: 4 (over x, core).
Axes of the slice: x: 2, y: 2, z: 4, core: 2. Of those that a mesh axis runs over, the one named last changes fastest.
Arguments:
- tokens: bfloat16 [8192, 768], P('expert'), may hold values from -6 to 6
- cotangent: bfloat16 [8192, 768], P('expert'), may hold values from -6 to 6
- gain_attn: bfloat16 [768], replicated, may hold values from 0.099609375 to 1.8984375
- gain_ffn: bfloat16 [768], replicated, may hold values from 0.099609375 to 1.8984375
- w_qkv: bfloat16 [3, 768, 768], P(None, None, 'tensor'), may hold values from -0.21875 to 0.21875
- w_out: bfloat16 [768, 768], P('tensor'), may hold values from -0.875 to 0.875
- bias_table: bfloat16 [32, 12], P(None, 'tensor'), may hold values from -4 to 4
- router: bfloat16 [768, 8], replicated, may hold values from -0.15625 to 0.15625
- w_in: bfloat16 [8, 768, 3072], P('expert', None, 'tensor'), may hold values from -0.21875 to 0.21875
- w_down: bfloat16 [8, 3072, 768], P('expert', 'tensor'), may hold values from -0.109375 to 0.109375
- routes: int32 [8192, 2], P('expert'), may hold values from 0 to 7, all different within a row; in each aligned block of 1024 rows (0 to 1023, 1024 to 2047, ...) at most 512 rows name the same one
- sequence_ids: int32 [8192], P('expert'), may hold values from 0 to 1023, as said below
- rel_buckets: int32 [1024], replicated, may hold values from 0 to 31, as said below
Outputs:
- output_rows: bfloat16 [8192, 768], P('expert')
- d_tokens: bfloat16 [8192, 768], P('expert')
- d_gain_attn: float32 [768], replicated
- d_gain_ffn: float32 [768], replicated
- d_qkv: float32 [3, 768, 768], P(None, None, 'tensor')
- d_out: float32 [768, 768], P('tensor')
- d_bias: float32 [32, 12], P(None, 'tensor')
- d_router: float32 [768, 8], replicated
- d_w_in: float32 [8, 768, 3072], P('expert', None, 'tensor')
- d_w_down: float32 [8, 3072, 768], P('expert', 'tensor')
Inputs may be any that keep to these rules, and one draw needn't show every extreme that they name: `routes`: each token names two different experts. Among the 1024 tokens of one device no expert is named more than 512 times, and in every draw some expert is named exactly 512 times by one device's tokens. `sequence_ids`: on each device the numbers of its 1024 tokens start at 0 and never fall, and may skip values; equal numbers on one device form one sequence. On some device all 1024 tokens form one sequence; on some device the last token alone has the number 1024 - 1. `rel_buckets`: entry d is the bucket of a key d positions before its query; it is 0 at d = 0, never falls, and is 31 at d = 1023.
All inputs are finite; a program needn't handle non-finite values.
Results may differ from a plain program's by a relative error of at most 0.018.
Values may be sent and summed in bfloat16 or wider, within the bound.
No kernel may reach another device: no remote copies, remote signals or barrier semaphores. Data moves between devices by JAX's collectives and lax.ppermute only.
A program may use at most 192 MiB of HBM per device.

v0:
```python
import jax
import jax.numpy as jnp
from jax import lax
from jax.sharding import PartitionSpec as P

EPSILON = 1e-06
PRECISE = lax.Precision.HIGHEST
FLOOR_SCORE = -1e30


def cross_rows(left, right, precision=None):
    return lax.dot_general(
        left,
        right,
        (((0,), (0,)), ((), ())),
        precision=precision,
        preferred_element_type=jnp.float32,
    )


def cross_cols(left, right, precision=None):
    return lax.dot_general(
        left,
        right,
        (((1,), (1,)), ((), ())),
        precision=precision,
        preferred_element_type=jnp.float32,
    )


def normalize(values, gain_vec):
    scale_rows = lax.rsqrt(jnp.mean(values * values, axis=-1, keepdims=True) + EPSILON)
    plain_rows = values * scale_rows
    return (plain_rows, scale_rows, plain_rows * gain_vec)


def norm_back(grad_in, plain_rows, scale_rows, gain_vec):
    gain_grad = jnp.sum(grad_in * plain_rows, axis=0)
    inner_grad = grad_in * gain_vec
    spread_grad = scale_rows * (
        inner_grad - plain_rows * jnp.mean(inner_grad * plain_rows, axis=-1, keepdims=True)
    )
    return (spread_grad, gain_grad)


def spread_bias(reversed_table, row_start, block_rows, length):
    line_width = block_rows + length
    distance_line = lax.slice_in_dim(
        reversed_table, length - row_start - block_rows, length - row_start + length + 1, axis=1
    )
    head_count = distance_line.shape[0]
    tiled_line = jnp.tile(distance_line, (1, block_rows))[:, : block_rows * line_width]
    return tiled_line.reshape(head_count, block_rows, line_width)[:, :, block_rows:]


def fold_distances(block_grad):
    head_count, block_rows, length = block_grad.shape
    line_width = block_rows + length
    padded = jnp.pad(block_grad, ((0, 0), (0, 0), (block_rows, 0))).reshape(
        head_count, block_rows * line_width
    )
    padded = jnp.pad(padded, ((0, 0), (0, block_rows)))
    return jnp.sum(padded.reshape(head_count, block_rows, line_width + 1), axis=1)


def pick_slots(buffer, flat_experts, slot_index, first_slot, slot_count):
    local_slot = slot_index - first_slot
    inside = ((local_slot >= 0) & (local_slot < slot_count)).astype(jnp.float32)
    rows = buffer[flat_experts, 0, jnp.clip(local_slot, 0, slot_count - 1)].astype(jnp.float32)
    return rows * inside[:, None]


def body(
    tokens,
    cotangent,
    gain_attn,
    gain_ffn,
    w_qkv,
    w_out,
    bias_table,
    router,
    w_in,
    w_down,
    routes,
    sequence_ids,
    rel_buckets,
):
    length, model_width = tokens.shape
    block_rows = min(512, length)
    head_count = bias_table.shape[1]
    head_size = w_qkv.shape[2] // head_count
    scale_factor = head_size ** (-0.5)
    bucket_count = bias_table.shape[0]
    experts = router.shape[1]
    capacity = 4 * length // experts
    sources = lax.axis_size("expert")
    tensor_size = lax.axis_size("tensor")
    share_rows = capacity // tensor_size
    inputs = tokens.astype(jnp.float32)
    gain_one = gain_attn.astype(jnp.float32)
    gain_two = gain_ffn.astype(jnp.float32)
    plain_one, scale_one, normed_one = normalize(inputs, gain_one)
    normed_low = normed_one.astype(jnp.bfloat16)
    projected = jnp.einsum(
        "td,cdh->cth", normed_low, w_qkv, preferred_element_type=jnp.float32
    ).astype(jnp.bfloat16)
    query_heads = projected[0].reshape(length, head_count, head_size)
    key_heads = projected[1].reshape(length, head_count, head_size)
    value_heads = projected[2].reshape(length, head_count, head_size)
    bucket_pick = (rel_buckets[:, None] == jnp.arange(bucket_count)[None, :]).astype(jnp.float32)
    by_distance = lax.dot_general(
        bias_table.astype(jnp.float32), bucket_pick, (((0,), (1,)), ((), ())), precision=PRECISE
    )
    reversed_table = jnp.pad(by_distance, ((0, 0), (length + 2, 1)))[:, ::-1]
    positions = jnp.arange(length)

    def block_scores(row_start):
        query_block = query_heads[row_start : row_start + block_rows]
        raw_scores = (
            jnp.einsum("rhk,jhk->hrj", query_block, key_heads, preferred_element_type=jnp.float32)
            * scale_factor
        )
        raw_scores = raw_scores + spread_bias(reversed_table, row_start, block_rows, length)
        block_ids = sequence_ids[row_start : row_start + block_rows]
        query_places = row_start + positions[:block_rows]
        allowed = (query_places[:, None] >= positions[None, :]) & (
            block_ids[:, None] == sequence_ids[None, :]
        )
        return (jnp.where(allowed[None], raw_scores, FLOOR_SCORE), query_block)

    starts = list(range(0, length, block_rows))
    log_totals = []
    mixed_blocks = []
    for row_start in starts:
        scores, query_block = block_scores(row_start)
        row_max = jnp.max(scores, axis=-1, keepdims=True)
        exp_scores = jnp.exp(scores - row_max)
        row_total = jnp.sum(exp_scores, axis=-1, keepdims=True)
        probs_low = (exp_scores / row_total).astype(jnp.bfloat16)
        mixed_blocks.append(
            jnp.einsum(
                "hrj,jhk->rhk", probs_low, value_heads, preferred_element_type=jnp.float32
            ).astype(jnp.bfloat16)
        )
        log_totals.append(row_max + jnp.log(row_total))
    mixed_flat = jnp.concatenate(mixed_blocks, axis=0).reshape(length, head_count * head_size)
    attention = lax.psum(jnp.dot(mixed_flat, w_out, preferred_element_type=jnp.float32), "tensor")
    middle = inputs + attention
    plain_two, scale_two, normed_two = normalize(middle, gain_two)
    normed_two_low = normed_two.astype(jnp.bfloat16)
    router_float = router.astype(jnp.float32)
    logits = jnp.dot(normed_two, router_float, precision=PRECISE)
    choose = (routes[:, :, None] == jnp.arange(experts)[None, None, :]).astype(jnp.float32)
    chosen = jnp.sum(logits[:, None, :] * choose, axis=-1)
    gate_values = jax.nn.softmax(chosen, axis=1)
    flat_experts = routes.reshape(-1)
    marks = (flat_experts[:, None] == jnp.arange(experts)[None, :]).astype(jnp.int32)
    slot_index = jnp.sum((jnp.cumsum(marks, axis=0) - 1) * marks, axis=1)
    token_index = jnp.arange(2 * length) // 2
    first_share = lax.axis_index("tensor") * share_rows

    def place_rows(values):
        empty_buffer = jnp.zeros((experts, 1, capacity, model_width), jnp.bfloat16)
        return empty_buffer.at[flat_experts, 0, slot_index].set(values)

    outgoing = place_rows(normed_two_low[token_index])
    arrived = lax.all_to_all(outgoing, "expert", split_axis=0, concat_axis=1, tiled=True)
    expert_rows = arrived.reshape(sources * capacity, model_width)
    hidden_pre = jnp.dot(expert_rows, w_in[0], preferred_element_type=jnp.float32)
    hidden_act = jax.nn.gelu(hidden_pre).astype(jnp.bfloat16)
    part_rows = jnp.dot(hidden_act, w_down[0], preferred_element_type=jnp.float32).astype(
        jnp.bfloat16
    )
    summed_parts = lax.psum_scatter(
        part_rows.astype(jnp.float32).reshape(sources, capacity, model_width).astype(jnp.bfloat16),
        "tensor",
        scatter_dimension=1,
        tiled=True,
    ).astype(jnp.float32)
    returned = lax.all_to_all(
        summed_parts.reshape(1, sources, share_rows, model_width).astype(jnp.bfloat16),
        "expert",
        split_axis=1,
        concat_axis=0,
        tiled=True,
    ).astype(jnp.float32)
    picked = pick_slots(returned, flat_experts, slot_index, first_share, share_rows).reshape(
        length, 2, model_width
    )
    expert_mix = lax.psum(
        jnp.sum(gate_values[:, :, None] * picked, axis=1).astype(jnp.bfloat16), "tensor"
    ).astype(jnp.float32)
    output_rows = (middle + expert_mix).astype(jnp.bfloat16)
    grad_output = cotangent.astype(jnp.float32)
    toward = (
        (gate_values[:, :, None] * grad_output[:, None, :])
        .astype(jnp.bfloat16)
        .reshape(2 * length, model_width)
    )
    outgoing_grad = place_rows(toward)
    arrived_grad = lax.all_to_all(outgoing_grad, "expert", split_axis=0, concat_axis=1, tiled=True)
    grad_rows = arrived_grad.reshape(sources * capacity, model_width)
    grad_act = cross_cols(grad_rows, w_down[0])
    gelu_value, gelu_back = jax.vjp(jax.nn.gelu, hidden_pre)
    grad_pre = gelu_back(grad_act)[0].astype(jnp.bfloat16)
    d_w_down = cross_rows(hidden_act, grad_rows)[None]
    d_w_in = cross_rows(expert_rows, grad_pre)[None]
    grad_share = cross_cols(grad_pre, w_in[0]).astype(jnp.bfloat16)
    summed_grads = lax.psum_scatter(
        grad_share.astype(jnp.float32).reshape(sources, capacity, model_width).astype(jnp.bfloat16),
        "tensor",
        scatter_dimension=1,
        tiled=True,
    ).astype(jnp.float32)
    came_back = lax.all_to_all(
        summed_grads.reshape(1, sources, share_rows, model_width),
        "expert",
        split_axis=1,
        concat_axis=0,
        tiled=True,
    )
    back_rows = pick_slots(came_back, flat_experts, slot_index, first_share, share_rows)
    grad_normed_part = jnp.sum(back_rows.reshape(length, 2, model_width), axis=1)
    gate_part = jnp.sum(picked * grad_output[:, None, :], axis=-1)
    grad_normed_two, gate_grad = lax.psum((grad_normed_part, gate_part), "tensor")
    mean_grad = jnp.sum(gate_values * gate_grad, axis=1, keepdims=True)
    select_grad = gate_values * (gate_grad - mean_grad)
    logit_grad = jnp.sum(select_grad[:, :, None] * choose, axis=1)
    d_router = cross_rows(normed_two, logit_grad, PRECISE)
    grad_normed_two = grad_normed_two + cross_cols(logit_grad, router_float, PRECISE)
    back_two, d_gain_ffn = norm_back(grad_normed_two, plain_two, scale_two, gain_two)
    grad_middle = grad_output + back_two
    grad_attn = grad_middle.astype(jnp.bfloat16)
    d_out = cross_rows(mixed_flat, grad_attn)
    grad_mixed = (
        cross_cols(grad_attn, w_out).astype(jnp.bfloat16).reshape(length, head_count, head_size)
    )
    grad_keys = jnp.zeros((length, head_count, head_size), jnp.float32)
    grad_values = jnp.zeros((length, head_count, head_size), jnp.float32)
    query_grads = []
    table_grad = jnp.zeros((head_count, 2 * length + 3), jnp.float32)
    for block_number, row_start in enumerate(starts):
        scores, query_block = block_scores(row_start)
        prob_rows = jnp.exp(scores - log_totals[block_number])
        grad_block = grad_mixed[row_start : row_start + block_rows]
        grad_values = grad_values + jnp.einsum(
            "hrj,rhk->jhk",
            prob_rows.astype(jnp.bfloat16),
            grad_block,
            preferred_element_type=jnp.float32,
        )
        grad_probs = jnp.einsum(
            "rhk,jhk->hrj", grad_block, value_heads, preferred_element_type=jnp.float32
        )
        inner_sums = jnp.sum(prob_rows * grad_probs, axis=-1, keepdims=True)
        grad_scores = (prob_rows * (grad_probs - inner_sums)).astype(jnp.bfloat16)
        query_grad = (
            jnp.einsum("hrj,jhk->rhk", grad_scores, key_heads, preferred_element_type=jnp.float32)
            * scale_factor
        )
        query_grads.append(query_grad.astype(jnp.bfloat16))
        grad_keys = (
            grad_keys
            + jnp.einsum(
                "hrj,rhk->jhk", grad_scores, query_block, preferred_element_type=jnp.float32
            )
            * scale_factor
        )
        offset = length - row_start - block_rows
        table_grad = table_grad.at[:, offset : offset + length + block_rows + 1].add(
            fold_distances(grad_scores.astype(jnp.float32))
        )
    grad_proj = jnp.stack(
        [
            jnp.concatenate(query_grads, axis=0).reshape(length, -1),
            grad_keys.reshape(length, -1).astype(jnp.bfloat16),
            grad_values.reshape(length, -1).astype(jnp.bfloat16),
        ]
    )
    d_qkv = jnp.einsum("td,cth->cdh", normed_low, grad_proj, preferred_element_type=jnp.float32)
    grad_normed_one = lax.psum(
        jnp.einsum("cth,cdh->td", grad_proj, w_qkv, preferred_element_type=jnp.float32).astype(
            jnp.bfloat16
        ),
        "tensor",
    ).astype(jnp.float32)
    back_one, d_gain_attn = norm_back(grad_normed_one, plain_one, scale_one, gain_one)
    d_tokens = (grad_middle + back_one).astype(jnp.bfloat16)
    distance_grad = table_grad[:, ::-1][:, length + 2 : 2 * length + 2]
    d_bias = lax.dot_general(
        bucket_pick, distance_grad, (((0,), (1,)), ((), ())), precision=PRECISE
    )
    d_qkv, d_out, d_bias, d_router, d_gain_attn, d_gain_ffn = lax.psum(
        (d_qkv, d_out, d_bias, d_router, d_gain_attn, d_gain_ffn), "expert"
    )
    return (
        output_rows,
        d_tokens,
        d_gain_attn,
        d_gain_ffn,
        d_qkv,
        d_out,
        d_bias,
        d_router,
        d_w_in,
        d_w_down,
    )


def solution(mesh):
    return jax.shard_map(
        body,
        mesh=mesh,
        in_specs=(
            P("expert", None),
            P("expert", None),
            P(),
            P(),
            P(None, None, "tensor"),
            P("tensor", None),
            P(None, "tensor"),
            P(),
            P("expert", None, "tensor"),
            P("expert", "tensor", None),
            P("expert", None),
            P("expert"),
            P(),
        ),
        out_specs=(
            P("expert", None),
            P("expert", None),
            P(),
            P(),
            P(None, None, "tensor"),
            P("tensor", None),
            P(None, "tensor"),
            P(),
            P("expert", None, "tensor"),
            P("expert", "tensor", None),
        ),
        check_vma=False,
    )
```

profile of v0, /device:TPU:0, one launch (start us, length us, event | category | flops | bytes accessed | tf_op | source)
XLA Modules:
  0.0 1149.5 jit_solution(703396785690117133)
XLA Ops:
  20.7 15.9 %reshape.629 = f32[2360832]{0:T(1024)} reshape(f32[3,512,1537]{2,1,0:T(8,128)} %tile.10) | data formatting | bytes 18886656
  36.6 13.2 %tile.11 = f32[3,786944]{1,0:T(4,128)} reshape(f32[2360832]{0:T(1024)} %reshape.629) | data formatting | bytes 18886656 | tf_op jit(solution)/shard_map/tile | solution.py:52
  60.9 11.2 copy.57
  76.6 16.1 %reshape.631 = f32[2360832]{0:T(1024)} reshape(f32[3,512,1537]{2,1,0:T(8,128)} %tile.8) | data formatting | bytes 18886656
  92.7 13.2 %tile.9 = f32[3,786944]{1,0:T(4,128)} reshape(f32[2360832]{0:T(1024)} %reshape.631) | data formatting | bytes 18886656 | tf_op jit(solution)/shard_map/tile | solution.py:52
  159.4 53.9 %all-reduce.14.cloned.1.call-done = f32[1024,768]{1,0:T(8,128)} async-done(((f32[1024,768]{1,0:T(8,128)}), f32[1024,768]{1,0:T(8,128)}) %all-reduce.14.cloned.1.call-update) | async-done | bytes 3145744 | tf_op jit(solution)/shard_map/psum | solution.py:147
  222.1 15.1 %scatter_custom_fusion.1 = bf16[4096,768]{1,0:T(8,128)(2,1)} fusion(s32[2048]{0:T(1024)S(1)} %get-tuple-element.82, f32[2048,768]{1,0:T(8,128)} %mul.277, bf16[]{:T(256)} %constant.115.clone.1, f32[2048]{0:T(1024)S(1)} %div.59), kind=kCustom, calls=%fused_computation.63 | custom fusion | flops 3145728 | bytes 12591106
  244.9 25.8 %scatter_custom_fusion = bf16[4096,768]{1,0:T(8,128)(2,1)} fusion(s32[2048]{0:T(1024)S(1)} %get-tuple-element.82, bf16[1024,768]{1,0:T(8,128)(2,1)S(1)} %multiply_convert_fusion.5, s32[2048]{0:T(1024)S(1)} %get-tuple-element.81, bf16[]{:T(256)} %constant.115.clone.1), kind=kCustom, calls=%fused_computation.65 | custom fusion | bytes 6291458
  270.7 110.1 %all-to-all-done.2 = bf16[8,1,512,768]{3,2,1,0:T(8,128)(2,1)} async-done(((bf16[8,1,512,768]{3,2,1,0:T(8,128)(2,1)}), bf16[8,1,512,768]{3,2,1,0:T(8,128)(2,1)}, u32[]{:S(2)}, u32[]{:S(2)}) %all-to-all-start.2) | async-done | bytes 6291488 | tf_op jit(solution)/shard_map/all_to_all | solution.py:201
  396.9 126.1 %all-to-all-done = bf16[8,1,512,768]{3,2,1,0:T(8,128)(2,1)} async-done(((bf16[8,1,512,768]{3,2,1,0:T(8,128)(2,1)}), bf16[8,1,512,768]{3,2,1,0:T(8,128)(2,1)}, u32[]{:S(2)}, u32[]{:S(2)}) %all-to-all-start) | async-done | bytes 6291488 | tf_op jit(solution)/shard_map/all_to_all | solution.py:167
  523.0 17.3 %fusion.6 = (bf16[4096,768]{1,0:T(8,128)(2,1)}, f32[4096,768]{1,0:T(8,128)S(1)}) fusion(f32[4096,768]{1,0:T(8,128)} %fusion.64, bf16[4096,768]{1,0:T(8,128)(2,1)} %bitcast.16, bf16[1,768,768]{2,1,0:T(8,128)(2,1)S(1)} %copy-done), kind=kOutput, calls=%fused_computation.13 | convolution fusion | flops 4894752768 | bytes 38928384 | tf_op jit(solution)/shard_map/dot_general | solution.py:169
  559.7 47.1 %reduce-scatter.3.cloned.1.call-done = bf16[8,128,768]{2,1,0:T(8,128)(2,1)} async-done(((bf16[8,512,768]{2,1,0:T(8,128)(2,1)}), bf16[8,128,768]{2,1,0:T(8,128)(2,1)}) %reduce-scatter.3.cloned.1.call-update) | async-done | bytes 1572880 | tf_op jit(solution)/shard_map/reduce_scatter | solution.py:174
  612.3 55.6 %reduce-scatter.5.cloned.1.call-done = bf16[8,128,768]{2,1,0:T(8,128)(2,1)} async-done(((bf16[8,512,768]{2,1,0:T(8,128)(2,1)}), bf16[8,128,768]{2,1,0:T(8,128)(2,1)}) %reduce-scatter.5.cloned.1.call-update) | async-done | bytes 1572880 | tf_op jit(solution)/shard_map/reduce_scatter | solution.py:209
  683.9 11.5 convolution_bitcast_fusion
  697.4 56.8 %gather_fusion = f32[2048,768]{1,0:T(8,128)} fusion(f32[8,1,128,768]{3,2,1,0:T(8,128)} %bitcast_convert_fusion.1, s32[2048]{0:T(1024)S(1)} %bitcast.146), kind=kCustom, calls=%fused_computation.1 | custom fusion | bytes 12607488 | tf_op jit(solution)/shard_map/gather | solution.py:69
  762.4 27.9 %gather_fusion.1 = f32[2048,768]{1,0:T(8,128)} fusion(f32[8,1,128,768]{3,2,1,0:T(8,128)S(1)} %bitcast.145, s32[2048]{0:T(1024)S(1)} %bitcast.147), kind=kCustom, calls=%fused_computation.2 | custom fusion | bytes 12607488 | tf_op jit(solution)/shard_map/gather | solution.py:69
  798.6 24.7 %multiply_reduce_fusion.2 = (f32[1024,2]{1,0:T(8,128)}, bf16[1024,768]{1,0:T(8,128)(2,1)}, f32[1024,768]{1,0:T(8,128)}) fusion(f32[1024,2,768]{2,1,0:T(2,128)} %gather.15, f32[1024,768]{1,0:T(8,128)S(1)} %copy-done.9, f32[1024,2]{1,0:T(8,128)} %reshape.575, f32[1024,2]{1,0:T(8,128)} %copy-done.14, f32[1024,2,768]{2,1,0:T(2,128)} %gather.17), kind=kLoop, calls=%fused_computation.31 | loop fusion | flops 9435136 | bytes 20471808 | tf_op jit(solution)/shard_map/reduce_sum | solution.py:224
  845.6 45.4 %all-reduce.16.cloned.1.call-done = f32[1024,768]{1,0:T(8,128)} async-done(((f32[1024,768]{1,0:T(8,128)}), f32[1024,768]{1,0:T(8,128)}) %all-reduce.16.cloned.1.call-update) | async-done | bytes 3145744 | tf_op jit(solution)/shard_map/psum | solution.py:225
  951.2 13.3 %reshape.633 = f32[2360832]{0:T(1024)} reshape(f32[3,786944]{1,0:T(4,128)} %pad_convert_fusion) | data formatting | bytes 18886656
  964.5 16.8 %reshape.581 = f32[3,512,1537]{2,1,0:T(8,128)} reshape(f32[2360832]{0:T(1024)} %reshape.633) | data formatting | bytes 18886656 | tf_op jit(solution)/shard_map/reshape | solution.py:63
  981.3 13.9 %reshape.635 = f32[2360832]{0:T(1024)} reshape(f32[3,786944]{1,0:T(4,128)} %pad_convert_fusion.1) | data formatting | bytes 18886656
  995.2 16.5 %reshape.579 = f32[3,512,1537]{2,1,0:T(8,128)} reshape(f32[2360832]{0:T(1024)} %reshape.635) | data formatting | bytes 18886656 | tf_op jit(solution)/shard_map/reshape | solution.py:63
  1032.6 40.1 %all-reduce.6 = (f32[768]{0:T(1024)}, f32[768]{0:T(1024)}, f32[32,3]{0,1:T(4,128)}, f32[768,8]{0,1:T(8,128)}) all-reduce(f32[768]{0:T(1024)S(1)} %get-tuple-element.38, f32[768]{0:T(1024)S(1)} %get-tuple-element.36, f32[32,3]{0,1:T(4,128)S(1)} %fusion.81, f32[768,8]{0,1:T(8,128)S(1)} %copy-done.38), channel_id=1, replica_groups=mesh['expert'=8,'tensor'=4] {'expert'}, use_global_device_ids=true, to_apply=%region_31.32 | all-reduce | flops 7776 | bytes 62208 | tf_op jit(solution)/shard_map/psum | solution.py:293
  1081.1 56.7 %all-reduce.18.cloned.1.call-done = (f32[3,768,192]{1,2,0:T(8,128)}, f32[192,768]{1,0:T(8,128)}) async-done(((f32[3,768,192]{1,2,0:T(8,128)}, f32[192,768]{1,0:T(8,128)}), (f32[3,768,192]{1,2,0:T(8,128)}, f32[192,768]{1,0:T(8,128)})) %all-reduce.18.cloned.1.call-update) | async-done | bytes 2359312 | tf_op jit(solution)/shard_map/psum | solution.py:293
  (266 shorter events, 290.2 us)
Async XLA Ops:
  7.2 515.8 %copy-start = (bf16[1,768,768]{2,1,0:T(8,128)(2,1)S(1)}, bf16[1,768,768]{2,1,0:T(8,128)(2,1)}, u32[]{:S(2)}) copy-start(bf16[1,768,768]{2,1,0:T(8,128)(2,1)} %param.25) | copy-start | bytes 3538948
  7.2 206.0 %all-reduce.14.cloned.1.call-start = ((), (), s32[]{:S(2)}) async-start(), calls=%async_computation.6 | async-start | bytes 6291456 | tf_op jit(solution)/shard_map/psum | solution.py:147
  12.9 112.7 %copy-start.19 = (bf16[1,512,192]{1,2,0:T(8,128)(2,1)}, bf16[1,512,192]{1,2,0:T(8,128)(2,1)S(1)}, u32[]{:S(2)}) copy-start(bf16[1,512,192]{1,2,0:T(8,128)(2,1)S(1)} %get-tuple-element.52) | copy-start | bytes 589828
  12.9 120.8 %copy-start.22 = (bf16[1,512,192]{1,2,0:T(8,128)(2,1)}, bf16[1,512,192]{1,2,0:T(8,128)(2,1)S(1)}, u32[]{:S(2)}) copy-start(bf16[1,512,192]{1,2,0:T(8,128)(2,1)S(1)} %get-tuple-element.51) | copy-start | bytes 589828
  13.4 120.4 %copy-start.10 = (bf16[1,1024,192]{1,2,0:T(8,128)(2,1)}, bf16[1,1024,192]{1,2,0:T(8,128)(2,1)S(1)}, u32[]{:S(2)}) copy-start(bf16[1,1024,192]{1,2,0:T(8,128)(2,1)S(1)} %get-tuple-element.53) | copy-start | bytes 1179652
  13.4 123.6 %copy-start.15 = (bf16[1,1024,192]{1,2,0:T(8,128)(2,1)}, bf16[1,1024,192]{1,2,0:T(8,128)(2,1)S(1)}, u32[]{:S(2)}) copy-start(bf16[1,1024,192]{1,2,0:T(8,128)(2,1)S(1)} %get-tuple-element.54) | copy-start | bytes 1179652
  143.1 99.6 %copy-start.31 = (f32[768]{0:T(1024)}, f32[768]{0:T(1024)S(1)}, u32[]{:S(2)}) copy-start(f32[768]{0:T(1024)S(1)} %convert_element_type.212) | copy-start | bytes 9220
  150.2 63.0 %copy-start.5 = (bf16[1024,768]{1,0:T(8,128)(2,1)S(1)}, bf16[1024,768]{1,0:T(8,128)(2,1)}, u32[]{:S(2)}) copy-start(bf16[1024,768]{1,0:T(8,128)(2,1)} %param.17) | copy-start | bytes 4718596
  158.9 58.3 %copy-start.44 = (bf16[768,8]{0,1:T(8,128)(2,1)S(1)}, bf16[768,8]{0,1:T(8,128)(2,1)}, u32[]{:S(2)}) copy-start(bf16[768,8]{0,1:T(8,128)(2,1)} %param.24) | copy-start | bytes 36868
  217.2 25.5 %copy-start.33 = (f32[1024]{0:T(1024)}, f32[1024]{0:T(1024)S(1)}, u32[]{:S(2)}) copy-start(f32[1024]{0:T(1024)S(1)} %add_rsqrt_fusion) | copy-start | bytes 12292
  237.2 143.6 %all-to-all-start.2 = ((bf16[8,1,512,768]{3,2,1,0:T(8,128)(2,1)}), bf16[8,1,512,768]{3,2,1,0:T(8,128)(2,1)}, u32[]{:S(2)}, u32[]{:S(2)}) async-start(bf16[8,1,512,768]{3,2,1,0:T(8,128)(2,1)} %bitcast.157), calls=%async_computation.3 | async-start | bytes 12582912 | tf_op jit(solution)/shard_map/all_to_all | solution.py:201
  380.8 142.2 %all-to-all-start = ((bf16[8,1,512,768]{3,2,1,0:T(8,128)(2,1)}), bf16[8,1,512,768]{3,2,1,0:T(8,128)(2,1)}, u32[]{:S(2)}, u32[]{:S(2)}) async-start(bf16[8,1,512,768]{3,2,1,0:T(8,128)(2,1)} %bitcast.156), calls=%async_computation | async-start | bytes 12582912 | tf_op jit(solution)/shard_map/all_to_all | solution.py:167
  385.8 221.1 %reduce-scatter.3.cloned.1.call-start = ((), (), s32[]{:S(2)}) async-start(), calls=%async_computation.7 | async-start | bytes 7864320 | tf_op jit(solution)/shard_map/reduce_scatter | solution.py:174
  549.7 118.2 %reduce-scatter.5.cloned.1.call-start = ((), (), s32[]{:S(2)}) async-start(), calls=%async_computation.8 | async-start | bytes 7864320 | tf_op jit(solution)/shard_map/reduce_scatter | solution.py:209
  606.8 64.4 %all-to-all-start.1 = ((bf16[1,8,128,768]{3,2,0,1:T(8,128)(2,1)}), bf16[1,8,128,768]{3,2,0,1:T(8,128)(2,1)S(1)}, u32[]{:S(2)}, u32[]{:S(2)}) async-start(bf16[1,8,128,768]{3,2,0,1:T(8,128)(2,1)} %bitcast.181), calls=%async_computation.2 | async-start | bytes 3145728 | tf_op jit(solution)/shard_map/all_to_all | solution.py:180
  672.4 90.0 %all-to-all-start.3 = ((f32[1,8,128,768]{3,2,0,1:T(8,128)}), f32[1,8,128,768]{3,2,0,1:T(8,128)S(1)}, u32[]{:S(2)}, u32[]{:S(2)}) async-start(f32[1,8,128,768]{3,2,0,1:T(8,128)} %bitcast_convert_fusion.2), calls=%async_computation.5 | async-start | bytes 6291456 | tf_op jit(solution)/shard_map/all_to_all | solution.py:215
  677.9 213.1 %all-reduce.16.cloned.1.call-start = ((), (), s32[]{:S(2)}) async-start(), calls=%async_computation.9 | async-start | bytes 6291456 | tf_op jit(solution)/shard_map/psum | solution.py:225
  823.3 17.6 %copy-start.32 = (f32[768]{0:T(1024)S(1)}, f32[768]{0:T(1024)}, u32[]{:S(2)}) copy-start(f32[768]{0:T(1024)} %copy-done.31) | copy-start | bytes 9220
  823.4 17.6 %copy-start.34 = (f32[1024]{0:T(1024)S(1)}, f32[1024]{0:T(1024)}, u32[]{:S(2)}) copy-start(f32[1024]{0:T(1024)} %copy-done.33) | copy-start | bytes 12292
  823.4 67.6 %copy-start.45 = (bf16[768,8]{0,1:T(8,128)(2,1)S(1)}, bf16[768,8]{0,1:T(8,128)(2,1)}, u32[]{:S(2)}) copy-start(bf16[768,8]{0,1:T(8,128)(2,1)} %param.24) | copy-start | bytes 36868
  823.4 206.6 %all-reduce.20.cloned.1.call-start = ((), (), s32[]{:S(2)}) async-start(), calls=%async_computation.11 | async-start | bytes 6291456 | tf_op jit(solution)/shard_map/psum | solution.py:190
  899.1 122.7 %copy-start.4 = (f32[1024,768]{1,0:T(8,128)}, f32[1024,768]{1,0:T(8,128)S(1)}, u32[]{:S(2)}) copy-start(f32[1024,768]{1,0:T(8,128)S(1)} %multiply_add_fusion) | copy-start | bytes 9437188
  943.2 194.6 %all-reduce.18.cloned.1.call-start = ((), (), s32[]{:S(2)}) async-start(), calls=%async_computation.10 | async-start | bytes 4718592 | tf_op jit(solution)/shard_map/psum | solution.py:293
  1072.7 69.8 %copy-start.1 = (bf16[1,768,768]{2,1,0:T(8,128)(2,1)S(1)}, bf16[1,768,768]{2,1,0:T(8,128)(2,1)}, u32[]{:S(2)}) copy-start(bf16[1,768,768]{2,1,0:T(8,128)(2,1)} %param.25) | copy-start | bytes 3538948
  (50 other events, 329.5 us)
Sparse Core Ops, SparseCore 0:
  142.1 71.1 all-reduce.13
  549.9 56.9 reduce-scatter.2
  609.5 58.3 reduce-scatter.4
  823.4 67.5 all-reduce.15
  943.3 68.7 all-reduce.19
  1027.5 110.1 all-reduce.17
where the time goes:
time: 1170 us; the launch traced here: 1150 us
  waiting for transfers between devices  495 us (42%)
  local copies, waits for them, and re-layouts  344 us (29%)
  matrix products  119 us (10%)
  other arithmetic  107 us (9%)
  blocking collectives  46.8 us (4%)
  starting transfers between devices  21.7 us (2%)
  between operations  15.4 us (1%)
    unnamed x146, local copies, waits for them, and re-layouts  135 us
    all_to_all x1, waiting for transfers between devices, body(): lax.all_to_all(outgoing, 'expert', split_axis=0, concat_axis=1, tiled=True)  126 us
    all_to_all x1, waiting for transfers between devices, body(): lax.all_to_all(outgoing_grad, 'expert', split_axis=0, concat_axis=1, tile...  110 us
    gather x4, local copies, waits for them, and re-layouts, pick_slots(): buffer[flat_experts, 0, jnp.clip(local_slot, 0, slot_count - 1)]  101 us
    psum x1, waiting for transfers between devices, body(): lax.psum((d_qkv, d_out, d_bias, d_router, d_gain_attn, d_gain_ffn), 'expe...  56.7 us
    reduce_scatter x1, waiting for transfers between devices, body(): lax.psum_scatter(grad_share.astype(jnp.float32).reshape(sources, capacity...  55.6 us
    psum x1, waiting for transfers between devices, body(): lax.psum(jnp.dot(mixed_flat, w_out, preferred_element_type=jnp.float32),...  53.9 us
    reduce_scatter x1, waiting for transfers between devices, body(): lax.psum_scatter(part_rows.astype(jnp.float32).reshape(sources, capacity,...  47.1 us
  transfers between devices with their start and end apart: 10, of which 7 were waited for; matrix products, arithmetic and copies ran while one was open for 23% of the time, Pallas kernels for 0%

commit v1 on v0

v1 whole, which is shorter than its diff:
```python
import functools

import jax
import jax.numpy as jnp
from jax import lax
from jax.experimental import pallas as pl
from jax.experimental.pallas import tpu as pltpu
from jax.sharding import PartitionSpec as P

EPSILON = 1e-06
PRECISE = lax.Precision.HIGHEST
FLOOR_SCORE = -1e30
LOW = jnp.bfloat16
WIDE = jnp.float32
VMEM_BYTES = 56 * 1024 * 1024
QUERY_ROWS = 256


def dot_nn(left, right):
    return lax.dot_general(left, right, (((1,), (0,)), ((), ())), preferred_element_type=WIDE)


def dot_tn(left, right, precision=None):
    return lax.dot_general(
        left, right, (((0,), (0,)), ((), ())), precision=precision, preferred_element_type=WIDE
    )


def dot_nt(left, right, precision=None):
    return lax.dot_general(
        left, right, (((1,), (1,)), ((), ())), precision=precision, preferred_element_type=WIDE
    )


def normalize(values, gain_vec):
    scale_rows = lax.rsqrt(jnp.mean(values * values, axis=-1, keepdims=True) + EPSILON)
    plain_rows = values * scale_rows
    return (plain_rows, scale_rows, plain_rows * gain_vec)


def norm_back(grad_in, plain_rows, scale_rows, gain_vec):
    gain_grad = jnp.sum(grad_in * plain_rows, axis=0)
    inner_grad = grad_in * gain_vec
    spread_grad = scale_rows * (
        inner_grad - plain_rows * jnp.mean(inner_grad * plain_rows, axis=-1, keepdims=True)
    )
    return (spread_grad, gain_grad)


def head_lanes(width, head_size, head):
    lane = lax.broadcasted_iota(jnp.int32, (1, width), 1)
    return ((lane >= head * head_size) & (lane < (head + 1) * head_size)).astype(LOW)


def build_strips(lines_ref, strip_ref, heads, rows, length):
    for head in range(heads):
        line = jnp.broadcast_to(lines_ref[head : head + 1, :], (rows, length + rows))
        strip_ref[head] = pltpu.roll(line, 0, 1, stride=1, stride_axis=0)[:, :length]


def strip_scores(query, key, strip_ref, head, first, rows, width, length, col_ids, row_ids):
    scores = dot_nt(query, key) + strip_ref[head, :, length - width :]
    return jnp.where(col_ids == row_ids, scores, FLOOR_SCORE)


def attend_kernel(heads, head_size, rows, qkv_ref, lines_ref, ids_col, ids_row, o_ref, lse_ref, strip_ref):
    length, width_all = qkv_ref.shape[1:]
    build_strips(lines_ref, strip_ref, heads, rows, length)
    scale = head_size ** (-0.5)
    for first in range(0, length, rows):
        width = first + rows
        query = qkv_ref[0, first:width, :]
        key = qkv_ref[1, :width, :]
        value = qkv_ref[2, :width, :]
        mixed = jnp.zeros((rows, width_all), WIDE)
        for head in range(heads):
            lanes = head_lanes(width_all, head_size, head)
            scores = strip_scores(
                query * (lanes * LOW(scale)), key, strip_ref, head, first, rows, width, length,
                ids_col[first:width, :], ids_row[:, :width],
            )
            row_max = jnp.max(scores, axis=-1, keepdims=True)
            exp_scores = jnp.exp(scores - row_max)
            row_total = jnp.sum(exp_scores, axis=-1, keepdims=True)
            probs = (exp_scores * (1.0 / row_total)).astype(LOW)
            mixed = mixed + dot_nn(probs, value) * lanes.astype(WIDE)
            lse_ref[first:width, head : head + 1] = row_max + jnp.log(row_total)
        o_ref[first:width, :] = mixed.astype(LOW)


def attend_back_kernel(
    heads, head_size, rows, qkv_ref, do_ref, lse_ref, lines_ref, ids_col, ids_row,
    dqkv_ref, fold_ref, strip_ref, grad_strip, dk_acc, dv_acc,
):
    length, width_all = qkv_ref.shape[1:]
    build_strips(lines_ref, strip_ref, heads, rows, length)
    scale = head_size ** (-0.5)
    grad_strip[...] = jnp.zeros_like(grad_strip)
    dk_acc[...] = jnp.zeros_like(dk_acc)
    dv_acc[...] = jnp.zeros_like(dv_acc)
    for first in range(0, length, rows):
        width = first + rows
        query = qkv_ref[0, first:width, :]
        key = qkv_ref[1, :width, :]
        value = qkv_ref[2, :width, :]
        grad_out = do_ref[first:width, :]
        dq = jnp.zeros((rows, width_all), WIDE)
        for head in range(heads):
            lanes = head_lanes(width_all, head_size, head)
            query_head = query * (lanes * LOW(scale))
            grad_head = grad_out * lanes
            scores = strip_scores(
                query_head, key, strip_ref, head, first, rows, width, length,
                ids_col[first:width, :], ids_row[:, :width],
            )
            probs = jnp.exp(scores - lse_ref[first:width, head : head + 1])
            grad_probs = dot_nt(grad_head, value)
            inner = jnp.sum(probs * grad_probs, axis=-1, keepdims=True)
            grad_scores = (probs * (grad_probs - inner)).astype(LOW)
            grad_strip[head, :, length - width :] += grad_scores.astype(WIDE)
            dv_acc[:width, :] += dot_tn(probs.astype(LOW), grad_head)
            dk_acc[:width, :] += dot_tn(grad_scores, query_head)
            dq = dq + dot_nn(grad_scores, key) * lanes.astype(WIDE)
        dqkv_ref[0, first:width, :] = (dq * scale).astype(LOW)
    dqkv_ref[1] = dk_acc[...].astype(LOW)
    dqkv_ref[2] = dv_acc[...].astype(LOW)
    line_width = length + rows
    for head in range(heads):
        folded = jnp.concatenate(
            [grad_strip[head], jnp.zeros((rows, rows), WIDE)], axis=1
        )
        left = rows
        while left > 1:
            left //= 2
            folded = folded[:left] + pltpu.roll(folded[left:], line_width - left, 1)
        fold_ref[head : head + 1, :] = folded


def attend(qkv, lines, ids_col, ids_row, heads, head_size, rows):
    _, length, width = qkv.shape
    return pl.pallas_call(
        functools.partial(attend_kernel, heads, head_size, rows),
        out_shape=(
            jax.ShapeDtypeStruct((length, width), LOW),
            jax.ShapeDtypeStruct((length, heads), WIDE),
        ),
        scratch_shapes=[pltpu.VMEM((heads, rows, length), WIDE)],
        compiler_params=pltpu.CompilerParams(vmem_limit_bytes=VMEM_BYTES),
        name="attend",
    )(qkv, lines, ids_col, ids_row)


def attend_back(qkv, grad_out, lse, lines, ids_col, ids_row, heads, head_size, rows):
    _, length, width = qkv.shape
    return pl.pallas_call(
        functools.partial(attend_back_kernel, heads, head_size, rows),
        out_shape=(
            jax.ShapeDtypeStruct((3, length, width), LOW),
            jax.ShapeDtypeStruct((heads, length + rows), WIDE),
        ),
        scratch_shapes=[
            pltpu.VMEM((heads, rows, length), WIDE),
            pltpu.VMEM((heads, rows, length), WIDE),
            pltpu.VMEM((length, width), WIDE),
            pltpu.VMEM((length, width), WIDE),
        ],
        compiler_params=pltpu.CompilerParams(vmem_limit_bytes=VMEM_BYTES),
        name="attend_back",
    )(qkv, grad_out, lse, lines, ids_col, ids_row)


def swap(values, axis_name, bit):
    size = lax.axis_size(axis_name)
    return lax.ppermute(values, axis_name, [(i, i ^ bit) for i in range(size)])


def tensor_bits():
    size = lax.axis_size("tensor")
    return [1 << b for b in range(size.bit_length() - 1)]


def gather_tensor(values):
    blocks = {0: values}
    for bit in reversed(tensor_bits()):
        blocks.update({r | bit: swap(block, "tensor", bit) for r, block in blocks.items()})
    return [blocks[r] for r in range(len(blocks))]


def reduce_tensor(blocks):
    held = dict(enumerate(blocks))
    for bit in tensor_bits():
        sent = {r: block for r, block in held.items() if r & bit}
        held = {r: block for r, block in held.items() if not r & bit}
        for r, block in sent.items():
            arrived = swap(block.astype(LOW), "tensor", bit)
            held[r ^ bit] = held[r ^ bit].astype(WIDE) + arrived.astype(WIDE)
    return held[0]


def place_blocks(blocks):
    mine = lax.axis_index("tensor")
    rows = blocks[0].shape[0]
    whole = jnp.zeros((len(blocks) * rows,) + blocks[0].shape[1:], blocks[0].dtype)
    for r, block in enumerate(blocks):
        whole = lax.dynamic_update_slice_in_dim(whole, block, (mine ^ r) * rows, 0)
    return whole


def sum_small(values):
    for axis_name in ("tensor", "expert"):
        for b in range(lax.axis_size(axis_name).bit_length() - 1):
            values = values + swap(values, axis_name, 1 << b)
    return values


def line_pairs(size, move, held):
    return [(i, i + 2 * move) for i in range(size) if 0 <= i // 2 + move < size // 2 and held(i // 2)]


def side_pairs(size, held):
    return [(i, i ^ 1) for i in range(size) if held(i // 2)]


def gather_expert(values):
    size = lax.axis_size("expert")
    planes = size // 2
    plane = lax.axis_index("expert") // 2
    other = lax.ppermute(values, "expert", side_pairs(size, lambda p: True))
    up, down = [(values, other)], [(values, other)]
    for k in range(1, planes):
        above = lax.ppermute(up[-1][0], "expert", line_pairs(size, 1, lambda p: p >= k - 1))
        below = lax.ppermute(down[-1][0], "expert", line_pairs(size, -1, lambda p: p < planes - k + 1))
        up.append((above, lax.ppermute(above, "expert", side_pairs(size, lambda p: p >= k))))
        down.append((below, lax.ppermute(below, "expert", side_pairs(size, lambda p: p < planes - k))))
    blocks = [up[0]]
    for k in range(1, planes):
        blocks.append(tuple(jnp.where(plane >= k, up[k][s], down[planes - k][s]) for s in (0, 1)))
    return blocks


def reduce_expert(blocks):
    size = lax.axis_size("expert")
    planes = size // 2
    held = [
        near.astype(WIDE)
        + lax.ppermute(far, "expert", side_pairs(size, lambda p: True)).astype(WIDE)
        for near, far in blocks
    ]
    up = down = None
    for d in range(planes - 1, 0, -1):
        to_above = held[planes - d] if up is None else held[planes - d] + up
        to_below = held[d] if down is None else held[d] + down
        up = lax.ppermute(
            to_above.astype(LOW), "expert", line_pairs(size, 1, lambda p: p + d < planes)
        ).astype(WIDE)
        down = lax.ppermute(
            to_below.astype(LOW), "expert", line_pairs(size, -1, lambda p: p - d >= 0)
        ).astype(WIDE)
    return held[0] + up + down


def sum_expert(values):
    bits = [1 << b for b in range(lax.axis_size("expert").bit_length() - 1)]
    mine = lax.axis_index("expert")
    part = values
    for bit in bits:
        half = part.shape[0] // 2
        upper = (mine & bit) != 0
        keep = jnp.where(upper, part[half:], part[:half])
        give = jnp.where(upper, part[:half], part[half:])
        part = keep.astype(WIDE) + swap(give.astype(LOW), "expert", bit).astype(WIDE)
    part = part.astype(LOW)
    for bit in reversed(bits):
        other = swap(part, "expert", bit)
        upper = (mine & bit) != 0
        part = jnp.concatenate(
            [jnp.where(upper, other, part), jnp.where(upper, part, other)], axis=0
        )
    return part.astype(WIDE)


def dense_experts(normed_low, grad_low, gates, choose, routes, w_in, w_down):
    rows = normed_low.shape[0]
    size = lax.axis_size("expert")
    mine = lax.axis_index("expert")
    planes = size // 2
    order = jnp.stack(
        [
            ((mine // 2 - k) % planes) * 2 + ((mine % 2) ^ s)
            for k in range(planes)
            for s in (0, 1)
        ]
    )
    back_order = jnp.stack(
        [
            ((mine // 2 - source // 2) % planes) * 2 + ((mine % 2) ^ (source % 2))
            for source in range(size)
        ]
    )
    grad_rows = jnp.concatenate([b for pair in gather_expert(grad_low) for b in pair], axis=0)
    in_blocks = gather_tensor(w_in[0])
    down_blocks = gather_tensor(w_down[0])
    dense_gates = jnp.sum(gates[:, :, None] * choose, axis=1).T
    gate_rows = lax.all_to_all(dense_gates, "expert", split_axis=0, concat_axis=0, tiled=True)
    gate_rows = jnp.take(gate_rows, order, axis=0).reshape(size * rows, 1)
    token_rows = jnp.concatenate([b for pair in gather_expert(normed_low) for b in pair], axis=0)
    gated_grad = (gate_rows * grad_rows.astype(WIDE)).astype(LOW)
    expert_out = 0.0
    row_grad = 0.0
    in_grads = []
    down_grads = []
    for w_in_block, w_down_block in zip(in_blocks, down_blocks):
        hidden_pre = dot_nn(token_rows, w_in_block)
        hidden, gelu_back = jax.vjp(functools.partial(jax.nn.gelu, approximate=True), hidden_pre)
        hidden = hidden.astype(LOW)
        expert_out = expert_out + dot_nn(hidden, w_down_block).astype(LOW).astype(WIDE)
        grad_pre = gelu_back(dot_nt(gated_grad, w_down_block))[0].astype(LOW)
        row_grad = row_grad + dot_nt(grad_pre, w_in_block).astype(LOW).astype(WIDE)
        in_grads.append(dot_tn(token_rows, grad_pre))
        down_grads.append(dot_tn(hidden, gated_grad))

    def as_blocks(values):
        parts = values.reshape(planes, 2, rows, -1)
        return [(parts[k, 0], parts[k, 1]) for k in range(planes)]

    row_grad = reduce_expert(as_blocks(row_grad.astype(LOW)))
    mixed = reduce_expert(as_blocks((gate_rows * expert_out).astype(LOW)))
    gate_grad = jnp.sum(grad_rows.astype(WIDE) * expert_out, axis=1).reshape(size, rows)
    gate_grad = lax.all_to_all(
        jnp.take(gate_grad, back_order, axis=0), "expert", split_axis=0, concat_axis=0, tiled=True
    )
    gate_grad = jnp.sum(gate_grad.T[:, None, :] * choose, axis=-1)
    d_w_in = reduce_tensor(in_grads)[None]
    d_w_down = reduce_tensor(down_grads)[None]
    return mixed, gate_grad, row_grad, d_w_in, d_w_down


def pick_slots(buffer, flat_experts, slot_index, first_slot, slot_count):
    local_slot = slot_index - first_slot
    inside = ((local_slot >= 0) & (local_slot < slot_count)).astype(WIDE)
    rows = buffer[flat_experts, 0, jnp.clip(local_slot, 0, slot_count - 1)].astype(WIDE)
    return rows * inside[:, None]


def slot_experts(normed_low, grad_low, gates, choose, routes, w_in, w_down):
    own = normed_low.shape[0]
    tensor_size = lax.axis_size("tensor")
    sources = lax.axis_size("expert")
    first_own = lax.axis_index("tensor") * own
    length = own * tensor_size
    experts = choose.shape[2]
    model_width = normed_low.shape[1]
    capacity = 4 * length // experts
    share_rows = capacity // tensor_size
    first_share = lax.axis_index("tensor") * share_rows
    normed_all = lax.all_gather(normed_low, "tensor", axis=0, tiled=True)
    grad_all = lax.all_gather(grad_low, "tensor", axis=0, tiled=True)
    gates_all = lax.all_gather(gates, "tensor", axis=0, tiled=True)
    flat_experts = routes.reshape(-1)
    marks = (flat_experts[:, None] == jnp.arange(experts)[None, :]).astype(jnp.int32)
    slot_index = jnp.sum((jnp.cumsum(marks, axis=0) - 1) * marks, axis=1)
    token_index = jnp.arange(2 * length) // 2

    def send(values):
        empty = jnp.zeros((experts, 1, capacity, model_width), LOW)
        placed = empty.at[flat_experts, 0, slot_index].set(values)
        arrived = lax.all_to_all(placed, "expert", split_axis=0, concat_axis=1, tiled=True)
        return arrived.reshape(sources * capacity, model_width)

    def give_back(values):
        summed = lax.psum_scatter(
            values.reshape(sources, capacity, model_width), "tensor", scatter_dimension=1, tiled=True
        )
        returned = lax.all_to_all(
            summed.reshape(1, sources, share_rows, model_width),
            "expert", split_axis=1, concat_axis=0, tiled=True,
        )
        return pick_slots(returned, flat_experts, slot_index, first_share, share_rows).reshape(
            length, 2, model_width
        )

    expert_rows = send(normed_all[token_index])
    grad_wide = grad_all.astype(WIDE)
    toward = (gates_all[:, :, None] * grad_wide[:, None, :]).astype(LOW)
    grad_rows = send(toward.reshape(2 * length, model_width))
    hidden_pre = dot_nn(expert_rows, w_in[0])
    hidden, gelu_back = jax.vjp(functools.partial(jax.nn.gelu, approximate=True), hidden_pre)
    hidden = hidden.astype(LOW)
    picked = give_back(dot_nn(hidden, w_down[0]).astype(LOW))
    grad_pre = gelu_back(dot_nt(grad_rows, w_down[0]))[0].astype(LOW)
    d_w_down = dot_tn(hidden, grad_rows)[None]
    d_w_in = dot_tn(expert_rows, grad_pre)[None]
    back_rows = give_back(dot_nt(grad_pre, w_in[0]).astype(LOW))
    mixed = jnp.sum(gates_all[:, :, None] * picked, axis=1)
    gate_grad = jnp.sum(picked * grad_wide[:, None, :], axis=-1)
    mixed, gate_grad, row_grad = (
        lax.dynamic_slice_in_dim(values, first_own, own, 0)
        for values in lax.psum((mixed, gate_grad, jnp.sum(back_rows, axis=1)), "tensor")
    )
    return mixed, gate_grad, row_grad, d_w_in, d_w_down


def body(
    tokens,
    cotangent,
    gain_attn,
    gain_ffn,
    w_qkv,
    w_out,
    bias_table,
    router,
    w_in,
    w_down,
    routes,
    sequence_ids,
    rel_buckets,
):
    length, model_width = tokens.shape
    rows = min(QUERY_ROWS, length)
    bucket_count, heads = bias_table.shape
    width = w_qkv.shape[2]
    head_size = width // heads
    experts = router.shape[1]
    tensor_size = lax.axis_size("tensor")
    own = length // tensor_size
    mine = lax.axis_index("tensor")

    def own_rows(values):
        return lax.dynamic_slice_in_dim(values, mine * own, own, 0)

    gain_one = gain_attn.astype(WIDE)
    gain_two = gain_ffn.astype(WIDE)
    grad_low = own_rows(cotangent)
    grad_output = grad_low.astype(WIDE)
    own_inputs = own_rows(tokens).astype(WIDE)
    own_routes = own_rows(routes)
    out_blocks = gather_tensor(w_out)

    _, _, normed_one = normalize(tokens.astype(WIDE), gain_one)
    normed_low = normed_one.astype(LOW)
    qkv = jnp.einsum("td,cdh->cth", normed_low, w_qkv, preferred_element_type=WIDE).astype(LOW)
    line_width = length + rows
    place = jnp.arange(line_width)
    distance = jnp.where(place < length, length - rows - place, length - rows + line_width - place)
    buckets = rel_buckets[jnp.clip(distance, 0, length - 1)]
    bucket_pick = (
        (buckets[:, None] == jnp.arange(bucket_count)[None, :]) & (distance >= 0)[:, None]
    ).astype(WIDE)
    lines = dot_tn(bias_table.astype(WIDE), bucket_pick.T, PRECISE)
    lines = jnp.where((distance >= 0)[None, :], lines, FLOOR_SCORE)
    ids_col = sequence_ids[:, None]
    ids_row = sequence_ids[None, :]
    mixed_heads, lse = attend(qkv, lines, ids_col, ids_row, heads, head_size, rows)

    half = [mixed_heads]
    tags = [0]
    span = length
    for bit in reversed(tensor_bits()):
        span //= 2
        keep_at = jnp.where((mine & bit) != 0, span, 0)
        give_at = span - keep_at
        arrived = [
            swap(lax.dynamic_slice_in_dim(block, give_at, span, 0), "tensor", bit) for block in half
        ]
        half = [lax.dynamic_slice_in_dim(block, keep_at, span, 0) for block in half] + arrived
        tags = tags + [tag | bit for tag in tags]
    attention = sum(dot_nn(block, out_blocks[tag]) for tag, block in zip(tags, half))
    middle = own_inputs + attention
    plain_two, scale_two, normed_two = normalize(middle, gain_two)
    router_float = router.astype(WIDE)
    logits = jnp.dot(normed_two, router_float, precision=PRECISE)
    choose = (own_routes[:, :, None] == jnp.arange(experts)[None, None, :]).astype(WIDE)
    chosen = jnp.sum(logits[:, None, :] * choose, axis=-1)
    gates = jax.nn.softmax(chosen, axis=1)

    run_experts = dense_experts if lax.axis_size("expert") == 8 else slot_experts
    mixed, gate_grad, grad_normed_two, d_w_in, d_w_down = run_experts(
        normed_two.astype(LOW), grad_low, gates, choose, routes, w_in, w_down
    )
    output_rows = place_blocks(gather_tensor((middle + mixed).astype(LOW)))

    mean_grad = jnp.sum(gates * gate_grad, axis=1, keepdims=True)
    select_grad = gates * (gate_grad - mean_grad)
    logit_grad = jnp.sum(select_grad[:, :, None] * choose, axis=1)
    d_router = dot_tn(normed_two, logit_grad, PRECISE)
    grad_normed_two = grad_normed_two + dot_nt(logit_grad, router_float, PRECISE)
    back_two, d_gain_ffn = norm_back(grad_normed_two, plain_two, scale_two, gain_two)
    grad_middle = grad_output + back_two
    grad_attn = place_blocks(gather_tensor(grad_middle.astype(LOW)))
    d_out = sum_expert(dot_tn(mixed_heads, grad_attn))
    grad_mixed = dot_nt(grad_attn, w_out).astype(LOW)
    grad_qkv, fold = attend_back(
        qkv, grad_mixed, lse, lines, ids_col, ids_row, heads, head_size, rows
    )
    d_bias = dot_tn(bucket_pick, fold.T, PRECISE)
    d_qkv = sum_expert(
        jnp.concatenate([dot_tn(normed_low, grad_qkv[c]) for c in range(3)], axis=0)
    ).reshape(3, model_width, width)
    grad_one = sum(dot_nt(grad_qkv[c], w_qkv[c]) for c in range(3)).astype(LOW)
    grad_one = reduce_tensor(
        [lax.dynamic_slice_in_dim(grad_one, (mine ^ r) * own, own, 0) for r in range(tensor_size)]
    )
    plain_one, scale_one, _ = normalize(own_inputs, gain_one)
    back_one, d_gain_attn = norm_back(grad_one, plain_one, scale_one, gain_one)
    d_tokens = place_blocks(gather_tensor((grad_middle + back_one).astype(LOW)))

    bias_places = jnp.zeros((tensor_size, bucket_count * heads), WIDE)
    bias_places = lax.dynamic_update_slice_in_dim(bias_places, d_bias.reshape(1, -1), mine, 0)
    flat = jnp.concatenate(
        [d_gain_attn, d_gain_ffn, d_router.T.reshape(-1), bias_places.reshape(-1)]
    )
    pad = -flat.shape[0] % 1024
    flat = sum_small(jnp.pad(flat, (0, pad)).reshape(-1, 128)).reshape(-1)
    d_gain_attn = flat[:model_width]
    d_gain_ffn = flat[model_width : 2 * model_width]
    router_end = (2 + experts) * model_width
    d_router = flat[2 * model_width : router_end].reshape(experts, model_width).T
    bias_places = flat[router_end : router_end + bias_places.size].reshape(tensor_size, -1)
    d_bias = lax.dynamic_slice_in_dim(bias_places, mine, 1, 0).reshape(bucket_count, heads)
    return (
        output_rows,
        d_tokens,
        d_gain_attn,
        d_gain_ffn,
        d_qkv,
        d_out,
        d_bias,
        d_router,
        d_w_in,
        d_w_down,
    )


def solution(mesh):
    return jax.shard_map(
        body,
        mesh=mesh,
        in_specs=(
            P("expert", None),
            P("expert", None),
            P(),
            P(),
            P(None, None, "tensor"),
            P("tensor", None),
            P(None, "tensor"),
            P(),
            P("expert", None, "tensor"),
            P("expert", "tensor", None),
            P("expert", None),
            P("expert"),
            P(),
        ),
        out_specs=(
            P("expert", None),
            P("expert", None),
            P(),
            P(),
            P(None, None, "tensor"),
            P("tensor", None),
            P(None, "tensor"),
            P(),
            P("expert", None, "tensor"),
            P("expert", "tensor", None),
        ),
        check_vma=False,
    )
```

time: 1170 us -> 517 us (0.44)
  waiting for transfers between devices: 495 us -> 121 us
  local copies, waits for them, and re-layouts: 344 us -> 41.2 us
  starting transfers between devices: 21.7 us -> 143 us
  other arithmetic: 107 us -> 32.5 us
  blocking collectives: 46.8 us -> 0 us
  Pallas kernels: 0 us -> 26 us
  matrix products: 119 us -> 140 us
  between operations: 15.4 us -> 2.96 us
    all_to_all x4 -> x2, waiting for transfers between devices: 236 us -> 10.7 us  [the longest x1 5.96 us: dense_experts(): lax.all_to_all(jnp.take(gate_grad, back_order, axis=0), 'expert', split_a...]
    psum x4 -> x0, waiting for transfers between devices: 156 us -> none  [the longest x1 56.7 us: body(): lax.psum((d_qkv, d_out, d_bias, d_router, d_gain_attn, d_gain_ffn), 'expe...]
    ppermute x0 -> x93, starting transfers between devices: none -> 132 us  [the longest x47 38.9 us: swap(): return lax.ppermute(values, axis_name, [(i, i ^ bit) for i in range(size)])]
    unnamed x146 -> x167, local copies, waits for them, and re-layouts: 135 us -> 8.35 us
    ppermute x0 -> x93, waiting for transfers between devices: none -> 110 us  [the longest x47 41 us: swap(): return lax.ppermute(values, axis_name, [(i, i ^ bit) for i in range(size)])]
    reduce_scatter x2 -> x0, waiting for transfers between devices: 103 us -> none  [the longest x1 55.6 us: body(): lax.psum_scatter(grad_share.astype(jnp.float32).reshape(sources, capacity...]
    gather x4 -> x3, local copies, waits for them, and re-layouts: 101 us -> 6.33 us  [the longest x1 4.96 us: body(): buckets = rel_buckets[jnp.clip(distance, 0, length - 1)]]
    psum x2 -> x0, blocking collectives: 46.8 us -> none  [the longest x1 40.1 us: body(): lax.psum((d_qkv, d_out, d_bias, d_router, d_gain_attn, d_gain_ffn), 'expe...]
  transfers between devices with their start and end apart: 10 -> 95, of which waited for: 7 -> 35; matrix products, arithmetic and copies ran while one was open for 23% -> 29% of each run, Pallas kernels for 0% -> 5%
where the time goes in v1:
time: 517 us; the launch traced here: 507 us
  starting transfers between devices  143 us (28%)
  matrix products  140 us (27%)
  waiting for transfers between devices  121 us (23%)
  local copies, waits for them, and re-layouts  41.2 us (8%)
  other arithmetic  32.5 us (6%)
  Pallas kernels  26 us (5%)
    dot_general x15, matrix products, dot_tn(): lax.dot_general(left, right, (((0,), (0,)), ((), ())), precision=precisio...  52.2 us
    dot_general x13, matrix products, dot_nt(): lax.dot_general(left, right, (((1,), (1,)), ((), ())), precision=precisio...  50.6 us
    ppermute x47, waiting for transfers between devices, swap(): return lax.ppermute(values, axis_name, [(i, i ^ bit) for i in range(size)])  41 us
    ppermute x47, starting transfers between devices, swap(): return lax.ppermute(values, axis_name, [(i, i ^ bit) for i in range(size)])  38.9 us
    ppermute x6, starting transfers between devices, reduce_expert(): lax.ppermute(to_above.astype(LOW), 'expert', line_pairs(size, 1, lambda p...  38.4 us
    dot_general x12, matrix products, dot_nn(): lax.dot_general(left, right, (((1,), (0,)), ((), ())), preferred_element_...  34.2 us
    ppermute x8, waiting for transfers between devices, reduce_expert(): lax.ppermute(far, 'expert', side_pairs(size, lambda p: True)).astype(WIDE)  21.2 us
    ppermute x6, waiting for transfers between devices, gather_expert(): lax.ppermute(below, 'expert', side_pairs(size, lambda p: p < planes - k))  20.7 us
  transfers between devices with their start and end apart: 95, of which 35 were waited for; matrix products, arithmetic and copies ran while one was open for 29% of the time, Pallas kernels for 5%

profile of v1, /device:TPU:0, one launch (start us, length us, event | category | flops | bytes accessed | tf_op | source)
XLA Modules:
  0.0 507.2 jit_solution(17488524182510974627)
XLA Ops:
  23.3 13.4 %attend.1 = (bf16[1024,192]{1,0:T(8,128)(2,1)}, f32[1024,3]{1,0:T(8,128)}) custom-call(bf16[3,1024,192]{2,1,0:T(8,128)(2,1)} %bitcast.212, f32[3,1280]{1,0:T(4,128)} %fusion.33.lines_ref, s32[1024,1]{1,0:T(8,128)} %copy.62.ids_col, s32[1,1024]{1,0:T(1,128)} %bitcast.228), custom_call_target="tpu_custom_call" | custom-call | tf_op jit(solution)/shard_map/attend/pallas_call | solution.py:141
  58.3 11.6 %collective-permute-done.41 = bf16[256,768]{1,0:T(8,128)(2,1)} collective-permute-done((bf16[256,768]{1,0:T(8,128)(2,1)S(1)}, bf16[256,768]{1,0:T(8,128)(2,1)}, u32[]{:S(2)}, u32[]{:S(2)}) %collective-permute-start.41) | collective-permute-done | bytes 393248 | tf_op jit(solution)/shard_map/ppermute | solution.py:232
  77.3 5.4 %collective-permute-done.42 = bf16[256,768]{1,0:T(8,128)(2,1)} collective-permute-done((bf16[256,768]{1,0:T(8,128)(2,1)}, bf16[256,768]{1,0:T(8,128)(2,1)}, u32[]{:S(2)}, u32[]{:S(2)}) %collective-permute-start.42) | collective-permute-done | bytes 393248 | tf_op jit(solution)/shard_map/ppermute | solution.py:232
  127.3 6.3 %collective-permute-done.12 = bf16[256,768]{1,0:T(8,128)(2,1)S(1)} collective-permute-done((bf16[256,768]{1,0:T(8,128)(2,1)S(1)}, bf16[256,768]{1,0:T(8,128)(2,1)S(1)}, u32[]{:S(2)}, u32[]{:S(2)}) %collective-permute-start.12) | collective-permute-done | bytes 393248 | tf_op jit(solution)/shard_map/ppermute | solution.py:234
  141.6 6.4 %collective-permute-done.18 = bf16[256,768]{1,0:T(8,128)(2,1)S(1)} collective-permute-done((bf16[256,768]{1,0:T(8,128)(2,1)S(1)}, bf16[256,768]{1,0:T(8,128)(2,1)S(1)}, u32[]{:S(2)}, u32[]{:S(2)}) %collective-permute-start.18) | collective-permute-done | bytes 393248 | tf_op jit(solution)/shard_map/ppermute | solution.py:234
  172.9 6.6 %fusion.1 = (f32[2048]{0:T(1024)S(1)}, f32[2048,768]{1,0:T(8,128)}) fusion(bf16[2048,768]{1,0:T(8,128)(2,1)S(1)} %copy-done.30, bf16[768,768]{1,0:T(8,128)(2,1)S(1)} %collective-permute-done.24, f32[2048,768]{1,0:T(8,128)S(1)} %fusion.151, bf16[2048,768]{1,0:T(8,128)(2,1)S(1)} %convolution_convert_fusion.5, ...), kind=kOutput, calls=%fused_computation.14 | convolution fusion | flops 2447374336 | bytes 26353664 | tf_op jit(solution)/shard_map/dot_general | solution.py:20
  180.9 7.7 %all-to-all-start.1 = ((f32[8,1,256]{2,1,0:T(1,128)}), f32[8,1,256]{2,1,0:T(1,128)S(1)}, u32[]{:S(2)}, u32[]{:S(2)}) async-start(f32[8,1,256]{2,1,0:T(1,128)} %copy.64), calls=%async_computation.1 | async-start | bytes 16384 | tf_op jit(solution)/shard_map/all_to_all | solution.py:329
  189.2 6.0 %all-to-all-done.1 = f32[8,1,256]{2,1,0:T(1,128)S(1)} async-done(((f32[8,1,256]{2,1,0:T(1,128)}), f32[8,1,256]{2,1,0:T(1,128)S(1)}, u32[]{:S(2)}, u32[]{:S(2)}) %all-to-all-start.1) | async-done | bytes 8224 | tf_op jit(solution)/shard_map/all_to_all | solution.py:329
  206.5 7.4 %convolution_convert_fusion.9 = bf16[768,768]{1,0:T(8,128)(2,1)S(1)} fusion(f32[2048,768]{1,0:T(8,128)} %copy-done.73, bf16[2048,768]{1,0:T(8,128)(2,1)} %select_dynamic-update-slice_fusion, f32[2048]{0:T(1024)S(1)} %bitcast.233), kind=kOutput, calls=%fused_computation.72 | convolution fusion | flops 2435383296 | bytes 10625024 | tf_op jit(solution)/shard_map/dot_general | solution.py:24
  213.9 8.1 %fusion.8 = bf16[2048,768]{1,0:T(8,128)(2,1)S(1)} fusion(f32[2048,768]{1,0:T(8,128)} %copy-done.70, bf16[1,768,768]{2,1,0:T(8,128)(2,1)S(1)} %copy-done.49, bf16[2048,768]{1,0:T(8,128)(2,1)S(1)} %copy-done.31, f32[2048]{0:T(1024)S(1)} %bitcast.234), kind=kOutput, calls=%fused_computation.21 | convolution fusion | flops 2452094976 | bytes 13770752 | tf_op jit(solution)/shard_map/dot_general | solution.py:30
  226.1 6.4 %fusion.15 = bf16[2048,768]{1,0:T(8,128)(2,1)S(1)} fusion(f32[2048,768]{1,0:T(8,128)S(1)} %bitcast.250, bf16[768,768]{1,0:T(8,128)(2,1)S(1)} %copy-done.61, bf16[2048,768]{1,0:T(8,128)(2,1)S(1)} %copy-done.31, f32[2048]{0:T(1024)S(1)} %bitcast.235), kind=kOutput, calls=%fused_computation.28 | convolution fusion | flops 2452094976 | bytes 13770752 | tf_op jit(solution)/shard_map/dot_general | solution.py:30
  232.5 8.0 %fusion.29 = bf16[2048,768]{1,0:T(8,128)(2,1)S(1)} fusion(f32[2048,768]{1,0:T(8,128)} %copy-done.72, bf16[768,768]{1,0:T(8,128)(2,1)S(1)} %copy-done.63, bf16[2048,768]{1,0:T(8,128)(2,1)S(1)} %copy-done.31, f32[2048]{0:T(1024)S(1)} %bitcast.236), kind=kOutput, calls=%fused_computation.42 | convolution fusion | flops 2452094976 | bytes 13770752 | tf_op jit(solution)/shard_map/dot_general | solution.py:30
  240.7 6.8 %fusion.22 = bf16[2048,768]{1,0:T(8,128)(2,1)S(1)} fusion(f32[2048,768]{1,0:T(8,128)S(1)} %bitcast.248, bf16[768,768]{1,0:T(8,128)(2,1)S(1)} %copy-done.55, bf16[2048,768]{1,0:T(8,128)(2,1)S(1)} %copy-done.31, f32[2048]{0:T(1024)S(1)} %bitcast.237), kind=kOutput, calls=%fused_computation.35 | convolution fusion | flops 2452094976 | bytes 13770752 | tf_op jit(solution)/shard_map/dot_general | solution.py:30
  255.6 5.6 %add_convert_fusion = bf16[2048,768]{1,0:T(8,128)(2,1)S(1)} fusion(bf16[2048,768]{1,0:T(8,128)(2,1)} %convolution_convert_fusion.1, bf16[2048,768]{1,0:T(8,128)(2,1)} %convolution_convert_fusion.2, bf16[2048,768]{1,0:T(8,128)(2,1)} %convolution_convert_fusion.3, bf16[2048,768]{1,0:T(8,128)(2,1)S(1)} %fusion.29, bf16[768,768]{1,0:T(8,128)(2,1)S(1)} %copy-done.59), kind=kOutput, calls=%fused_computation.43 | convolution fusion | flops 2430074880 | bytes 16908288 | tf_op jit(solution)/shard_map/dot_general | solution.py:30
  264.0 6.4 %convolution_convert_fusion.8 = bf16[768,768]{1,0:T(8,128)(2,1)S(1)} fusion(f32[2048,768]{1,0:T(8,128)} %copy-done.72, bf16[2048,768]{1,0:T(8,128)(2,1)S(1)} %copy-done.31, f32[2048]{0:T(1024)S(1)} %bitcast.239), kind=kOutput, calls=%fused_computation.71 | convolution fusion | flops 2435383296 | bytes 10625024 | tf_op jit(solution)/shard_map/dot_general | solution.py:24
  275.9 5.9 %collective-permute-done.28 = bf16[256,768]{1,0:T(8,128)(2,1)S(1)} collective-permute-done((bf16[256,768]{1,0:T(8,128)(2,1)S(1)}, bf16[256,768]{1,0:T(8,128)(2,1)S(1)}, u32[]{:S(2)}, u32[]{:S(2)}) %collective-permute-start.28) | collective-permute-done | bytes 393248 | tf_op jit(solution)/shard_map/ppermute | solution.py:246
  292.4 6.2 %collective-permute-done.27 = bf16[256,768]{1,0:T(8,128)(2,1)S(1)} collective-permute-done((bf16[256,768]{1,0:T(8,128)(2,1)S(1)}, bf16[256,768]{1,0:T(8,128)(2,1)S(1)}, u32[]{:S(2)}, u32[]{:S(2)}) %collective-permute-start.27) | collective-permute-done | bytes 393248 | tf_op jit(solution)/shard_map/ppermute | solution.py:246
  313.5 7.4 %add_convert_fusion.2 = bf16[768,768]{1,0:T(8,128)(2,1)} fusion(bf16[768,768]{1,0:T(8,128)(2,1)S(1)} %collective-permute-done.91, f32[2048,768]{1,0:T(8,128)} %copy-done.71, bf16[2048,768]{1,0:T(8,128)(2,1)S(1)} %copy-done.31, f32[2048]{0:T(1024)S(1)} %bitcast.240), kind=kOutput, calls=%fused_computation.65 | convolution fusion | flops 2436562944 | bytes 11804672 | tf_op jit(solution)/shard_map/dot_general | solution.py:24
  331.9 23.9 %collective-permute-start.57 = (bf16[256,768]{1,0:T(8,128)(2,1)S(1)}, bf16[256,768]{1,0:T(8,128)(2,1)S(1)}, u32[]{:S(2)}, u32[]{:S(2)}) collective-permute-start(bf16[256,768]{1,0:T(8,128)(2,1)S(1)} %get-tuple-element.90), channel_id=1, source_target_pairs={{0,8},{4,12},{8,16},{12,20},{16,24},{20,28},{1,9},{5,13},{9,17},{1... | collective-permute-start | bytes 1179656 | tf_op jit(solution)/shard_map/ppermute | solution.py:253
  357.0 7.8 %add_bitcast_fusion = f32[1,768,768]{2,1,0:T(8,128)} fusion(bf16[768,768]{1,0:T(8,128)(2,1)S(1)} %collective-permute-done.92, bf16[768,768]{1,0:T(8,128)(2,1)S(1)} %collective-permute-done.90, f32[2048,768]{1,0:T(8,128)} %copy-done.70, bf16[2048,768]{1,0:T(8,128)(2,1)S(1)} %copy-done.31, f32[2048]{0:T(1024)S(1)} %bitcast.241), kind=kOutput, calls=%fused_computation.64 | convolution fusion | flops 2437152768 | bytes 14163968 | tf_op jit(solution)/shard_map/dot_general | solution.py:24
  387.7 5.7 %collective-permute-done.36 = bf16[256,768]{1,0:T(8,128)(2,1)} collective-permute-done((bf16[256,768]{1,0:T(8,128)(2,1)S(1)}, bf16[256,768]{1,0:T(8,128)(2,1)}, u32[]{:S(2)}, u32[]{:S(2)}) %collective-permute-start.36) | collective-permute-done | bytes 393248 | tf_op jit(solution)/shard_map/ppermute | solution.py:174
  401.0 12.5 %attend_back.1 = (bf16[3,1024,192]{2,1,0:T(8,128)(2,1)}, f32[3,1280]{1,0:T(4,128)}) custom-call(bf16[3,1024,192]{2,1,0:T(8,128)(2,1)} %bitcast.213, bf16[1024,192]{1,0:T(8,128)(2,1)} %copy.65.do_ref, f32[1024,3]{1,0:T(8,128)} %get-tuple-element.16.lse_ref, f32[3,1280]{1,0:T(4,128)} %fusion.33.lines_ref, s32[1024,1]{1,0:T(8,128)} %copy.62.ids_col, ...), custom_call_target="tpu_custom_call" | custom-call | tf_op jit(solution)/shard_map/attend_back/pallas_call | solution.py:155
  455.5 5.7 %collective-permute-done.76 = bf16[576,192]{0,1:T(8,128)(2,1)S(1)} collective-permute-done((bf16[576,192]{0,1:T(8,128)(2,1)S(1)}, bf16[576,192]{0,1:T(8,128)(2,1)S(1)}, u32[]{:S(2)}, u32[]{:S(2)}) %collective-permute-start.76) | collective-permute-done | bytes 221216 | tf_op jit(solution)/shard_map/ppermute | solution.py:174
  494.1 6.3 %collective-permute-done.68 = bf16[256,768]{1,0:T(8,128)(2,1)S(1)} collective-permute-done((bf16[256,768]{1,0:T(8,128)(2,1)}, bf16[256,768]{1,0:T(8,128)(2,1)S(1)}, u32[]{:S(2)}, u32[]{:S(2)}) %collective-permute-start.68) | collective-permute-done | bytes 393248 | tf_op jit(solution)/shard_map/ppermute | solution.py:174
  (506 shorter events, 310.8 us)
Async XLA Ops:
  0.7 47.5 %collective-permute-start.1 = (bf16[192,768]{1,0:T(8,128)(2,1)}, bf16[192,768]{1,0:T(8,128)(2,1)}, u32[]{:S(2)}, u32[]{:S(2)}) collective-permute-start(bf16[192,768]{1,0:T(8,128)(2,1)} %param.20), channel_id=1, source_target_pairs={{0,2},{1,3},{2,0},{3,1},{4,6},{5,7},{6,4},{7,5},{8,10},{9,11},{10,... | collective-permute-start | bytes 884744 | tf_op jit(solution)/shard_map/ppermute | solution.py:174
  3.7 51.4 %collective-permute-start.3 = (bf16[192,768]{1,0:T(8,128)(2,1)}, bf16[192,768]{1,0:T(8,128)(2,1)}, u32[]{:S(2)}, u32[]{:S(2)}) collective-permute-start(bf16[192,768]{1,0:T(8,128)(2,1)} %param.20), channel_id=1, source_target_pairs={{0,1},{1,0},{2,3},{3,2},{4,5},{5,4},{6,7},{7,6},{8,9},{9,8},{10,11... | collective-permute-start | bytes 884744 | tf_op jit(solution)/shard_map/ppermute | solution.py:174
  5.5 70.6 %collective-permute-start.38 = (bf16[256,768]{1,0:T(8,128)(2,1)S(1)}, bf16[256,768]{1,0:T(8,128)(2,1)S(1)}, u32[]{:S(2)}, u32[]{:S(2)}) collective-permute-start(bf16[256,768]{1,0:T(8,128)(2,1)S(1)} %get-tuple-element.87), channel_id=1, source_target_pairs={{0,4},{4,0},{8,12},{12,8},{16,20},{20,16},{24,28},{28,24},{1,5},{5... | collective-permute-start | bytes 1179656 | tf_op jit(solution)/shard_map/ppermute | solution.py:228
  7.0 49.3 %collective-permute-start.40 = (bf16[256,768]{1,0:T(8,128)(2,1)S(1)}, bf16[256,768]{1,0:T(8,128)(2,1)S(1)}, u32[]{:S(2)}, u32[]{:S(2)}) collective-permute-start(bf16[256,768]{1,0:T(8,128)(2,1)S(1)} %get-tuple-element.87), channel_id=1, source_target_pairs={{8,0},{12,4},{16,8},{20,12},{24,16},{28,20},{9,1},{13,5},{17,9},{2... | collective-permute-start | bytes 1179656 | tf_op jit(solution)/shard_map/ppermute | solution.py:232
  50.1 24.6 %collective-permute-start.39 = (bf16[256,768]{1,0:T(8,128)(2,1)S(1)}, bf16[256,768]{1,0:T(8,128)(2,1)}, u32[]{:S(2)}, u32[]{:S(2)}) collective-permute-start(bf16[256,768]{1,0:T(8,128)(2,1)S(1)} %get-tuple-element.87), channel_id=1, source_target_pairs={{0,8},{4,12},{8,16},{12,20},{16,24},{20,28},{1,9},{5,13},{9,17},{1... | collective-permute-start | bytes 1179656 | tf_op jit(solution)/shard_map/ppermute | solution.py:231
  86.0 55.0 %collective-permute-start.21 = (bf16[768,768]{1,0:T(8,128)(2,1)}, bf16[768,768]{1,0:T(8,128)(2,1)S(1)}, u32[]{:S(2)}, u32[]{:S(2)}) collective-permute-start(bf16[768,768]{1,0:T(8,128)(2,1)} %bitcast.245), channel_id=1, source_target_pairs={{0,2},{1,3},{2,0},{3,1},{4,6},{5,7},{6,4},{7,5},{8,10},{9,11},{10,... | collective-permute-start | bytes 3538952 | tf_op jit(solution)/shard_map/ppermute | solution.py:174
  112.3 28.8 %collective-permute-start.22 = (bf16[768,768]{1,0:T(8,128)(2,1)S(1)}, bf16[768,768]{1,0:T(8,128)(2,1)S(1)}, u32[]{:S(2)}, u32[]{:S(2)}) collective-permute-start(bf16[768,768]{1,0:T(8,128)(2,1)S(1)} %bitcast.243), channel_id=1, source_target_pairs={{0,2},{1,3},{2,0},{3,1},{4,6},{5,7},{6,4},{7,5},{8,10},{9,11},{10,... | collective-permute-start | bytes 3538952 | tf_op jit(solution)/shard_map/ppermute | solution.py:174
  134.5 27.6 %collective-permute-start.19 = (bf16[768,768]{1,0:T(8,128)(2,1)S(1)}, bf16[768,768]{1,0:T(8,128)(2,1)S(1)}, u32[]{:S(2)}, u32[]{:S(2)}) collective-permute-start(bf16[768,768]{1,0:T(8,128)(2,1)S(1)} %bitcast.246), channel_id=1, source_target_pairs={{0,1},{1,0},{2,3},{3,2},{4,5},{5,4},{6,7},{7,6},{8,9},{9,8},{10,11... | collective-permute-start | bytes 3538952 | tf_op jit(solution)/shard_map/ppermute | solution.py:174
  141.0 23.7 %collective-permute-start.20 = (bf16[768,768]{1,0:T(8,128)(2,1)S(1)}, bf16[768,768]{1,0:T(8,128)(2,1)S(1)}, u32[]{:S(2)}, u32[]{:S(2)}) collective-permute-start(bf16[768,768]{1,0:T(8,128)(2,1)S(1)} %bitcast.244), channel_id=1, source_target_pairs={{0,1},{1,0},{2,3},{3,2},{4,5},{5,4},{6,7},{7,6},{8,9},{9,8},{10,11... | collective-permute-start | bytes 3538952 | tf_op jit(solution)/shard_map/ppermute | solution.py:174
  141.1 29.0 %collective-permute-start.23 = (bf16[768,768]{1,0:T(8,128)(2,1)S(1)}, bf16[768,768]{1,0:T(8,128)(2,1)S(1)}, u32[]{:S(2)}, u32[]{:S(2)}) collective-permute-start(bf16[768,768]{1,0:T(8,128)(2,1)S(1)} %collective-permute-done.21), channel_id=1, source_target_pairs={{0,1},{1,0},{2,3},{3,2},{4,5},{5,4},{6,7},{7,6},{8,9},{9,8},{10,11... | collective-permute-start | bytes 3538952 | tf_op jit(solution)/shard_map/ppermute | solution.py:174
  148.0 24.9 %collective-permute-start.24 = (bf16[768,768]{1,0:T(8,128)(2,1)S(1)}, bf16[768,768]{1,0:T(8,128)(2,1)S(1)}, u32[]{:S(2)}, u32[]{:S(2)}) collective-permute-start(bf16[768,768]{1,0:T(8,128)(2,1)S(1)} %collective-permute-done.22), channel_id=1, source_target_pairs={{0,1},{1,0},{2,3},{3,2},{4,5},{5,4},{6,7},{7,6},{8,9},{9,8},{10,11... | collective-permute-start | bytes 3538952 | tf_op jit(solution)/shard_map/ppermute | solution.py:174
  271.2 27.4 %collective-permute-start.27 = (bf16[256,768]{1,0:T(8,128)(2,1)S(1)}, bf16[256,768]{1,0:T(8,128)(2,1)S(1)}, u32[]{:S(2)}, u32[]{:S(2)}) collective-permute-start(bf16[256,768]{1,0:T(8,128)(2,1)S(1)} %get-tuple-element.100), channel_id=1, source_target_pairs={{0,4},{4,0},{8,12},{12,8},{16,20},{20,16},{24,28},{28,24},{1,5},{5... | collective-permute-start | bytes 1179656 | tf_op jit(solution)/shard_map/ppermute | solution.py:246
  287.3 25.5 %collective-permute-start.91 = (bf16[768,768]{1,0:T(8,128)(2,1)S(1)}, bf16[768,768]{1,0:T(8,128)(2,1)S(1)}, u32[]{:S(2)}, u32[]{:S(2)}) collective-permute-start(bf16[768,768]{1,0:T(8,128)(2,1)S(1)} %convolution_convert_fusion.8), channel_id=1, source_target_pairs={{0,1},{1,0},{2,3},{3,2},{4,5},{5,4},{6,7},{7,6},{8,9},{9,8},{10,11... | collective-permute-start | bytes 3538952 | tf_op jit(solution)/shard_map/ppermute | solution.py:174
  290.8 21.2 %collective-permute-start.26 = (bf16[256,768]{1,0:T(8,128)(2,1)S(1)}, bf16[256,768]{1,0:T(8,128)(2,1)S(1)}, u32[]{:S(2)}, u32[]{:S(2)}) collective-permute-start(bf16[256,768]{1,0:T(8,128)(2,1)S(1)} %get-tuple-element.101), channel_id=1, source_target_pairs={{0,4},{4,0},{8,12},{12,8},{16,20},{20,16},{24,28},{28,24},{1,5},{5... | collective-permute-start | bytes 1179656 | tf_op jit(solution)/shard_map/ppermute | solution.py:246
  307.1 24.8 %collective-permute-start.90 = (bf16[768,768]{1,0:T(8,128)(2,1)S(1)}, bf16[768,768]{1,0:T(8,128)(2,1)S(1)}, u32[]{:S(2)}, u32[]{:S(2)}) collective-permute-start(bf16[768,768]{1,0:T(8,128)(2,1)S(1)} %convolution_convert_fusion.9), channel_id=1, source_target_pairs={{0,1},{1,0},{2,3},{3,2},{4,5},{5,4},{6,7},{7,6},{8,9},{9,8},{10,11... | collective-permute-start | bytes 3538952 | tf_op jit(solution)/shard_map/ppermute | solution.py:174
  307.1 74.7 %collective-permute-start.87 = (bf16[768,768]{1,0:T(8,128)(2,1)S(1)}, bf16[768,768]{1,0:T(8,128)(2,1)S(1)}, u32[]{:S(2)}, u32[]{:S(2)}) collective-permute-start(bf16[768,768]{1,0:T(8,128)(2,1)S(1)} %convolution_convert_fusion.11), channel_id=1, source_target_pairs={{0,1},{1,0},{2,3},{3,2},{4,5},{5,4},{6,7},{7,6},{8,9},{9,8},{10,11... | collective-permute-start | bytes 3538952 | tf_op jit(solution)/shard_map/ppermute | solution.py:174
  320.9 34.8 %collective-permute-start.92 = (bf16[768,768]{1,0:T(8,128)(2,1)}, bf16[768,768]{1,0:T(8,128)(2,1)S(1)}, u32[]{:S(2)}, u32[]{:S(2)}) collective-permute-start(bf16[768,768]{1,0:T(8,128)(2,1)} %add_convert_fusion.2), channel_id=1, source_target_pairs={{0,2},{1,3},{2,0},{3,1},{4,6},{5,7},{6,4},{7,5},{8,10},{9,11},{10,... | collective-permute-start | bytes 3538952 | tf_op jit(solution)/shard_map/ppermute | solution.py:174
  329.4 35.5 %collective-permute-start.51 = (bf16[256,768]{1,0:T(8,128)(2,1)S(1)}, bf16[256,768]{1,0:T(8,128)(2,1)S(1)}, u32[]{:S(2)}, u32[]{:S(2)}) collective-permute-start(bf16[256,768]{1,0:T(8,128)(2,1)S(1)} %get-tuple-element.94), channel_id=1, source_target_pairs={{0,4},{4,0},{8,12},{12,8},{16,20},{20,16},{24,28},{28,24},{1,5},{5... | collective-permute-start | bytes 1179656 | tf_op jit(solution)/shard_map/ppermute | solution.py:246
  330.2 53.2 %collective-permute-start.89 = (bf16[768,768]{1,0:T(8,128)(2,1)S(1)}, bf16[768,768]{1,0:T(8,128)(2,1)S(1)}, u32[]{:S(2)}, u32[]{:S(2)}) collective-permute-start(bf16[768,768]{1,0:T(8,128)(2,1)S(1)} %add_convert_fusion.3), channel_id=1, source_target_pairs={{0,2},{1,3},{2,0},{3,1},{4,6},{5,7},{6,4},{7,5},{8,10},{9,11},{10,... | collective-permute-start | bytes 3538952 | tf_op jit(solution)/shard_map/ppermute | solution.py:174
  331.9 33.4 %collective-permute-start.57 = (bf16[256,768]{1,0:T(8,128)(2,1)S(1)}, bf16[256,768]{1,0:T(8,128)(2,1)S(1)}, u32[]{:S(2)}, u32[]{:S(2)}) collective-permute-start(bf16[256,768]{1,0:T(8,128)(2,1)S(1)} %get-tuple-element.90), channel_id=1, source_target_pairs={{0,8},{4,12},{8,16},{12,20},{16,24},{20,28},{1,9},{5,13},{9,17},{1... | collective-permute-start | bytes 1179656 | tf_op jit(solution)/shard_map/ppermute | solution.py:253
  373.0 20.5 %collective-permute-start.61 = (bf16[256,768]{1,0:T(8,128)(2,1)S(1)}, bf16[256,768]{1,0:T(8,128)(2,1)S(1)}, u32[]{:S(2)}, u32[]{:S(2)}) collective-permute-start(bf16[256,768]{1,0:T(8,128)(2,1)S(1)} %get-tuple-element.80), channel_id=1, source_target_pairs={{0,1},{1,0},{2,3},{3,2},{4,5},{5,4},{6,7},{7,6},{8,9},{9,8},{10,11... | collective-permute-start | bytes 1179656 | tf_op jit(solution)/shard_map/ppermute | solution.py:174
  393.4 49.5 %collective-permute-start.37 = (bf16[256,768]{1,0:T(8,128)(2,1)}, bf16[256,768]{1,0:T(8,128)(2,1)}, u32[]{:S(2)}, u32[]{:S(2)}) collective-permute-start(bf16[256,768]{1,0:T(8,128)(2,1)} %collective-permute-done.36), channel_id=1, source_target_pairs={{0,1},{1,0},{2,3},{3,2},{4,5},{5,4},{6,7},{7,6},{8,9},{9,8},{10,11... | collective-permute-start | bytes 1179656 | tf_op jit(solution)/shard_map/ppermute | solution.py:174
  421.0 30.5 %collective-permute-start.75 = (bf16[1152,192]{0,1:T(8,128)(2,1)}, bf16[1152,192]{0,1:T(8,128)(2,1)}, u32[]{:S(2)}, u32[]{:S(2)}) collective-permute-start(bf16[1152,192]{0,1:T(8,128)(2,1)} %select_convert_fusion), channel_id=1, source_target_pairs={{0,4},{4,0},{8,12},{12,8},{16,20},{20,16},{24,28},{28,24},{1,5},{5... | collective-permute-start | bytes 1327112 | tf_op jit(solution)/shard_map/ppermute | solution.py:174
  433.8 29.9 %collective-permute-start.64 = (bf16[256,768]{1,0:T(8,128)(2,1)}, bf16[256,768]{1,0:T(8,128)(2,1)}, u32[]{:S(2)}, u32[]{:S(2)}) collective-permute-start(bf16[256,768]{1,0:T(8,128)(2,1)} %get-tuple-element.102), channel_id=1, source_target_pairs={{0,1},{1,0},{2,3},{3,2},{4,5},{5,4},{6,7},{7,6},{8,9},{9,8},{10,11... | collective-permute-start | bytes 1179656 | tf_op jit(solution)/shard_map/ppermute | solution.py:174
  (151 other events, 1759.1 us)

commit v2 on v1

--- a/solution.py
+++ b/solution.py
@@ -12,7 +12,7 @@
 FLOOR_SCORE = -1e30
 LOW = jnp.bfloat16
 WIDE = jnp.float32
-VMEM_BYTES = 56 * 1024 * 1024
+VMEM_BYTES = 62 * 1024 * 1024
 QUERY_ROWS = 256
 
 
@@ -30,6 +30,10 @@
     return lax.dot_general(
         left, right, (((1,), (1,)), ((), ())), precision=precision, preferred_element_type=WIDE
     )
+
+
+def dot_nn_precise(left, right):
+    return jnp.dot(left, right, precision=PRECISE, preferred_element_type=WIDE)
 
 
 def normalize(values, gain_vec):
@@ -89,15 +93,20 @@
 
 
 def attend_back_kernel(
-    heads, head_size, rows, qkv_ref, do_ref, lse_ref, lines_ref, ids_col, ids_row,
-    dqkv_ref, fold_ref, strip_ref, grad_strip, dk_acc, dv_acc,
+    heads, head_size, rows, tokens, qkv_ref, mixed_ref, grad_ref, normed_ref, w_qkv_ref, w_out_ref,
+    lse_ref, lines_ref, ids_col, ids_row, *refs
 ):
+    sums_ref, back_ref, fold_ref = refs[tokens : tokens + 3]
+    strip_ref, grad_strip, do_ref, dqkv_ref, dk_acc, dv_acc = refs[tokens + 3 :]
     length, width_all = qkv_ref.shape[1:]
+    model_width = normed_ref.shape[1]
     build_strips(lines_ref, strip_ref, heads, rows, length)
     scale = head_size ** (-0.5)
     grad_strip[...] = jnp.zeros_like(grad_strip)
     dk_acc[...] = jnp.zeros_like(dk_acc)
     dv_acc[...] = jnp.zeros_like(dv_acc)
+    do_ref[...] = dot_nt(grad_ref[...], w_out_ref[...]).astype(LOW)
+    sums_ref[3 * model_width :] = dot_tn(grad_ref[...], mixed_ref[...]).astype(LOW)
     for first in range(0, length, rows):
         width = first + rows
         query = qkv_ref[0, first:width, :]
@@ -124,6 +133,16 @@
         dqkv_ref[0, first:width, :] = (dq * scale).astype(LOW)
     dqkv_ref[1] = dk_acc[...].astype(LOW)
     dqkv_ref[2] = dv_acc[...].astype(LOW)
+    for c in range(3):
+        sums_ref[c * model_width : (c + 1) * model_width] = dot_tn(
+            normed_ref[...], dqkv_ref[c]
+        ).astype(LOW)
+    for first in range(0, length, rows):
+        part = slice(first, first + rows)
+        back = dot_nt(dqkv_ref[0, part], w_qkv_ref[0])
+        for c in (1, 2):
+            back = back + dot_nt(dqkv_ref[c, part], w_qkv_ref[c])
+        back_ref[part] = back.astype(LOW)
     line_width = length + rows
     for head in range(heads):
         folded = jnp.concatenate(
@@ -146,27 +165,59 @@
         ),
         scratch_shapes=[pltpu.VMEM((heads, rows, length), WIDE)],
         compiler_params=pltpu.CompilerParams(vmem_limit_bytes=VMEM_BYTES),
+        cost_estimate=pl.CostEstimate(
+            flops=200 * length * length * width, bytes_accessed=1 << 22, transcendentals=0
+        ),
         name="attend",
     )(qkv, lines, ids_col, ids_row)
 
 
-def attend_back(qkv, grad_out, lse, lines, ids_col, ids_row, heads, head_size, rows):
+def attend_back(
+    qkv, mixed, grad_attn, normed, w_qkv, w_out, lse, lines, ids_col, ids_row,
+    heads, head_size, rows, tokens,
+):
     _, length, width = qkv.shape
+    model_width = normed.shape[1]
+    operands = (qkv, mixed, grad_attn, normed, w_qkv, w_out, lse, lines, ids_col, ids_row)
     return pl.pallas_call(
-        functools.partial(attend_back_kernel, heads, head_size, rows),
+        functools.partial(attend_back_kernel, heads, head_size, rows, len(tokens)),
+        in_specs=[pl.BlockSpec(memory_space=pltpu.VMEM)] * len(operands) + [ANYWHERE] * len(tokens),
         out_shape=(
-            jax.ShapeDtypeStruct((3, length, width), LOW),
+            jax.ShapeDtypeStruct((4 * model_width, width), LOW),
+            jax.ShapeDtypeStruct((length, model_width), LOW),
             jax.ShapeDtypeStruct((heads, length + rows), WIDE),
         ),
         scratch_shapes=[
             pltpu.VMEM((heads, rows, length), WIDE),
             pltpu.VMEM((heads, rows, length), WIDE),
+            pltpu.VMEM((length, width), LOW),
+            pltpu.VMEM((3, length, width), LOW),
             pltpu.VMEM((length, width), WIDE),
             pltpu.VMEM((length, width), WIDE),
         ],
         compiler_params=pltpu.CompilerParams(vmem_limit_bytes=VMEM_BYTES),
+        cost_estimate=pl.CostEstimate(
+            flops=200 * length * length * width, bytes_accessed=1 << 22, transcendentals=0
+        ),
         name="attend_back",
-    )(qkv, grad_out, lse, lines, ids_col, ids_row)
+    )(*operands, *tokens)
+
+
+ANYWHERE = pl.BlockSpec(memory_space=pltpu.HBM)
+
+
+def tie(values, *earlier):
+    def kernel(*refs):
+        pass
+
+    return pl.pallas_call(
+        kernel,
+        out_shape=jax.ShapeDtypeStruct(values.shape, values.dtype),
+        in_specs=[ANYWHERE] * (1 + len(earlier)),
+        out_specs=ANYWHERE,
+        input_output_aliases={0: 0},
+        name="tie",
+    )(values, *earlier)
 
 
 def swap(values, axis_name, bit):
@@ -186,24 +237,23 @@
     return [blocks[r] for r in range(len(blocks))]
 
 
-def reduce_tensor(blocks):
-    held = dict(enumerate(blocks))
-    for bit in tensor_bits():
-        sent = {r: block for r, block in held.items() if r & bit}
-        held = {r: block for r, block in held.items() if not r & bit}
-        for r, block in sent.items():
-            arrived = swap(block.astype(LOW), "tensor", bit)
-            held[r ^ bit] = held[r ^ bit].astype(WIDE) + arrived.astype(WIDE)
-    return held[0]
-
-
 def place_blocks(blocks):
-    mine = lax.axis_index("tensor")
     rows = blocks[0].shape[0]
-    whole = jnp.zeros((len(blocks) * rows,) + blocks[0].shape[1:], blocks[0].dtype)
-    for r, block in enumerate(blocks):
-        whole = lax.dynamic_update_slice_in_dim(whole, block, (mine ^ r) * rows, 0)
-    return whole
+    count = len(blocks)
+
+    def kernel(mine, *refs):
+        for r in range(count):
+            first = pl.multiple_of((mine[0] ^ r) * rows, rows)
+            refs[count][pl.ds(first, rows)] = refs[r][...]
+
+    return pl.pallas_call(
+        kernel,
+        out_shape=jax.ShapeDtypeStruct((count * rows,) + blocks[0].shape[1:], blocks[0].dtype),
+        in_specs=[pl.BlockSpec(memory_space=pltpu.SMEM)]
+        + [pl.BlockSpec(memory_space=pltpu.VMEM)] * count,
+        out_specs=pl.BlockSpec(memory_space=pltpu.VMEM),
+        name="place",
+    )(lax.axis_index("tensor").astype(jnp.int32).reshape(1), *blocks)
 
 
 def sum_small(values):
@@ -213,126 +263,401 @@
     return values
 
 
-def line_pairs(size, move, held):
-    return [(i, i + 2 * move) for i in range(size) if 0 <= i // 2 + move < size // 2 and held(i // 2)]
-
-
-def side_pairs(size, held):
-    return [(i, i ^ 1) for i in range(size) if held(i // 2)]
-
-
-def gather_expert(values):
+def sum_expert(values, beside):
     size = lax.axis_size("expert")
-    planes = size // 2
-    plane = lax.axis_index("expert") // 2
-    other = lax.ppermute(values, "expert", side_pairs(size, lambda p: True))
-    up, down = [(values, other)], [(values, other)]
-    for k in range(1, planes):
-        above = lax.ppermute(up[-1][0], "expert", line_pairs(size, 1, lambda p: p >= k - 1))
-        below = lax.ppermute(down[-1][0], "expert", line_pairs(size, -1, lambda p: p < planes - k + 1))
-        up.append((above, lax.ppermute(above, "expert", side_pairs(size, lambda p: p >= k))))
-        down.append((below, lax.ppermute(below, "expert", side_pairs(size, lambda p: p < planes - k))))
-    blocks = [up[0]]
-    for k in range(1, planes):
-        blocks.append(tuple(jnp.where(plane >= k, up[k][s], down[planes - k][s]) for s in (0, 1)))
-    return blocks
-
-
-def reduce_expert(blocks):
+    parts = values.astype(LOW).reshape((size, values.shape[0] // size) + values.shape[1:])
+    parts = tie(lax.all_to_all(parts, "expert", split_axis=0, concat_axis=0, tiled=True), beside)
+    part = jnp.sum(parts.astype(WIDE), axis=0).astype(LOW)
+    parts = jnp.broadcast_to(part[None], parts.shape)
+    parts = lax.all_to_all(parts, "expert", split_axis=0, concat_axis=0, tiled=True)
+    return parts.reshape(values.shape).astype(WIDE)
+
+
+def pick_rows(near, far, chosen):
+    rows = near.shape[0]
+    return dot_nn(chosen[:, :rows], near) + dot_nn(chosen[:, rows:], far)
+
+
+def gelu_pair(values):
+    slope = (2.0 / jnp.pi) ** 0.5
+    square = values * values
+    bend = jnp.tanh(slope * values * (1.0 + 0.044715 * square))
+    outer = 0.5 + 0.5 * bend
+    steep = slope * (1.0 + 3 * 0.044715 * square)
+    return values * outer, outer + 0.5 * values * (1.0 - bend * bend) * steep
+
+
+def short_rows(rows):
+    return rows * 9 // 16 // 16 * 16
+
+
+def split_low(values, rounded=lambda values: values.astype(LOW).astype(WIDE)):
+    pieces = []
+    for _ in range(3):
+        piece = rounded(values)
+        pieces.append(piece.astype(LOW))
+        values = values - piece
+    return pieces
+
+
+def round_low(values):
+    return lax.reduce_precision(values, 8, 7)
+
+
+def expert_kernel(blocks, chunk, experts, tokens, joined, meta, near, far, grads, *refs):
+    weights, refs = refs[: 2 * blocks], refs[2 * blocks + tokens :]
+    (kept_rows, kept_grads, count, hidden_out, pre_out), refs = refs[:5], refs[5:]
+    if joined:
+        backs, refs = refs[:2], refs[2:]
+        mix_outs = None
+    else:
+        backs, mix_outs, refs = refs[:2], refs[2:4], refs[4:]
+    weight_buf, grad_buf, hidden_buf, pre_buf, weight_sem, grad_sem, out_sem = refs
+    span = grad_buf.shape[0]
+    rows = span // 2
+    model_width = near.shape[1]
+    mine = meta[0]
+
+    def weight_copy(n):
+        return pltpu.make_async_copy(weights[n], weight_buf.at[n], weight_sem.at[n])
+
+    def side_rows(side):
+        return pl.ds(pl.multiple_of((mine ^ (2 * chunk + side)) * rows, rows), rows)
+
+    def grad_copy(side):
+        return pltpu.make_async_copy(
+            grads.at[side_rows(side)], grad_buf.at[pl.ds(side * rows, rows)], grad_sem.at[side]
+        )
+
+    for side in (0, 1):
+        grad_copy(side).start()
+    for n in range(2 * blocks):
+        weight_copy(n).start()
+
+    def gates_of(payload):
+        extra = payload[rows : rows + experts, :].astype(WIDE)
+        here = lax.broadcasted_iota(jnp.int32, extra.shape, 0) == mine
+        line = jnp.sum(jnp.where(here, extra, 0.0), axis=0, keepdims=True)
+        return line[:, :rows] + line[:, rows : 2 * rows] + line[:, 2 * rows :]
+
+    gate_row = jnp.concatenate([gates_of(near), gates_of(far)], axis=1)
+    routed = gate_row != 0.0
+    earlier = lax.broadcasted_iota(jnp.int32, (span, span), 0) < lax.broadcasted_iota(
+        jnp.int32, (span, span), 1
+    )
+    routed_wide = routed.astype(WIDE)
+    rank = dot_nn(
+        jnp.broadcast_to(routed_wide, (8, span)).astype(LOW), earlier.astype(WIDE).astype(LOW)
+    )[:1]
+    rank = jnp.where(routed, rank, -1.0).astype(jnp.int32)
+    total = jnp.sum(routed_wide).astype(jnp.int32)
+    count[0] = total
+
+    def run(taken):
+        def out_copy(n, buffer, target, lane):
+            return pltpu.make_async_copy(
+                buffer.at[n, pl.ds(0, taken)], target.at[n, pl.ds(0, taken)], out_sem.at[lane, n]
+            )
+
+        chosen_wide = (rank == lax.broadcasted_iota(jnp.int32, (taken, span), 0)).astype(WIDE)
+        chosen = chosen_wide.astype(LOW)
+        picked = pick_rows(near[:rows], far[:rows], chosen).astype(LOW)
+        gate_col = jnp.sum(chosen_wide * gate_row, axis=1, keepdims=True)
+        for side in (0, 1):
+            grad_copy(side).wait()
+        grad_rows = pick_rows(grad_buf[:rows], grad_buf[rows:], chosen)
+        gated = (gate_col * grad_rows).astype(LOW)
+        kept_rows[:taken] = picked
+        kept_grads[:taken] = gated
+        expert_out = jnp.zeros((taken, model_width), WIDE)
+        row_grad = jnp.zeros((taken, model_width), WIDE)
+        for n in range(blocks):
+            w_in, w_down = weight_buf.at[2 * n], weight_buf.at[2 * n + 1]
+            weight_copy(2 * n).wait()
+            weight_copy(2 * n + 1).wait()
+            value, slope = gelu_pair(dot_nn(picked, w_in[...]))
+            hidden = value.astype(LOW)
+            hidden_buf[n, :taken] = hidden
+            out_copy(n, hidden_buf, hidden_out, 0).start()
+            pre_grad = (dot_nt(gated, w_down[...]) * slope).astype(LOW)
+            pre_buf[n, :taken] = pre_grad
+            out_copy(n, pre_buf, pre_out, 1).start()
+            expert_out = expert_out + dot_nn(hidden, w_down[...]).astype(LOW).astype(WIDE)
+            row_grad = row_grad + dot_nt(pre_grad, w_in[...]).astype(LOW).astype(WIDE)
+        mixed = dot_tn(chosen, (gate_col * expert_out).astype(LOW)).astype(LOW)
+        back = dot_tn(chosen, row_grad.astype(LOW)).astype(LOW)
+        grad_col = jnp.sum(grad_rows * expert_out, axis=1, keepdims=True)
+        gate_grad = jnp.sum(chosen_wide * grad_col, axis=0, keepdims=True)
+        extra = payload_rows(rows, experts) - rows
+        for side, back_out in enumerate(backs):
+            part = slice(side * rows, (side + 1) * rows)
+            back_out[:rows] = back[part]
+            pieces = split_low(gate_grad[:, part])
+            line = jnp.concatenate([piece.astype(WIDE) for piece in pieces], axis=1)
+            here = lax.broadcasted_iota(jnp.int32, (extra, model_width), 0) == mine
+            back_out[rows : rows + extra] = jnp.where(here, line, 0.0).astype(LOW)
+            if joined:
+                back_out[rows + extra :] = mixed[part]
+            else:
+                mix_outs[side][...] = mixed[part]
+        for n in range(blocks):
+            out_copy(n, hidden_buf, hidden_out, 0).wait()
+            out_copy(n, pre_buf, pre_out, 1).wait()
+
+    few = total <= short_rows(span)
+
+    @pl.when(few)
+    def _():
+        run(short_rows(span))
+
+    @pl.when(jnp.logical_not(few))
+    def _():
+        run(span)
+
+
+def payload_rows(rows, experts):
+    return rows + -(-experts // 16) * 16
+
+
+def expert_chunk(chunk, experts, rows, joined, meta, near, far, grads, weights, tokens):
+    payload, model_width = near.shape
+    span = 2 * rows
+    blocks = len(weights) // 2
+    block_width = weights[0].shape[1]
+    low = functools.partial(jax.ShapeDtypeStruct, dtype=LOW)
+    vmem = pl.BlockSpec(memory_space=pltpu.VMEM)
+    smem = pl.BlockSpec(memory_space=pltpu.SMEM)
+    sides = [low((payload + rows, model_width))] * 2
+    if not joined:
+        sides = [low((payload, model_width))] * 2 + [low((rows, model_width))] * 2
+    return pl.pallas_call(
+        functools.partial(expert_kernel, blocks, chunk, experts, len(tokens), joined),
+        out_shape=(
+            low((span, model_width)),
+            low((span, model_width)),
+            jax.ShapeDtypeStruct((1,), jnp.int32),
+            low((blocks, span, block_width)),
+            low((blocks, span, block_width)),
+            *sides,
+        ),
+        in_specs=[smem, vmem, vmem] + [ANYWHERE] * (1 + len(weights) + len(tokens)),
+        out_specs=(vmem, vmem, smem, ANYWHERE, ANYWHERE) + (vmem,) * len(sides),
+        scratch_shapes=[
+            pltpu.VMEM((2 * blocks,) + weights[0].shape, LOW),
+            pltpu.VMEM((span, model_width), LOW),
+            pltpu.VMEM((blocks, span, block_width), LOW),
+            pltpu.VMEM((blocks, span, block_width), LOW),
+            pltpu.SemaphoreType.DMA((2 * blocks,)),
+            pltpu.SemaphoreType.DMA((2,)),
+            pltpu.SemaphoreType.DMA((2, blocks)),
+        ],
+        compiler_params=pltpu.CompilerParams(vmem_limit_bytes=VMEM_BYTES),
+        cost_estimate=pl.CostEstimate(
+            flops=200 * short_rows(span) * model_width * block_width * blocks,
+            bytes_accessed=1 << 24,
+            transcendentals=0,
+        ),
+        name="expert_chunk",
+    )(meta, near, far, grads, *weights, *tokens)
+
+
+def weight_grad_kernel(chunks, block, tokens, *refs):
+    counts, refs = refs[:chunks], refs[chunks:]
+    kept, refs = refs[: 4 * chunks], refs[4 * chunks + tokens :]
+    done, refs = refs[0], refs[1:]
+    done[0] = counts[0][0]
+    if block:
+        out_ref, refs = refs[0], refs[1:]
+    in_grad, down_grad, row_buf, grad_buf, hidden_buf, pre_buf, sem = refs
+    span = row_buf.shape[1]
+
+    def by_count(chunk, action):
+        few = counts[chunk][0] <= short_rows(span)
+
+        @pl.when(few)
+        def _():
+            action(short_rows(span))
+
+        @pl.when(jnp.logical_not(few))
+        def _():
+            action(span)
+
+    def copies(chunk, taken):
+        rows, grads, hidden, pre = kept[4 * chunk : 4 * chunk + 4]
+        part = pl.ds(0, taken)
+        return [
+            pltpu.make_async_copy(source, target, sem.at[chunk, n])
+            for n, (source, target) in enumerate(
+                (
+                    (rows.at[part], row_buf.at[chunk, part]),
+                    (grads.at[part], grad_buf.at[chunk, part]),
+                    (hidden.at[block, part], hidden_buf.at[chunk, part]),
+                    (pre.at[block, part], pre_buf.at[chunk, part]),
+                )
+            )
+        ]
+
+    for chunk in range(chunks):
+        by_count(chunk, lambda taken, chunk=chunk: [copy.start() for copy in copies(chunk, taken)])
+
+    def add(chunk, taken):
+        for copy in copies(chunk, taken):
+            copy.wait()
+        in_part = dot_tn(row_buf[chunk, :taken], pre_buf[chunk, :taken])
+        down_part = dot_tn(hidden_buf[chunk, :taken], grad_buf[chunk, :taken])
+        if chunk == 0:
+            in_grad[...] = in_part
+            down_grad[...] = down_part
+        elif chunk == chunks - 1 and block:
+            out_ref[0] = (in_grad[...] + in_part).astype(LOW)
+            out_ref[1] = (down_grad[...] + down_part).astype(LOW)
+        else:
+            in_grad[...] += in_part
+            down_grad[...] += down_part
+
+    for chunk in range(chunks):
+        by_count(chunk, functools.partial(add, chunk))
+
+
+def weight_grads(block, counts, kept, tokens):
+    chunks = len(kept)
+    span, model_width = kept[0][0].shape
+    block_width = kept[0][2].shape[2]
+    accumulators = [(model_width, block_width), (block_width, model_width)]
+    if block:
+        out_shape = (jax.ShapeDtypeStruct((2, model_width, block_width), LOW),)
+        extra = [pltpu.VMEM(shape, WIDE) for shape in accumulators]
+    else:
+        out_shape = tuple(jax.ShapeDtypeStruct(shape, WIDE) for shape in accumulators)
+        extra = []
+    return pl.pallas_call(
+        functools.partial(weight_grad_kernel, chunks, block, len(tokens)),
+        out_shape=(jax.ShapeDtypeStruct((1,), jnp.int32),) + out_shape,
+        out_specs=(pl.BlockSpec(memory_space=pltpu.SMEM),)
+        + (pl.BlockSpec(memory_space=pltpu.VMEM),) * len(out_shape),
+        in_specs=[pl.BlockSpec(memory_space=pltpu.SMEM)] * chunks
+        + [ANYWHERE] * (4 * chunks + len(tokens)),
+        scratch_shapes=extra
+        + [
+            pltpu.VMEM((chunks, span, model_width), LOW),
+            pltpu.VMEM((chunks, span, model_width), LOW),
+            pltpu.VMEM((chunks, span, block_width), LOW),
+            pltpu.VMEM((chunks, span, block_width), LOW),
+            pltpu.SemaphoreType.DMA((chunks, 4)),
+        ],
+        compiler_params=pltpu.CompilerParams(vmem_limit_bytes=VMEM_BYTES),
+        cost_estimate=pl.CostEstimate(
+            flops=120 * chunks * short_rows(span) * model_width * block_width,
+            bytes_accessed=1 << 23,
+            transcendentals=0,
+        ),
+        name="weight_grads",
+    )(*counts, *[array for four in kept for array in four], *tokens)
+
+
+def dense_experts(normed_low, grad_low, gates, choose, routes, gathered):
+    rows, model_width = normed_low.shape
+    experts = choose.shape[2]
     size = lax.axis_size("expert")
-    planes = size // 2
-    held = [
-        near.astype(WIDE)
-        + lax.ppermute(far, "expert", side_pairs(size, lambda p: True)).astype(WIDE)
-        for near, far in blocks
+    chunks = size // 2
+    meta = lax.axis_index("expert").astype(jnp.int32).reshape(1)
+    w_in_blocks, w_down_own, w_down_far, grad_all = gathered
+    dense_gates = jnp.sum(gates[:, :, None] * choose, axis=1).T
+    gate_rows = jnp.concatenate(split_low(dense_gates, round_low), axis=1)
+    payload = jnp.concatenate([normed_low, gate_rows], axis=0)
+    payload = jnp.pad(payload, ((0, payload_rows(rows, experts) - payload.shape[0]), (0, 0)))
+    run = functools.partial(expert_chunk, rows=rows, experts=experts, meta=meta, grads=grad_all)
+
+    def side_swap(values):
+        return swap(values, "expert", 1)
+
+    def plane_swap(chunk, values):
+        return swap(values, "expert", 2 * chunk)
+
+    far = [side_swap(payload)]
+    near = [payload, plane_swap(1, payload)]
+    near[1] = tie(near[1], far[0])
+    far.append(side_swap(near[1]))
+    near.append(plane_swap(2, tie(payload, near[1])))
+    last_down = tie(w_down_far, near[1])
+    in_blocks = w_in_blocks
+    down_blocks = [w_down_own, swap(w_down_own, "tensor", 1), last_down, swap(last_down, "tensor", 1)]
+    weights = [block for pair in zip(in_blocks, down_blocks) for block in pair]
+
+    kept, counts, held, flown, mixes, backs = [], [], [], [], [], []
+
+    def chunk_step(chunk, tokens):
+        joined = chunk < 2
+        rows_c, grads_c, count, hidden, pre, back_near, back_far, *mixed = run(
+            chunk, joined=joined, near=near[chunk], far=far[chunk], weights=weights, tokens=tokens
+        )
+        kept.append((rows_c, grads_c, hidden, pre))
+        counts.append(count)
+        mixes.append(mixed)
+        backs.append((back_near, side_swap(back_far)))
+
+    def hold(chunk, token):
+        back_near, arrived = backs[chunk]
+        return (back_near.astype(WIDE) + tie(arrived, token).astype(WIDE)).astype(LOW)
+
+    chunk_step(0, [])
+    near[2] = tie(near[2], counts[0])
+    far.append(side_swap(near[2]))
+    near.append(plane_swap(3, tie(payload, near[2])))
+    chunk_step(1, [counts[0]])
+    near[3] = tie(near[3], counts[1])
+    far.append(side_swap(near[3]))
+    held.append(hold(0, counts[1]))
+    chunk_step(2, [counts[1], held[0]])
+    held.append(hold(1, counts[2]))
+    flown.append(plane_swap(1, held[1]))
+    chunk_step(3, [counts[2], held[1]])
+    held.append(hold(2, counts[3]))
+    flown[0] = tie(flown[0], counts[3])
+    flown.append(plane_swap(2, held[2]))
+    joint = held[0].astype(WIDE) + flown[0].astype(WIDE)
+    grads_of = functools.partial(weight_grads, counts=counts, kept=kept)
+    done3, block3 = grads_of(3, tokens=[flown[0], held[2]])
+    held.append(hold(3, done3))
+    flown.append(plane_swap(3, held[3]))
+    core3 = swap(block3, "tensor", 1)
+    late = [side_swap(tie(mixes[chunk][1], held[3])) for chunk in (2, 3)]
+    done2, block2 = grads_of(2, tokens=[done3, held[3]])
+    flown[1] = tie(flown[1], done2)
+    flown[2] = tie(flown[2], done2)
+    chip_sum = (block2.astype(WIDE) + tie(core3, done2).astype(WIDE)).astype(LOW)
+    late = [
+        (mixes[chunk][0].astype(WIDE) + tie(arrived, done2).astype(WIDE)).astype(LOW)
+        for chunk, arrived in zip((2, 3), late)
     ]
-    up = down = None
-    for d in range(planes - 1, 0, -1):
-        to_above = held[planes - d] if up is None else held[planes - d] + up
-        to_below = held[d] if down is None else held[d] + down
-        up = lax.ppermute(
-            to_above.astype(LOW), "expert", line_pairs(size, 1, lambda p: p + d < planes)
-        ).astype(WIDE)
-        down = lax.ppermute(
-            to_below.astype(LOW), "expert", line_pairs(size, -1, lambda p: p - d >= 0)
-        ).astype(WIDE)
-    return held[0] + up + down
-
-
-def sum_expert(values):
-    bits = [1 << b for b in range(lax.axis_size("expert").bit_length() - 1)]
-    mine = lax.axis_index("expert")
-    part = values
-    for bit in bits:
-        half = part.shape[0] // 2
-        upper = (mine & bit) != 0
-        keep = jnp.where(upper, part[half:], part[:half])
-        give = jnp.where(upper, part[:half], part[half:])
-        part = keep.astype(WIDE) + swap(give.astype(LOW), "expert", bit).astype(WIDE)
-    part = part.astype(LOW)
-    for bit in reversed(bits):
-        other = swap(part, "expert", bit)
-        upper = (mine & bit) != 0
-        part = jnp.concatenate(
-            [jnp.where(upper, other, part), jnp.where(upper, part, other)], axis=0
+    late = [plane_swap(chunk, values) for chunk, values in zip((2, 3), late)]
+    payload = payload.shape[0]
+    row_grad = joint[:payload] + flown[1].astype(WIDE) + flown[2].astype(WIDE)
+    tail = row_grad[rows : rows + experts]
+    gate_grad = tail[:, :rows] + tail[:, rows : 2 * rows] + tail[:, 2 * rows :]
+    gate_grad = jnp.sum(gate_grad.T[:, None, :] * choose, axis=-1)
+
+    def early_weights(token):
+        return grads_of(1, tokens=[token])
+
+    def send_weights(n, arrived):
+        sent = chip_sum[n] if arrived is None else tie(chip_sum[n], arrived)
+        return swap(sent, "tensor", 2)
+
+    def finish_mixed(token):
+        mixed = joint[payload:]
+        for values in late:
+            mixed = mixed + tie(values, token).astype(WIDE)
+        return mixed
+
+    def finish_weights(block1, token):
+        done0, *block0 = grads_of(0, tokens=[token])
+        near_sum = tie(swap(block1, "tensor", 1), token)
+        return done0, lambda far_sums: tuple(
+            (block0[n] + near_sum[n].astype(WIDE) + far_sums[n].astype(WIDE))[None] for n in (0, 1)
         )
-    return part.astype(WIDE)
-
-
-def dense_experts(normed_low, grad_low, gates, choose, routes, w_in, w_down):
-    rows = normed_low.shape[0]
-    size = lax.axis_size("expert")
-    mine = lax.axis_index("expert")
-    planes = size // 2
-    order = jnp.stack(
-        [
-            ((mine // 2 - k) % planes) * 2 + ((mine % 2) ^ s)
-            for k in range(planes)
-            for s in (0, 1)
-        ]
-    )
-    back_order = jnp.stack(
-        [
-            ((mine // 2 - source // 2) % planes) * 2 + ((mine % 2) ^ (source % 2))
-            for source in range(size)
-        ]
-    )
-    grad_rows = jnp.concatenate([b for pair in gather_expert(grad_low) for b in pair], axis=0)
-    in_blocks = gather_tensor(w_in[0])
-    down_blocks = gather_tensor(w_down[0])
-    dense_gates = jnp.sum(gates[:, :, None] * choose, axis=1).T
-    gate_rows = lax.all_to_all(dense_gates, "expert", split_axis=0, concat_axis=0, tiled=True)
-    gate_rows = jnp.take(gate_rows, order, axis=0).reshape(size * rows, 1)
-    token_rows = jnp.concatenate([b for pair in gather_expert(normed_low) for b in pair], axis=0)
-    gated_grad = (gate_rows * grad_rows.astype(WIDE)).astype(LOW)
-    expert_out = 0.0
-    row_grad = 0.0
-    in_grads = []
-    down_grads = []
-    for w_in_block, w_down_block in zip(in_blocks, down_blocks):
-        hidden_pre = dot_nn(token_rows, w_in_block)
-        hidden, gelu_back = jax.vjp(functools.partial(jax.nn.gelu, approximate=True), hidden_pre)
-        hidden = hidden.astype(LOW)
-        expert_out = expert_out + dot_nn(hidden, w_down_block).astype(LOW).astype(WIDE)
-        grad_pre = gelu_back(dot_nt(gated_grad, w_down_block))[0].astype(LOW)
-        row_grad = row_grad + dot_nt(grad_pre, w_in_block).astype(LOW).astype(WIDE)
-        in_grads.append(dot_tn(token_rows, grad_pre))
-        down_grads.append(dot_tn(hidden, gated_grad))
-
-    def as_blocks(values):
-        parts = values.reshape(planes, 2, rows, -1)
-        return [(parts[k, 0], parts[k, 1]) for k in range(planes)]
-
-    row_grad = reduce_expert(as_blocks(row_grad.astype(LOW)))
-    mixed = reduce_expert(as_blocks((gate_rows * expert_out).astype(LOW)))
-    gate_grad = jnp.sum(grad_rows.astype(WIDE) * expert_out, axis=1).reshape(size, rows)
-    gate_grad = lax.all_to_all(
-        jnp.take(gate_grad, back_order, axis=0), "expert", split_axis=0, concat_axis=0, tiled=True
-    )
-    gate_grad = jnp.sum(gate_grad.T[:, None, :] * choose, axis=-1)
-    d_w_in = reduce_tensor(in_grads)[None]
-    d_w_down = reduce_tensor(down_grads)[None]
-    return mixed, gate_grad, row_grad, d_w_in, d_w_down
+
+    return gate_grad, row_grad[:rows], early_weights, send_weights, finish_mixed, finish_weights
 
 
 def pick_slots(buffer, flat_experts, slot_index, first_slot, slot_count):
@@ -342,7 +667,8 @@
     return rows * inside[:, None]
 
 
-def slot_experts(normed_low, grad_low, gates, choose, routes, w_in, w_down):
+def slot_experts(normed_low, grad_low, gates, choose, routes, gathered):
+    w_in, w_down = gathered
     own = normed_low.shape[0]
     tensor_size = lax.axis_size("tensor")
     sources = lax.axis_size("expert")
@@ -397,7 +723,15 @@
         lax.dynamic_slice_in_dim(values, first_own, own, 0)
         for values in lax.psum((mixed, gate_grad, jnp.sum(back_rows, axis=1)), "tensor")
     )
-    return mixed, gate_grad, row_grad, d_w_in, d_w_down
+    token = gate_grad[:1, :1]
+    return (
+        gate_grad,
+        row_grad,
+        lambda token: (token, token),
+        lambda n, arrived: token,
+        lambda token: mixed,
+        lambda block1, token: (token, lambda far_sums: (d_w_in, d_w_down)),
+    )
 
 
 def body(
@@ -441,8 +775,14 @@
     qkv = jnp.einsum("td,cdh->cth", normed_low, w_qkv, preferred_element_type=WIDE).astype(LOW)
     line_width = length + rows
     place = jnp.arange(line_width)
-    distance = jnp.where(place < length, length - rows - place, length - rows + line_width - place)
-    buckets = rel_buckets[jnp.clip(distance, 0, length - 1)]
+    distance = jnp.where(place < length, length - rows - place, 2 * length - place)
+    buckets = jnp.concatenate(
+        [
+            rel_buckets[: length - rows + 1][::-1],
+            jnp.zeros((rows,), jnp.int32),
+            rel_buckets[length - rows + 1 :][::-1],
+        ]
+    )
     bucket_pick = (
         (buckets[:, None] == jnp.arange(bucket_count)[None, :]) & (distance >= 0)[:, None]
     ).astype(WIDE)
@@ -452,6 +792,16 @@
     ids_row = sequence_ids[None, :]
     mixed_heads, lse = attend(qkv, lines, ids_col, ids_row, heads, head_size, rows)
 
+    whole_width = (
+        lax.axis_size("expert") == 8
+        and tensor_size == 4
+        and 3 * own == model_width
+        and w_in.shape[2] == model_width
+    )
+    if whole_width:
+        w_in_far = tie(swap(w_in[0], "tensor", 2), lse)
+        w_in_near = swap(w_in[0], "tensor", 1)
+
     half = [mixed_heads]
     tags = [0]
     span = length
@@ -459,9 +809,10 @@
         span //= 2
         keep_at = jnp.where((mine & bit) != 0, span, 0)
         give_at = span - keep_at
-        arrived = [
-            swap(lax.dynamic_slice_in_dim(block, give_at, span, 0), "tensor", bit) for block in half
-        ]
+        given = [lax.dynamic_slice_in_dim(block, give_at, span, 0) for block in half]
+        if whole_width and len(half) == 1:
+            given = [tie(given[0], w_in_far)]
+        arrived = [swap(block, "tensor", bit) for block in given]
         half = [lax.dynamic_slice_in_dim(block, keep_at, span, 0) for block in half] + arrived
         tags = tags + [tag | bit for tag in tags]
     attention = sum(dot_nn(block, out_blocks[tag]) for tag, block in zip(tags, half))
@@ -473,58 +824,88 @@
     chosen = jnp.sum(logits[:, None, :] * choose, axis=-1)
     gates = jax.nn.softmax(chosen, axis=1)
 
-    run_experts = dense_experts if lax.axis_size("expert") == 8 else slot_experts
-    mixed, gate_grad, grad_normed_two, d_w_in, d_w_down = run_experts(
-        normed_two.astype(LOW), grad_low, gates, choose, routes, w_in, w_down
-    )
-    output_rows = place_blocks(gather_tensor((middle + mixed).astype(LOW)))
+    if whole_width:
+        w_down_own = tie(w_down[0], half[1])
+        gathered = (
+            [w_in[0], w_in_near, w_in_far, swap(w_in_far, "tensor", 1)],
+            w_down_own,
+            swap(w_down_own, "tensor", 2),
+            lax.all_gather(grad_low, "expert", axis=0, tiled=True),
+        )
+    else:
+        gathered = (w_in, w_down)
+    run_experts = dense_experts if whole_width else slot_experts
+    gate_grad, grad_normed_two, early_weights, send_weights, finish_mixed, finish_weights = run_experts(
+        normed_two.astype(LOW), grad_low, gates, choose, routes, gathered
+    )
 
     mean_grad = jnp.sum(gates * gate_grad, axis=1, keepdims=True)
     select_grad = gates * (gate_grad - mean_grad)
     logit_grad = jnp.sum(select_grad[:, :, None] * choose, axis=1)
-    d_router = dot_tn(normed_two, logit_grad, PRECISE)
     grad_normed_two = grad_normed_two + dot_nt(logit_grad, router_float, PRECISE)
     back_two, d_gain_ffn = norm_back(grad_normed_two, plain_two, scale_two, gain_two)
     grad_middle = grad_output + back_two
-    grad_attn = place_blocks(gather_tensor(grad_middle.astype(LOW)))
-    d_out = sum_expert(dot_tn(mixed_heads, grad_attn))
-    grad_mixed = dot_nt(grad_attn, w_out).astype(LOW)
-    grad_qkv, fold = attend_back(
-        qkv, grad_mixed, lse, lines, ids_col, ids_row, heads, head_size, rows
-    )
-    d_bias = dot_tn(bucket_pick, fold.T, PRECISE)
-    d_qkv = sum_expert(
-        jnp.concatenate([dot_tn(normed_low, grad_qkv[c]) for c in range(3)], axis=0)
-    ).reshape(3, model_width, width)
-    grad_one = sum(dot_nt(grad_qkv[c], w_qkv[c]) for c in range(3)).astype(LOW)
-    grad_one = reduce_tensor(
-        [lax.dynamic_slice_in_dim(grad_one, (mine ^ r) * own, own, 0) for r in range(tensor_size)]
-    )
+    own_grad_attn = grad_middle.astype(LOW)
+    done1, block1 = early_weights(own_grad_attn)
+    grad_blocks = [own_grad_attn]
+    for bit in reversed(tensor_bits()):
+        arrived = [tie(swap(block, "tensor", bit), done1) for block in grad_blocks]
+        grad_blocks = grad_blocks + arrived if len(grad_blocks) == 1 else [
+            *(grad_blocks[:1] + arrived[:1] + grad_blocks[1:] + arrived[1:])
+        ]
+    far_sums = [send_weights(0, None), send_weights(1, grad_blocks[2])]
+    grad_attn = place_blocks(grad_blocks)
+    sums, grad_one, fold = attend_back(
+        qkv, mixed_heads, grad_attn, normed_low, w_qkv, w_out, lse, lines, ids_col, ids_row,
+        heads, head_size, rows, [done1, far_sums[0]],
+    )
+    sums = tie(sums, far_sums[1])
+    mixed = finish_mixed(fold)
+    d_router = dot_tn(logit_grad, normed_two, PRECISE)
+    done0, add_weights = finish_weights(block1, sums)
+    sums = sum_expert(sums, done0)
+    d_qkv = sums[: 3 * model_width].reshape(3, model_width, width)
+    d_out = sums[3 * model_width :].T
+    quarters = [
+        lax.dynamic_slice_in_dim(grad_one, (mine ^ r) * own, own, 0) for r in range(tensor_size)
+    ]
+    held = quarters
+    for bit in tensor_bits():
+        keep = jnp.concatenate([held[r] for r in range(len(held)) if not r & 1], axis=0)
+        give = jnp.concatenate([held[r] for r in range(len(held)) if r & 1], axis=0).astype(LOW)
+        arrived = swap(give, "tensor", bit)
+        held = keep.astype(WIDE) + arrived.astype(WIDE)
+        held = [held[n * own : (n + 1) * own] for n in range(held.shape[0] // own)]
+    grad_one = held[0]
+    d_w_in, d_w_down = add_weights(far_sums)
+    output_rows = place_blocks(gather_tensor((middle + mixed).astype(LOW)))
     plain_one, scale_one, _ = normalize(own_inputs, gain_one)
     back_one, d_gain_attn = norm_back(grad_one, plain_one, scale_one, gain_one)
     d_tokens = place_blocks(gather_tensor((grad_middle + back_one).astype(LOW)))
 
-    bias_places = jnp.zeros((tensor_size, bucket_count * heads), WIDE)
-    bias_places = lax.dynamic_update_slice_in_dim(bias_places, d_bias.reshape(1, -1), mine, 0)
+    d_bias = dot_nn_precise(fold, bucket_pick)
+    d_bias = jnp.pad(d_bias, ((0, 0), (0, model_width - bucket_count)))
+    here = (jnp.arange(tensor_size) == mine)[:, None, None]
     flat = jnp.concatenate(
-        [d_gain_attn, d_gain_ffn, d_router.T.reshape(-1), bias_places.reshape(-1)]
-    )
-    pad = -flat.shape[0] % 1024
-    flat = sum_small(jnp.pad(flat, (0, pad)).reshape(-1, 128)).reshape(-1)
-    d_gain_attn = flat[:model_width]
-    d_gain_ffn = flat[model_width : 2 * model_width]
-    router_end = (2 + experts) * model_width
-    d_router = flat[2 * model_width : router_end].reshape(experts, model_width).T
-    bias_places = flat[router_end : router_end + bias_places.size].reshape(tensor_size, -1)
-    d_bias = lax.dynamic_slice_in_dim(bias_places, mine, 1, 0).reshape(bucket_count, heads)
+        [
+            d_gain_attn[None],
+            d_gain_ffn[None],
+            d_router,
+            jnp.where(here, d_bias[None], 0.0).reshape(tensor_size * heads, model_width),
+        ],
+        axis=0,
+    )
+    flat = sum_small(flat)
+    d_router = flat[2 : 2 + experts].T
+    d_bias = lax.dynamic_slice_in_dim(flat, 2 + experts + mine * heads, heads, 0)
     return (
         output_rows,
         d_tokens,
-        d_gain_attn,
-        d_gain_ffn,
+        flat[0],
+        flat[1],
         d_qkv,
         d_out,
-        d_bias,
+        d_bias[:, :bucket_count].T,
         d_router,
         d_w_in,
         d_w_down,

time: 517 us -> 430 us (0.83); the launches traced: 507 us -> 426 us
  Pallas kernels: 26 us -> 182 us
  matrix products: 140 us -> 9.96 us
  starting transfers between devices: 143 us -> 59.1 us
  waiting for transfers between devices: 121 us -> 71.9 us
  between operations: 2.96 us -> 15.7 us
  local copies, waits for them, and re-layouts: 41.2 us -> 48.8 us
  other arithmetic: 32.5 us -> 39.2 us
    pallas_call x0 -> x41, Pallas kernels: none -> 151 us  [the longest x4 86.7 us: expert_chunk(): pl.pallas_call(functools.partial(expert_kernel, blocks, chunk, experts, l...]
    ppermute x46 -> x0, starting transfers between devices: 93.1 us -> none  [the longest x6 38.4 us: reduce_expert(): lax.ppermute(to_above.astype(LOW), 'expert', line_pairs(size, 1, lambda p...]
    ppermute x46 -> x0, waiting for transfers between devices: 69.4 us -> none  [the longest x8 21.2 us: reduce_expert(): lax.ppermute(far, 'expert', side_pairs(size, lambda p: True)).astype(WIDE)]
    dot_general x13 -> x1, matrix products: 50.6 us -> 0.77 us  [dot_nt(): lax.dot_general(left, right, (((1,), (1,)), ((), ())), precision=precisio...]
    dot_general x15 -> x2, matrix products: 52.2 us -> 2.93 us  [dot_tn(): lax.dot_general(left, right, (((0,), (0,)), ((), ())), precision=precisio...]
    dot_general x12 -> x4, matrix products: 34.2 us -> 4.02 us  [dot_nn(): lax.dot_general(left, right, (((1,), (0,)), ((), ())), preferred_element_...]
    ppermute x47 -> x50, waiting for transfers between devices: 41 us -> 67.1 us  [swap(): return lax.ppermute(values, axis_name, [(i, i ^ bit) for i in range(size)])]
    convert_element_type x22 -> x14, other arithmetic: 5.28 us -> 20 us  [the longest x4 6.67 us: hold(): (back_near.astype(WIDE) + tie(arrived, token).astype(WIDE)).astype(LOW)]
  transfers between devices with their start and end apart: 95 -> 53, of which waited for: 35 -> 13; matrix products, arithmetic and copies ran while one was open for 29% -> 17% of each run, Pallas kernels for 5% -> 38%
where the time goes in v2:
time: 430 us; the launch traced here: 426 us
  Pallas kernels  182 us (42%)
  waiting for transfers between devices  71.9 us (17%)
  starting transfers between devices  59.1 us (14%)
  local copies, waits for them, and re-layouts  48.8 us (11%)
  other arithmetic  39.2 us (9%)
  between operations  15.7 us (4%)
  matrix products  9.96 us (2%)
    pallas_call x4, Pallas kernels, expert_chunk(): pl.pallas_call(functools.partial(expert_kernel, blocks, chunk, experts, l...  86.7 us
    ppermute x50, waiting for transfers between devices, swap(): return lax.ppermute(values, axis_name, [(i, i ^ bit) for i in range(size)])  67.1 us
    ppermute x50, starting transfers between devices, swap(): return lax.ppermute(values, axis_name, [(i, i ^ bit) for i in range(size)])  51.5 us
    pallas_call x4, Pallas kernels, weight_grads(): pl.pallas_call(functools.partial(weight_grad_kernel, chunks, block, len(t...  46.2 us
    unnamed x151, local copies, waits for them, and re-layouts  22.8 us
    pallas_call x1, Pallas kernels, attend_back(): pl.pallas_call(functools.partial(attend_back_kernel, heads, head_size, ro...  17.3 us
    pallas_call x1, Pallas kernels, attend(): pl.pallas_call(functools.partial(attend_kernel, heads, head_size, rows),...  13.6 us
    pallas_call x30, Pallas kernels, tie(): pl.pallas_call(kernel, out_shape=jax.ShapeDtypeStruct(values.shape, value...  10.3 us
  transfers between devices with their start and end apart: 53, of which 13 were waited for; matrix products, arithmetic and copies ran while one was open for 17% of the time, Pallas kernels for 38%

profile of v2, /device:TPU:0, one launch (start us, length us, event | category | flops | bytes accessed | tf_op | source)
XLA Modules:
  0.0 426.3 jit_solution(1176775018494094405)
XLA Ops:
  9.8 2.9 collective-permute-start.2
  23.1 13.6 %attend.1 = (bf16[1024,192]{1,0:T(8,128)(2,1)}, f32[1024,3]{1,0:T(8,128)}) custom-call(bf16[3,1024,192]{2,1,0:T(8,128)(2,1)} %bitcast.73, f32[3,1280]{1,0:T(4,128)} %fusion.7.lines_ref, s32[1024,1]{1,0:T(8,128)} %copy.114.ids_col, s32[1,1024]{1,0:T(1,128)} %bitcast.78), custom_call_target="tpu_custom_call" | custom-call | flops 40265318400 | bytes 4194304 | tf_op jit(solution)/shard_map/attend/pallas_call | solution.py:160
  40.5 4.6 %collective-permute-done.refs_0_ = bf16[768,768]{1,0:T(8,128)(2,1)} collective-permute-done((bf16[768,768]{1,0:T(8,128)(2,1)}, bf16[768,768]{1,0:T(8,128)(2,1)}, u32[]{:S(2)}, u32[]{:S(2)}) %collective-permute-start) | collective-permute-done | bytes 1179680 | tf_op jit(solution)/shard_map/ppermute | solution.py:225
  48.1 4.7 %collective-permute-done.1 = bf16[512,192]{1,0:T(8,128)(2,1)S(1)} collective-permute-done((bf16[512,192]{1,0:T(8,128)(2,1)}, bf16[512,192]{1,0:T(8,128)(2,1)S(1)}, u32[]{:S(2)}, u32[]{:S(2)}) %collective-permute-start.1) | collective-permute-done | bytes 196640 | tf_op jit(solution)/shard_map/ppermute | solution.py:225
  63.6 18.8 %collective-permute-done.11.refs_0_ = bf16[272,768]{1,0:T(8,128)(2,1)S(1)} collective-permute-done((bf16[272,768]{1,0:T(8,128)(2,1)S(1)}, bf16[272,768]{1,0:T(8,128)(2,1)S(1)}, u32[]{:S(2)}, u32[]{:S(2)}) %collective-permute-start.11) | collective-permute-done | bytes 417824 | tf_op jit(solution)/shard_map/ppermute | solution.py:225
  88.2 21.0 %expert_chunk.4 = (bf16[512,768]{1,0:T(8,128)(2,1)}, bf16[512,768]{1,0:T(8,128)(2,1)}, s32[1]{0:T(128)}, bf16[4,512,768]{2,1,0:T(8,128)(2,1)}, bf16[4,512,768]{2...) custom-call(s32[1]{0:T(128)} %bitcast.9.meta, bf16[272,768]{1,0:T(8,128)(2,1)} %copy-done.9, ...), custom_call_target="tpu_custom_call" | custom-call | flops 135895449600 | bytes 16777216 | tf_op jit(solution)/shard_map/expert_chunk/pallas_call | solution.py:433
  115.0 16.0 %collective-permute-done.17.refs_0_ = bf16[272,768]{1,0:T(8,128)(2,1)S(1)} collective-permute-done((bf16[272,768]{1,0:T(8,128)(2,1)}, bf16[272,768]{1,0:T(8,128)(2,1)S(1)}, u32[]{:S(2)}, u32[]{:S(2)}) %collective-permute-start.17) | collective-permute-done | bytes 417824 | tf_op jit(solution)/shard_map/ppermute | solution.py:225
  135.5 21.2 %expert_chunk.5 = (bf16[512,768]{1,0:T(8,128)(2,1)}, bf16[512,768]{1,0:T(8,128)(2,1)}, s32[1]{0:T(128)}, bf16[4,512,768]{2,1,0:T(8,128)(2,1)}, bf16[4,512,768]{2...) custom-call(s32[1]{0:T(128)} %bitcast.9.meta, bf16[272,768]{1,0:T(8,128)(2,1)} %tie.33.refs_1_.near, ...), custom_call_target="tpu_custom_call" | custom-call | flops 135895449600 | bytes 16777216 | tf_op jit(solution)/shard_map/expert_chunk/pallas_call | solution.py:433
  163.2 21.0 %expert_chunk.6 = (bf16[512,768]{1,0:T(8,128)(2,1)}, bf16[512,768]{1,0:T(8,128)(2,1)}, s32[1]{0:T(128)}, bf16[4,512,768]{2,1,0:T(8,128)(2,1)}, bf16[4,512,768]{2...) custom-call(s32[1]{0:T(128)} %bitcast.9.meta, ...), custom_call_target="tpu_custom_call" | custom-call | flops 135895449600 | bytes 16777216 | tf_op jit(solution)/shard_map/expert_chunk/pallas_call | solution.py:433
  188.9 23.4 %expert_chunk.7 = (bf16[512,768]{1,0:T(8,128)(2,1)}, bf16[512,768]{1,0:T(8,128)(2,1)}, s32[1]{0:T(128)}, bf16[4,512,768]{2,1,0:T(8,128)(2,1)}, bf16[4,512,768]{2...) custom-call(s32[1]{0:T(128)} %bitcast.9.meta, ...), custom_call_target="tpu_custom_call" | custom-call | flops 135895449600 | bytes 16777216 | tf_op jit(solution)/shard_map/expert_chunk/pallas_call | solution.py:433
  219.2 11.1 %weight_grads.4 = (s32[1]{0:T(128)}, bf16[2,768,768]{2,1,0:T(8,128)(2,1)}) custom-call(s32[1]{0:T(128)} %get-tuple-element.60.refs_8_.refs_1_.refs_0_, s32[1]{0:T(128)} %get-tuple-element.61.refs_1_.refs_8_, s32[1]{0:T(128)} %get-tuple-element.64.refs_1_.refs_8_.refs_2_, s32[1]{0:T(128)} %get-tuple-element.65.refs_1_.refs_3_, ...), custom_call_target="tpu_custom_call" | custom-call | flops 81537269760 | bytes 8388608 | tf_op jit(solution)/shard_map/weight_grads/pallas_call | solution.py:533
  237.7 12.0 %weight_grads.5 = (s32[1]{0:T(128)}, bf16[2,768,768]{2,1,0:T(8,128)(2,1)}) custom-call(s32[1]{0:T(128)} %get-tuple-element.60.refs_8_.refs_1_.refs_0_, s32[1]{0:T(128)} %get-tuple-element.61.refs_1_.refs_8_, s32[1]{0:T(128)} %get-tuple-element.64.refs_1_.refs_8_.refs_2_, s32[1]{0:T(128)} %get-tuple-element.65.refs_1_.refs_3_, ...), custom_call_target="tpu_custom_call" | custom-call | flops 81537269760 | bytes 8388608 | tf_op jit(solution)/shard_map/weight_grads/pallas_call | solution.py:533
  265.5 2.9 add_convert_fusion
  270.6 11.2 %weight_grads.6 = (s32[1]{0:T(128)}, bf16[2,768,768]{2,1,0:T(8,128)(2,1)}) custom-call(s32[1]{0:T(128)} %get-tuple-element.60.refs_8_.refs_1_.refs_0_, s32[1]{0:T(128)} %get-tuple-element.61.refs_1_.refs_8_, s32[1]{0:T(128)} %get-tuple-element.64.refs_1_.refs_8_.refs_2_, s32[1]{0:T(128)} %get-tuple-element.65.refs_1_.refs_3_, ...), custom_call_target="tpu_custom_call" | custom-call | flops 81537269760 | bytes 8388608 | tf_op jit(solution)/shard_map/weight_grads/pallas_call | solution.py:533
  295.3 5.7 %collective-permute-done.32.refs_1_ = bf16[768,768]{1,0:T(8,128)(2,1)} collective-permute-done((bf16[768,768]{1,0:T(8,128)(2,1)}, bf16[768,768]{1,0:T(8,128)(2,1)}, u32[]{:S(2)}, u32[]{:S(2)}) %collective-permute-start.32) | collective-permute-done | bytes 1179680 | tf_op jit(solution)/shard_map/ppermute | solution.py:225
  301.0 17.3 %attend_back.1 = (bf16[3072,192]{1,0:T(8,128)(2,1)}, bf16[1024,768]{1,0:T(8,128)(2,1)}, f32[3,1280]{1,0:T(4,128)}) custom-call(bf16[3,1024,192]{2,1,0:T(8,128)(2,1)} %bitcast.74, bf16[1024,192]{1,0:T(8,128)(2,1)} %get-tuple-element.56.mixed_ref, bf16[1024,768]{1,0:T(8,128)(2,1)} %place.3.grad_ref, bf16[1024,768]{1,0:T(8,128)(2,1)} %copy-done.20, ...), custom_call_target="tpu_custom_call" | custom-call | flops 40265318400 | bytes 4194304 | tf_op jit(solution)/shard_map/attend_back/pallas_call | solution.py:182
  318.3 6.2 %collective-permute-done.48.refs_1_ = bf16[768,768]{1,0:T(8,128)(2,1)S(1)} collective-permute-done((bf16[768,768]{1,0:T(8,128)(2,1)}, bf16[768,768]{1,0:T(8,128)(2,1)S(1)}, u32[]{:S(2)}, u32[]{:S(2)}) %collective-permute-start.48) | collective-permute-done | bytes 1179680 | tf_op jit(solution)/shard_map/ppermute | solution.py:225
  328.1 3.6 all-to-all-start
  334.9 11.8 %weight_grads.7 = (s32[1]{0:T(128)}, f32[768,768]{1,0:T(8,128)}, f32[768,768]{1,0:T(8,128)}) custom-call(s32[1]{0:T(128)} %get-tuple-element.60.refs_8_.refs_1_.refs_0_, s32[1]{0:T(128)} %get-tuple-element.61.refs_1_.refs_8_, s32[1]{0:T(128)} %get-tuple-element.64.refs_1_.refs_8_.refs_2_, s32[1]{0:T(128)} %get-tuple-element.65.refs_1_.refs_3_, ...), custom_call_target="tpu_custom_call" | custom-call | flops 81537269760 | bytes 8388608 | tf_op jit(solution)/shard_map/weight_grads/pallas_call | solution.py:533
  354.5 4.7 %all-to-all-done = bf16[8,384,192]{1,2,0:T(8,128)(2,1)S(1)} async-done(((bf16[8,384,192]{1,2,0:T(8,128)(2,1)}), bf16[8,384,192]{1,2,0:T(8,128)(2,1)S(1)}, u32[]{:S(2)}, u32[]{:S(2)}) %all-to-all-start) | async-done | bytes 1179680 | tf_op jit(solution)/shard_map/all_to_all | solution.py:269
  364.5 3.9 all-to-all-start.1
  383.6 3.2 collective-permute-start.46
  390.6 7.1 %collective-permute-start.47 = (f32[22,768]{1,0:T(8,128)S(1)}, f32[22,768]{1,0:T(8,128)S(1)}, u32[]{:S(2)}, u32[]{:S(2)}) collective-permute-start(f32[22,768]{1,0:T(8,128)S(1)} %add.203), channel_id=1, source_target_pairs={{0,16},{4,20},{8,24},{12,28},{16,0},{20,4},{24,8},{28,12},{1,17},{... | collective-permute-start | bytes 202760 | tf_op jit(solution)/shard_map/ppermute | solution.py:225
  397.7 6.2 %fusion.4 = (f32[1,768,768]{2,1,0:T(8,128)}, f32[1,768,768]{2,1,0:T(8,128)}) fusion(f32[768,768]{1,0:T(8,128)} %get-tuple-element.101, bf16[768,768]{1,0:T(8,128)(2,1)S(1)} %copy-done.7, bf16[2,768,768]{2,1,0:T(8,128)(2,1)} %tie.59, bf16[768,768]{1,0:T(8,128)(2,1)} %collective-permute-done.32.refs_1_, f32[768,768]{1,0:T(8,128)} %get-tuple-element.99), kind=kLoop, calls=%fused_computation.8 | loop fusion | flops 4718592 | bytes 14155776 | tf_op jit(solution)/shard_map/broadcast_in_dim | solution.py:657
  (368 shorter events, 156.2 us)
Async XLA Ops:
  7.2 79.9 %all-gather.2.cloned.1.call-start = ((), (), s32[]{:S(2)}) async-start(), calls=%async_computation.2 | async-start | bytes 3538944 | tf_op jit(solution)/shard_map/all_gather | solution.py:833
  9.8 38.2 %collective-permute-start.2 = (bf16[192,768]{1,0:T(8,128)(2,1)S(1)}, bf16[192,768]{1,0:T(8,128)(2,1)}, u32[]{:S(2)}, u32[]{:S(2)}) collective-permute-start(bf16[192,768]{1,0:T(8,128)(2,1)S(1)} %copy-done.41), channel_id=1, source_target_pairs={{0,2},{1,3},{2,0},{3,1},{4,6},{5,7},{6,4},{7,5},{8,10},{9,11},{10,... | collective-permute-start | bytes 884744 | tf_op jit(solution)/shard_map/ppermute | solution.py:225
  12.7 43.5 %collective-permute-start.4 = (bf16[192,768]{1,0:T(8,128)(2,1)S(1)}, bf16[192,768]{1,0:T(8,128)(2,1)}, u32[]{:S(2)}, u32[]{:S(2)}) collective-permute-start(bf16[192,768]{1,0:T(8,128)(2,1)S(1)} %copy-done.41), channel_id=1, source_target_pairs={{0,1},{1,0},{2,3},{3,2},{4,5},{5,4},{6,7},{7,6},{8,9},{9,8},{10,11... | collective-permute-start | bytes 884744 | tf_op jit(solution)/shard_map/ppermute | solution.py:225
  12.7 32.4 %collective-permute-start = (bf16[768,768]{1,0:T(8,128)(2,1)}, bf16[768,768]{1,0:T(8,128)(2,1)}, u32[]{:S(2)}, u32[]{:S(2)}) collective-permute-start(bf16[768,768]{1,0:T(8,128)(2,1)} %bitcast.8.refs_0_), channel_id=1, source_target_pairs={{0,2},{1,3},{2,0},{3,1},{4,6},{5,7},{6,4},{7,5},{8,10},{9,11},{10,... | collective-permute-start | bytes 3538952 | tf_op jit(solution)/shard_map/ppermute | solution.py:225
  53.5 29.7 %collective-permute-start.10 = (bf16[768,768]{1,0:T(8,128)(2,1)}, bf16[768,768]{1,0:T(8,128)(2,1)}, u32[]{:S(2)}, u32[]{:S(2)}) collective-permute-start(bf16[768,768]{1,0:T(8,128)(2,1)} %tie.32.refs_1_), channel_id=1, source_target_pairs={{0,2},{1,3},{2,0},{3,1},{4,6},{5,7},{6,4},{7,5},{8,10},{9,11},{10,... | collective-permute-start | bytes 3538952 | tf_op jit(solution)/shard_map/ppermute | solution.py:225
  110.2 25.3 %collective-permute-start.15 = (bf16[272,768]{1,0:T(8,128)(2,1)S(1)}, bf16[272,768]{1,0:T(8,128)(2,1)}, u32[]{:S(2)}, u32[]{:S(2)}) collective-permute-start(bf16[272,768]{1,0:T(8,128)(2,1)S(1)} %copy-done.11), channel_id=1, source_target_pairs={{0,4},{4,0},{8,12},{12,8},{16,20},{20,16},{24,28},{28,24},{1,5},{5... | collective-permute-start | bytes 1253384 | tf_op jit(solution)/shard_map/ppermute | solution.py:225
  114.2 43.3 %collective-permute-start.14 = (bf16[528,768]{1,0:T(8,128)(2,1)}, bf16[528,768]{1,0:T(8,128)(2,1)}, u32[]{:S(2)}, u32[]{:S(2)}) collective-permute-start(bf16[528,768]{1,0:T(8,128)(2,1)} %get-tuple-element.59), channel_id=1, source_target_pairs={{0,4},{4,0},{8,12},{12,8},{16,20},{20,16},{24,28},{28,24},{1,5},{5... | collective-permute-start | bytes 2433032 | tf_op jit(solution)/shard_map/ppermute | solution.py:225
  132.3 30.9 %collective-permute-start.18 = (bf16[272,768]{1,0:T(8,128)(2,1)}, bf16[272,768]{1,0:T(8,128)(2,1)}, u32[]{:S(2)}, u32[]{:S(2)}) collective-permute-start(bf16[272,768]{1,0:T(8,128)(2,1)} %tie.37.near.refs_1_), channel_id=1, source_target_pairs={{0,4},{4,0},{8,12},{12,8},{16,20},{20,16},{24,28},{28,24},{1,5},{5... | collective-permute-start | bytes 1253384 | tf_op jit(solution)/shard_map/ppermute | solution.py:225
  133.5 26.9 %collective-permute-start.20 = (bf16[272,768]{1,0:T(8,128)(2,1)}, bf16[272,768]{1,0:T(8,128)(2,1)S(1)}, u32[]{:S(2)}, u32[]{:S(2)}) collective-permute-start(bf16[272,768]{1,0:T(8,128)(2,1)} %tie.39), channel_id=1, source_target_pairs={{0,24},{4,28},{8,16},{12,20},{16,8},{20,12},{24,0},{28,4},{1,25},{... | collective-permute-start | bytes 1253384 | tf_op jit(solution)/shard_map/ppermute | solution.py:225
  156.8 28.4 %collective-permute-start.16 = (bf16[528,768]{1,0:T(8,128)(2,1)}, bf16[528,768]{1,0:T(8,128)(2,1)S(1)}, u32[]{:S(2)}, u32[]{:S(2)}) collective-permute-start(bf16[528,768]{1,0:T(8,128)(2,1)} %get-tuple-element.63), channel_id=1, source_target_pairs={{0,4},{4,0},{8,12},{12,8},{16,20},{20,16},{24,28},{28,24},{1,5},{5... | collective-permute-start | bytes 2433032 | tf_op jit(solution)/shard_map/ppermute | solution.py:225
  161.9 26.2 %collective-permute-start.21 = (bf16[272,768]{1,0:T(8,128)(2,1)}, bf16[272,768]{1,0:T(8,128)(2,1)}, u32[]{:S(2)}, u32[]{:S(2)}) collective-permute-start(bf16[272,768]{1,0:T(8,128)(2,1)} %tie.40.near), channel_id=1, source_target_pairs={{0,4},{4,0},{8,12},{12,8},{16,20},{20,16},{24,28},{28,24},{1,5},{5... | collective-permute-start | bytes 1253384 | tf_op jit(solution)/shard_map/ppermute | solution.py:225
  184.3 29.3 %collective-permute-start.23 = (bf16[272,768]{1,0:T(8,128)(2,1)}, bf16[272,768]{1,0:T(8,128)(2,1)}, u32[]{:S(2)}, u32[]{:S(2)}) collective-permute-start(bf16[272,768]{1,0:T(8,128)(2,1)} %get-tuple-element.87), channel_id=1, source_target_pairs={{0,4},{4,0},{8,12},{12,8},{16,20},{20,16},{24,28},{28,24},{1,5},{5... | collective-permute-start | bytes 1253384 | tf_op jit(solution)/shard_map/ppermute | solution.py:225
  188.0 29.8 %collective-permute-start.19 = (bf16[528,768]{1,0:T(8,128)(2,1)S(1)}, bf16[528,768]{1,0:T(8,128)(2,1)S(1)}, u32[]{:S(2)}, u32[]{:S(2)}) collective-permute-start(bf16[528,768]{1,0:T(8,128)(2,1)S(1)} %add_convert_fusion.1.refs_9_), channel_id=1, source_target_pairs={{0,8},{4,12},{8,0},{12,4},{16,24},{20,28},{24,16},{28,20},{1,9},{5... | collective-permute-start | bytes 2433032 | tf_op jit(solution)/shard_map/ppermute | solution.py:225
  216.2 33.6 %collective-permute-start.26 = (bf16[272,768]{1,0:T(8,128)(2,1)}, bf16[272,768]{1,0:T(8,128)(2,1)}, u32[]{:S(2)}, u32[]{:S(2)}) collective-permute-start(bf16[272,768]{1,0:T(8,128)(2,1)} %add_convert_fusion.4.refs_21_), channel_id=1, source_target_pairs={{0,16},{4,20},{8,24},{12,28},{16,0},{20,4},{24,8},{28,12},{1,17},{... | collective-permute-start | bytes 1253384 | tf_op jit(solution)/shard_map/ppermute | solution.py:225
  230.4 34.4 %collective-permute-start.31 = (bf16[2,768,768]{2,1,0:T(8,128)(2,1)}, bf16[2,768,768]{2,1,0:T(8,128)(2,1)}, u32[]{:S(2)}, u32[]{:S(2)}) collective-permute-start(bf16[2,768,768]{2,1,0:T(8,128)(2,1)} %get-tuple-element.92), channel_id=1, source_target_pairs={{0,1},{1,0},{2,3},{3,2},{4,5},{5,4},{6,7},{7,6},{8,9},{9,8},{10,11... | collective-permute-start | bytes 7077896 | tf_op jit(solution)/shard_map/ppermute | solution.py:225
  253.8 93.7 %collective-permute-start.25 = (bf16[256,768]{1,0:T(8,128)(2,1)}, bf16[256,768]{1,0:T(8,128)(2,1)}, u32[]{:S(2)}, u32[]{:S(2)}) collective-permute-start(bf16[256,768]{1,0:T(8,128)(2,1)} %add_convert_fusion.6), channel_id=1, source_target_pairs={{0,16},{4,20},{8,24},{12,28},{16,0},{20,4},{24,8},{28,12},{1,17},{... | collective-permute-start | bytes 1179656 | tf_op jit(solution)/shard_map/ppermute | solution.py:225
  270.0 31.0 %collective-permute-start.32 = (bf16[768,768]{1,0:T(8,128)(2,1)}, bf16[768,768]{1,0:T(8,128)(2,1)}, u32[]{:S(2)}, u32[]{:S(2)}) collective-permute-start(bf16[768,768]{1,0:T(8,128)(2,1)} %get-tuple-element.173), channel_id=1, source_target_pairs={{0,2},{1,3},{2,0},{3,1},{4,6},{5,7},{6,4},{7,5},{8,10},{9,11},{10,... | collective-permute-start | bytes 3538952 | tf_op jit(solution)/shard_map/ppermute | solution.py:225
  284.6 62.9 %collective-permute-start.34 = (bf16[256,768]{1,0:T(8,128)(2,1)}, bf16[256,768]{1,0:T(8,128)(2,1)}, u32[]{:S(2)}, u32[]{:S(2)}) collective-permute-start(bf16[256,768]{1,0:T(8,128)(2,1)} %add_convert_fusion.5), channel_id=1, source_target_pairs={{0,24},{4,28},{8,16},{12,20},{16,8},{20,12},{24,0},{28,4},{1,25},{... | collective-permute-start | bytes 1179656 | tf_op jit(solution)/shard_map/ppermute | solution.py:225
  288.3 85.9 %collective-permute-start.49 = (bf16[2,768,768]{2,1,0:T(8,128)(2,1)}, bf16[2,768,768]{2,1,0:T(8,128)(2,1)}, u32[]{:S(2)}, u32[]{:S(2)}) collective-permute-start(bf16[2,768,768]{2,1,0:T(8,128)(2,1)} %get-tuple-element.100), channel_id=1, source_target_pairs={{0,1},{1,0},{2,3},{3,2},{4,5},{5,4},{6,7},{7,6},{8,9},{9,8},{10,11... | collective-permute-start | bytes 7077896 | tf_op jit(solution)/shard_map/ppermute | solution.py:225
  293.8 30.7 %collective-permute-start.48 = (bf16[768,768]{1,0:T(8,128)(2,1)}, bf16[768,768]{1,0:T(8,128)(2,1)S(1)}, u32[]{:S(2)}, u32[]{:S(2)}) collective-permute-start(bf16[768,768]{1,0:T(8,128)(2,1)} %tie.56), channel_id=1, source_target_pairs={{0,2},{1,3},{2,0},{3,1},{4,6},{5,7},{6,4},{7,5},{8,10},{9,11},{10,... | collective-permute-start | bytes 3538952 | tf_op jit(solution)/shard_map/ppermute | solution.py:225
  328.1 31.2 %all-to-all-start = ((bf16[8,384,192]{1,2,0:T(8,128)(2,1)}), bf16[8,384,192]{1,2,0:T(8,128)(2,1)S(1)}, u32[]{:S(2)}, u32[]{:S(2)}) async-start(bf16[8,384,192]{1,2,0:T(8,128)(2,1)} %copy.117), calls=%async_computation | async-start | bytes 2359296 | tf_op jit(solution)/shard_map/all_to_all | solution.py:269
  364.5 48.6 %all-to-all-start.1 = ((bf16[8,384,192]{1,2,0:T(8,128)(2,1)}), bf16[8,384,192]{1,2,0:T(8,128)(2,1)S(1)}, u32[]{:S(2)}, u32[]{:S(2)}) async-start(bf16[8,384,192]{1,2,0:T(8,128)(2,1)} %broadcast_in_dim.102), calls=%async_computation.1 | async-start | bytes 2359296 | tf_op jit(solution)/shard_map/all_to_all | solution.py:272
  374.2 29.7 %collective-permute-start.35 = (bf16[256,768]{1,0:T(8,128)(2,1)}, bf16[256,768]{1,0:T(8,128)(2,1)}, u32[]{:S(2)}, u32[]{:S(2)}) collective-permute-start(bf16[256,768]{1,0:T(8,128)(2,1)} %fusion.26.refs_0_), channel_id=1, source_target_pairs={{0,1},{1,0},{2,3},{3,2},{4,5},{5,4},{6,7},{7,6},{8,9},{9,8},{10,11... | collective-permute-start | bytes 1179656 | tf_op jit(solution)/shard_map/ppermute | solution.py:225
  374.2 29.7 %collective-permute-start.37 = (bf16[256,768]{1,0:T(8,128)(2,1)}, bf16[256,768]{1,0:T(8,128)(2,1)}, u32[]{:S(2)}, u32[]{:S(2)}) collective-permute-start(bf16[256,768]{1,0:T(8,128)(2,1)} %collective-permute-done.36.refs_2_), channel_id=1, source_target_pairs={{0,1},{1,0},{2,3},{3,2},{4,5},{5,4},{6,7},{7,6},{8,9},{9,8},{10,11... | collective-permute-start | bytes 1179656 | tf_op jit(solution)/shard_map/ppermute | solution.py:225
  (100 other events, 839.7 us)
Sparse Core Ops, SparseCore 0:
  14.7 67.4 all-gather.1

commit v3 on v2

--- a/solution.py
+++ b/solution.py
@@ -99,14 +99,13 @@
     sums_ref, back_ref, fold_ref = refs[tokens : tokens + 3]
     strip_ref, grad_strip, do_ref, dqkv_ref, dk_acc, dv_acc = refs[tokens + 3 :]
     length, width_all = qkv_ref.shape[1:]
-    model_width = normed_ref.shape[1]
     build_strips(lines_ref, strip_ref, heads, rows, length)
     scale = head_size ** (-0.5)
     grad_strip[...] = jnp.zeros_like(grad_strip)
     dk_acc[...] = jnp.zeros_like(dk_acc)
     dv_acc[...] = jnp.zeros_like(dv_acc)
     do_ref[...] = dot_nt(grad_ref[...], w_out_ref[...]).astype(LOW)
-    sums_ref[3 * model_width :] = dot_tn(grad_ref[...], mixed_ref[...]).astype(LOW)
+    sums_ref[3 * width_all :] = dot_tn(mixed_ref[...], grad_ref[...]).astype(LOW)
     for first in range(0, length, rows):
         width = first + rows
         query = qkv_ref[0, first:width, :]
@@ -134,8 +133,8 @@
     dqkv_ref[1] = dk_acc[...].astype(LOW)
     dqkv_ref[2] = dv_acc[...].astype(LOW)
     for c in range(3):
-        sums_ref[c * model_width : (c + 1) * model_width] = dot_tn(
-            normed_ref[...], dqkv_ref[c]
+        sums_ref[c * width_all : (c + 1) * width_all] = dot_tn(
+            dqkv_ref[c], normed_ref[...]
         ).astype(LOW)
     for first in range(0, length, rows):
         part = slice(first, first + rows)
@@ -183,7 +182,7 @@
         functools.partial(attend_back_kernel, heads, head_size, rows, len(tokens)),
         in_specs=[pl.BlockSpec(memory_space=pltpu.VMEM)] * len(operands) + [ANYWHERE] * len(tokens),
         out_shape=(
-            jax.ShapeDtypeStruct((4 * model_width, width), LOW),
+            jax.ShapeDtypeStruct((4 * width, model_width), LOW),
             jax.ShapeDtypeStruct((length, model_width), LOW),
             jax.ShapeDtypeStruct((heads, length + rows), WIDE),
         ),
@@ -864,8 +863,8 @@
     d_router = dot_tn(logit_grad, normed_two, PRECISE)
     done0, add_weights = finish_weights(block1, sums)
     sums = sum_expert(sums, done0)
-    d_qkv = sums[: 3 * model_width].reshape(3, model_width, width)
-    d_out = sums[3 * model_width :].T
+    d_qkv = sums[: 3 * width].reshape(3, width, model_width).transpose(0, 2, 1)
+    d_out = sums[3 * width :]
     quarters = [
         lax.dynamic_slice_in_dim(grad_one, (mine ^ r) * own, own, 0) for r in range(tensor_size)
     ]

time: 430 us -> 424 us (0.986)
  local copies, waits for them, and re-layouts: 48.8 us -> 41.7 us
  transfers between devices with their start and end apart: 53 -> 53, of which waited for: 13 -> 13; matrix products, arithmetic and copies ran while one was open for 17% -> 16% of each run, Pallas kernels for 38% -> 38%
where the time goes in v3:
time: 424 us; the launch traced here: 420 us
  Pallas kernels  182 us (43%)
  waiting for transfers between devices  72.6 us (17%)
  starting transfers between devices  59.4 us (14%)
  local copies, waits for them, and re-layouts  41.7 us (10%)
  other arithmetic  38.8 us (9%)
  between operations  15.7 us (4%)
  matrix products  9.97 us (2%)
    pallas_call x4, Pallas kernels, expert_chunk(): pl.pallas_call(functools.partial(expert_kernel, blocks, chunk, experts, l...  86.7 us
    ppermute x50, waiting for transfers between devices, swap(): return lax.ppermute(values, axis_name, [(i, i ^ bit) for i in range(size)])  67.9 us
    ppermute x50, starting transfers between devices, swap(): return lax.ppermute(values, axis_name, [(i, i ^ bit) for i in range(size)])  51.9 us
    pallas_call x4, Pallas kernels, weight_grads(): pl.pallas_call(functools.partial(weight_grad_kernel, chunks, block, len(t...  46.5 us
    unnamed x151, local copies, waits for them, and re-layouts  21.9 us
    pallas_call x1, Pallas kernels, attend_back(): pl.pallas_call(functools.partial(attend_back_kernel, heads, head_size, ro...  16.9 us
    pallas_call x1, Pallas kernels, attend(): pl.pallas_call(functools.partial(attend_kernel, heads, head_size, rows),...  13.6 us
    pallas_call x30, Pallas kernels, tie(): pl.pallas_call(kernel, out_shape=jax.ShapeDtypeStruct(values.shape, value...  10.1 us
  transfers between devices with their start and end apart: 53, of which 13 were waited for; matrix products, arithmetic and copies ran while one was open for 16% of the time, Pallas kernels for 38%

profile of v3, /device:TPU:0, one launch (start us, length us, event | category | flops | bytes accessed | tf_op | source)
XLA Modules:
  0.0 419.6 jit_solution(5450535866972223587)
XLA Ops:
  9.8 2.9 collective-permute-start.2
  23.1 13.6 %attend.1 = (bf16[1024,192]{1,0:T(8,128)(2,1)}, f32[1024,3]{1,0:T(8,128)}) custom-call(bf16[3,1024,192]{2,1,0:T(8,128)(2,1)} %bitcast.71, f32[3,1280]{1,0:T(4,128)} %fusion.7.lines_ref, s32[1024,1]{1,0:T(8,128)} %copy.70.ids_col, s32[1,1024]{1,0:T(1,128)} %bitcast.76), custom_call_target="tpu_custom_call" | custom-call | flops 40265318400 | bytes 4194304 | tf_op jit(solution)/shard_map/attend/pallas_call | solution.py:159
  40.5 4.6 %collective-permute-done.refs_0_ = bf16[768,768]{1,0:T(8,128)(2,1)} collective-permute-done((bf16[768,768]{1,0:T(8,128)(2,1)}, bf16[768,768]{1,0:T(8,128)(2,1)}, u32[]{:S(2)}, u32[]{:S(2)}) %collective-permute-start) | collective-permute-done | bytes 1179680 | tf_op jit(solution)/shard_map/ppermute | solution.py:224
  48.1 4.7 %collective-permute-done.1 = bf16[512,192]{1,0:T(8,128)(2,1)S(1)} collective-permute-done((bf16[512,192]{1,0:T(8,128)(2,1)}, bf16[512,192]{1,0:T(8,128)(2,1)S(1)}, u32[]{:S(2)}, u32[]{:S(2)}) %collective-permute-start.1) | collective-permute-done | bytes 196640 | tf_op jit(solution)/shard_map/ppermute | solution.py:224
  63.6 18.7 %collective-permute-done.11.refs_0_ = bf16[272,768]{1,0:T(8,128)(2,1)S(1)} collective-permute-done((bf16[272,768]{1,0:T(8,128)(2,1)S(1)}, bf16[272,768]{1,0:T(8,128)(2,1)S(1)}, u32[]{:S(2)}, u32[]{:S(2)}) %collective-permute-start.11) | collective-permute-done | bytes 417824 | tf_op jit(solution)/shard_map/ppermute | solution.py:224
  88.1 21.0 %expert_chunk.4 = (bf16[512,768]{1,0:T(8,128)(2,1)}, bf16[512,768]{1,0:T(8,128)(2,1)}, s32[1]{0:T(128)}, bf16[4,512,768]{2,1,0:T(8,128)(2,1)}, bf16[4,512,768]{2...) custom-call(s32[1]{0:T(128)} %bitcast.9.meta, bf16[272,768]{1,0:T(8,128)(2,1)} %copy-done.10, ...), custom_call_target="tpu_custom_call" | custom-call | flops 135895449600 | bytes 16777216 | tf_op jit(solution)/shard_map/expert_chunk/pallas_call | solution.py:432
  114.8 16.1 %collective-permute-done.17.refs_0_ = bf16[272,768]{1,0:T(8,128)(2,1)S(1)} collective-permute-done((bf16[272,768]{1,0:T(8,128)(2,1)}, bf16[272,768]{1,0:T(8,128)(2,1)S(1)}, u32[]{:S(2)}, u32[]{:S(2)}) %collective-permute-start.17) | collective-permute-done | bytes 417824 | tf_op jit(solution)/shard_map/ppermute | solution.py:224
  135.5 21.3 %expert_chunk.5 = (bf16[512,768]{1,0:T(8,128)(2,1)}, bf16[512,768]{1,0:T(8,128)(2,1)}, s32[1]{0:T(128)}, bf16[4,512,768]{2,1,0:T(8,128)(2,1)}, bf16[4,512,768]{2...) custom-call(s32[1]{0:T(128)} %bitcast.9.meta, bf16[272,768]{1,0:T(8,128)(2,1)} %tie.33.refs_1_.near, ...), custom_call_target="tpu_custom_call" | custom-call | flops 135895449600 | bytes 16777216 | tf_op jit(solution)/shard_map/expert_chunk/pallas_call | solution.py:432
  163.3 21.0 %expert_chunk.6 = (bf16[512,768]{1,0:T(8,128)(2,1)}, bf16[512,768]{1,0:T(8,128)(2,1)}, s32[1]{0:T(128)}, bf16[4,512,768]{2,1,0:T(8,128)(2,1)}, bf16[4,512,768]{2...) custom-call(s32[1]{0:T(128)} %bitcast.9.meta, ...), custom_call_target="tpu_custom_call" | custom-call | flops 135895449600 | bytes 16777216 | tf_op jit(solution)/shard_map/expert_chunk/pallas_call | solution.py:432
  188.6 23.4 %expert_chunk.7 = (bf16[512,768]{1,0:T(8,128)(2,1)}, bf16[512,768]{1,0:T(8,128)(2,1)}, s32[1]{0:T(128)}, bf16[4,512,768]{2,1,0:T(8,128)(2,1)}, bf16[4,512,768]{2...) custom-call(s32[1]{0:T(128)} %bitcast.9.meta, ...), custom_call_target="tpu_custom_call" | custom-call | flops 135895449600 | bytes 16777216 | tf_op jit(solution)/shard_map/expert_chunk/pallas_call | solution.py:432
  219.2 11.2 %weight_grads.4 = (s32[1]{0:T(128)}, bf16[2,768,768]{2,1,0:T(8,128)(2,1)}) custom-call(s32[1]{0:T(128)} %get-tuple-element.60.refs_8_.refs_1_.refs_0_, s32[1]{0:T(128)} %get-tuple-element.61.refs_1_.refs_8_, s32[1]{0:T(128)} %get-tuple-element.64.refs_1_.refs_8_.refs_2_, s32[1]{0:T(128)} %get-tuple-element.65.refs_1_.refs_3_, ...), custom_call_target="tpu_custom_call" | custom-call | flops 81537269760 | bytes 8388608 | tf_op jit(solution)/shard_map/weight_grads/pallas_call | solution.py:532
  237.9 12.1 %weight_grads.5 = (s32[1]{0:T(128)}, bf16[2,768,768]{2,1,0:T(8,128)(2,1)}) custom-call(s32[1]{0:T(128)} %get-tuple-element.60.refs_8_.refs_1_.refs_0_, s32[1]{0:T(128)} %get-tuple-element.61.refs_1_.refs_8_, s32[1]{0:T(128)} %get-tuple-element.64.refs_1_.refs_8_.refs_2_, s32[1]{0:T(128)} %get-tuple-element.65.refs_1_.refs_3_, ...), custom_call_target="tpu_custom_call" | custom-call | flops 81537269760 | bytes 8388608 | tf_op jit(solution)/shard_map/weight_grads/pallas_call | solution.py:532
  265.6 2.9 add_convert_fusion
  270.6 11.3 %weight_grads.6 = (s32[1]{0:T(128)}, bf16[2,768,768]{2,1,0:T(8,128)(2,1)}) custom-call(s32[1]{0:T(128)} %get-tuple-element.60.refs_8_.refs_1_.refs_0_, s32[1]{0:T(128)} %get-tuple-element.61.refs_1_.refs_8_, s32[1]{0:T(128)} %get-tuple-element.64.refs_1_.refs_8_.refs_2_, s32[1]{0:T(128)} %get-tuple-element.65.refs_1_.refs_3_, ...), custom_call_target="tpu_custom_call" | custom-call | flops 81537269760 | bytes 8388608 | tf_op jit(solution)/shard_map/weight_grads/pallas_call | solution.py:532
  295.1 5.9 %collective-permute-done.32.refs_1_ = bf16[768,768]{1,0:T(8,128)(2,1)} collective-permute-done((bf16[768,768]{1,0:T(8,128)(2,1)}, bf16[768,768]{1,0:T(8,128)(2,1)}, u32[]{:S(2)}, u32[]{:S(2)}) %collective-permute-start.32) | collective-permute-done | bytes 1179680 | tf_op jit(solution)/shard_map/ppermute | solution.py:224
  301.1 16.9 %attend_back.1 = (bf16[768,768]{1,0:T(8,128)(2,1)}, bf16[1024,768]{1,0:T(8,128)(2,1)}, f32[3,1280]{1,0:T(4,128)}) custom-call(bf16[3,1024,192]{2,1,0:T(8,128)(2,1)} %bitcast.72, bf16[1024,192]{1,0:T(8,128)(2,1)} %get-tuple-element.56.mixed_ref, bf16[1024,768]{1,0:T(8,128)(2,1)} %place.3.grad_ref, bf16[1024,768]{1,0:T(8,128)(2,1)} %copy-done.21, ...), custom_call_target="tpu_custom_call" | custom-call | flops 40265318400 | bytes 4194304 | tf_op jit(solution)/shard_map/attend_back/pallas_call | solution.py:181
  318.0 6.6 %collective-permute-done.48.refs_1_ = bf16[768,768]{1,0:T(8,128)(2,1)S(1)} collective-permute-done((bf16[768,768]{1,0:T(8,128)(2,1)}, bf16[768,768]{1,0:T(8,128)(2,1)S(1)}, u32[]{:S(2)}, u32[]{:S(2)}) %collective-permute-start.48) | collective-permute-done | bytes 1179680 | tf_op jit(solution)/shard_map/ppermute | solution.py:224
  325.6 3.6 all-to-all-start
  332.5 11.9 %weight_grads.7 = (s32[1]{0:T(128)}, f32[768,768]{1,0:T(8,128)}, f32[768,768]{1,0:T(8,128)}) custom-call(s32[1]{0:T(128)} %get-tuple-element.60.refs_8_.refs_1_.refs_0_, s32[1]{0:T(128)} %get-tuple-element.61.refs_1_.refs_8_, s32[1]{0:T(128)} %get-tuple-element.64.refs_1_.refs_8_.refs_2_, s32[1]{0:T(128)} %get-tuple-element.65.refs_1_.refs_3_, ...), custom_call_target="tpu_custom_call" | custom-call | flops 81537269760 | bytes 8388608 | tf_op jit(solution)/shard_map/weight_grads/pallas_call | solution.py:532
  352.1 4.7 %all-to-all-done.refs_0_ = bf16[8,96,768]{2,1,0:T(8,128)(2,1)S(1)} async-done(((bf16[8,96,768]{2,1,0:T(8,128)(2,1)}), bf16[8,96,768]{2,1,0:T(8,128)(2,1)S(1)}, u32[]{:S(2)}, u32[]{:S(2)}) %all-to-all-start) | async-done | bytes 1179680 | tf_op jit(solution)/shard_map/all_to_all | solution.py:268
  361.0 3.9 all-to-all-start.1
  380.1 4.4 %collective-permute-start.46 = (f32[22,768]{1,0:T(8,128)S(1)}, f32[22,768]{1,0:T(8,128)S(1)}, u32[]{:S(2)}, u32[]{:S(2)}) collective-permute-start(f32[22,768]{1,0:T(8,128)S(1)} %add.202), channel_id=1, source_target_pairs={{0,8},{4,12},{8,0},{12,4},{16,24},{20,28},{24,16},{28,20},{1,9},{5... | collective-permute-start | bytes 202760 | tf_op jit(solution)/shard_map/ppermute | solution.py:224
  388.3 6.5 %collective-permute-start.47 = (f32[22,768]{1,0:T(8,128)S(1)}, f32[22,768]{1,0:T(8,128)S(1)}, u32[]{:S(2)}, u32[]{:S(2)}) collective-permute-start(f32[22,768]{1,0:T(8,128)S(1)} %add.203), channel_id=1, source_target_pairs={{0,16},{4,20},{8,24},{12,28},{16,0},{20,4},{24,8},{28,12},{1,17},{... | collective-permute-start | bytes 202760 | tf_op jit(solution)/shard_map/ppermute | solution.py:224
  394.9 6.2 %fusion.4 = (f32[1,768,768]{2,1,0:T(8,128)}, f32[1,768,768]{2,1,0:T(8,128)}) fusion(f32[768,768]{1,0:T(8,128)} %get-tuple-element.101, bf16[768,768]{1,0:T(8,128)(2,1)S(1)} %copy-done.8, bf16[2,768,768]{2,1,0:T(8,128)(2,1)} %tie.59, bf16[768,768]{1,0:T(8,128)(2,1)} %collective-permute-done.32.refs_1_, f32[768,768]{1,0:T(8,128)} %get-tuple-element.99), kind=kLoop, calls=%fused_computation.8 | loop fusion | flops 4718592 | bytes 14155776 | tf_op jit(solution)/shard_map/broadcast_in_dim | solution.py:656
  (363 shorter events, 148.4 us)
Async XLA Ops:
  7.2 79.8 %all-gather.2.cloned.1.call-start = ((), (), s32[]{:S(2)}) async-start(), calls=%async_computation.2 | async-start | bytes 3538944 | tf_op jit(solution)/shard_map/all_gather | solution.py:832
  9.8 38.2 %collective-permute-start.2 = (bf16[192,768]{1,0:T(8,128)(2,1)S(1)}, bf16[192,768]{1,0:T(8,128)(2,1)}, u32[]{:S(2)}, u32[]{:S(2)}) collective-permute-start(bf16[192,768]{1,0:T(8,128)(2,1)S(1)} %copy-done.42), channel_id=1, source_target_pairs={{0,2},{1,3},{2,0},{3,1},{4,6},{5,7},{6,4},{7,5},{8,10},{9,11},{10,... | collective-permute-start | bytes 884744 | tf_op jit(solution)/shard_map/ppermute | solution.py:224
  12.7 43.5 %collective-permute-start.4 = (bf16[192,768]{1,0:T(8,128)(2,1)S(1)}, bf16[192,768]{1,0:T(8,128)(2,1)}, u32[]{:S(2)}, u32[]{:S(2)}) collective-permute-start(bf16[192,768]{1,0:T(8,128)(2,1)S(1)} %copy-done.42), channel_id=1, source_target_pairs={{0,1},{1,0},{2,3},{3,2},{4,5},{5,4},{6,7},{7,6},{8,9},{9,8},{10,11... | collective-permute-start | bytes 884744 | tf_op jit(solution)/shard_map/ppermute | solution.py:224
  12.7 32.4 %collective-permute-start = (bf16[768,768]{1,0:T(8,128)(2,1)}, bf16[768,768]{1,0:T(8,128)(2,1)}, u32[]{:S(2)}, u32[]{:S(2)}) collective-permute-start(bf16[768,768]{1,0:T(8,128)(2,1)} %bitcast.8.refs_0_), channel_id=1, source_target_pairs={{0,2},{1,3},{2,0},{3,1},{4,6},{5,7},{6,4},{7,5},{8,10},{9,11},{10,... | collective-permute-start | bytes 3538952 | tf_op jit(solution)/shard_map/ppermute | solution.py:224
  53.5 29.6 %collective-permute-start.10 = (bf16[768,768]{1,0:T(8,128)(2,1)}, bf16[768,768]{1,0:T(8,128)(2,1)}, u32[]{:S(2)}, u32[]{:S(2)}) collective-permute-start(bf16[768,768]{1,0:T(8,128)(2,1)} %tie.32.refs_1_), channel_id=1, source_target_pairs={{0,2},{1,3},{2,0},{3,1},{4,6},{5,7},{6,4},{7,5},{8,10},{9,11},{10,... | collective-permute-start | bytes 3538952 | tf_op jit(solution)/shard_map/ppermute | solution.py:224
  109.9 25.6 %collective-permute-start.15 = (bf16[272,768]{1,0:T(8,128)(2,1)S(1)}, bf16[272,768]{1,0:T(8,128)(2,1)}, u32[]{:S(2)}, u32[]{:S(2)}) collective-permute-start(bf16[272,768]{1,0:T(8,128)(2,1)S(1)} %copy-done.12), channel_id=1, source_target_pairs={{0,4},{4,0},{8,12},{12,8},{16,20},{20,16},{24,28},{28,24},{1,5},{5... | collective-permute-start | bytes 1253384 | tf_op jit(solution)/shard_map/ppermute | solution.py:224
  114.2 43.2 %collective-permute-start.14 = (bf16[528,768]{1,0:T(8,128)(2,1)}, bf16[528,768]{1,0:T(8,128)(2,1)}, u32[]{:S(2)}, u32[]{:S(2)}) collective-permute-start(bf16[528,768]{1,0:T(8,128)(2,1)} %get-tuple-element.59), channel_id=1, source_target_pairs={{0,4},{4,0},{8,12},{12,8},{16,20},{20,16},{24,28},{28,24},{1,5},{5... | collective-permute-start | bytes 2433032 | tf_op jit(solution)/shard_map/ppermute | solution.py:224
  132.3 31.0 %collective-permute-start.18 = (bf16[272,768]{1,0:T(8,128)(2,1)}, bf16[272,768]{1,0:T(8,128)(2,1)}, u32[]{:S(2)}, u32[]{:S(2)}) collective-permute-start(bf16[272,768]{1,0:T(8,128)(2,1)} %tie.37.near.refs_1_), channel_id=1, source_target_pairs={{0,4},{4,0},{8,12},{12,8},{16,20},{20,16},{24,28},{28,24},{1,5},{5... | collective-permute-start | bytes 1253384 | tf_op jit(solution)/shard_map/ppermute | solution.py:224
  133.4 26.9 %collective-permute-start.20 = (bf16[272,768]{1,0:T(8,128)(2,1)}, bf16[272,768]{1,0:T(8,128)(2,1)S(1)}, u32[]{:S(2)}, u32[]{:S(2)}) collective-permute-start(bf16[272,768]{1,0:T(8,128)(2,1)} %tie.39), channel_id=1, source_target_pairs={{0,24},{4,28},{8,16},{12,20},{16,8},{20,12},{24,0},{28,4},{1,25},{... | collective-permute-start | bytes 1253384 | tf_op jit(solution)/shard_map/ppermute | solution.py:224
  156.8 28.1 %collective-permute-start.16 = (bf16[528,768]{1,0:T(8,128)(2,1)}, bf16[528,768]{1,0:T(8,128)(2,1)S(1)}, u32[]{:S(2)}, u32[]{:S(2)}) collective-permute-start(bf16[528,768]{1,0:T(8,128)(2,1)} %get-tuple-element.63), channel_id=1, source_target_pairs={{0,4},{4,0},{8,12},{12,8},{16,20},{20,16},{24,28},{28,24},{1,5},{5... | collective-permute-start | bytes 2433032 | tf_op jit(solution)/shard_map/ppermute | solution.py:224
  161.7 26.1 %collective-permute-start.21 = (bf16[272,768]{1,0:T(8,128)(2,1)}, bf16[272,768]{1,0:T(8,128)(2,1)}, u32[]{:S(2)}, u32[]{:S(2)}) collective-permute-start(bf16[272,768]{1,0:T(8,128)(2,1)} %tie.40.near), channel_id=1, source_target_pairs={{0,4},{4,0},{8,12},{12,8},{16,20},{20,16},{24,28},{28,24},{1,5},{5... | collective-permute-start | bytes 1253384 | tf_op jit(solution)/shard_map/ppermute | solution.py:224
  184.3 29.2 %collective-permute-start.23 = (bf16[272,768]{1,0:T(8,128)(2,1)}, bf16[272,768]{1,0:T(8,128)(2,1)}, u32[]{:S(2)}, u32[]{:S(2)}) collective-permute-start(bf16[272,768]{1,0:T(8,128)(2,1)} %get-tuple-element.87), channel_id=1, source_target_pairs={{0,4},{4,0},{8,12},{12,8},{16,20},{20,16},{24,28},{28,24},{1,5},{5... | collective-permute-start | bytes 1253384 | tf_op jit(solution)/shard_map/ppermute | solution.py:224
  187.7 29.9 %collective-permute-start.19 = (bf16[528,768]{1,0:T(8,128)(2,1)S(1)}, bf16[528,768]{1,0:T(8,128)(2,1)S(1)}, u32[]{:S(2)}, u32[]{:S(2)}) collective-permute-start(bf16[528,768]{1,0:T(8,128)(2,1)S(1)} %add_convert_fusion.1.refs_9_), channel_id=1, source_target_pairs={{0,8},{4,12},{8,0},{12,4},{16,24},{20,28},{24,16},{28,20},{1,9},{5... | collective-permute-start | bytes 2433032 | tf_op jit(solution)/shard_map/ppermute | solution.py:224
  216.2 33.8 %collective-permute-start.26 = (bf16[272,768]{1,0:T(8,128)(2,1)}, bf16[272,768]{1,0:T(8,128)(2,1)}, u32[]{:S(2)}, u32[]{:S(2)}) collective-permute-start(bf16[272,768]{1,0:T(8,128)(2,1)} %add_convert_fusion.4.refs_21_), channel_id=1, source_target_pairs={{0,16},{4,20},{8,24},{12,28},{16,0},{20,4},{24,8},{28,12},{1,17},{... | collective-permute-start | bytes 1253384 | tf_op jit(solution)/shard_map/ppermute | solution.py:224
  230.4 34.5 %collective-permute-start.31 = (bf16[2,768,768]{2,1,0:T(8,128)(2,1)}, bf16[2,768,768]{2,1,0:T(8,128)(2,1)}, u32[]{:S(2)}, u32[]{:S(2)}) collective-permute-start(bf16[2,768,768]{2,1,0:T(8,128)(2,1)} %get-tuple-element.92), channel_id=1, source_target_pairs={{0,1},{1,0},{2,3},{3,2},{4,5},{5,4},{6,7},{7,6},{8,9},{9,8},{10,11... | collective-permute-start | bytes 7077896 | tf_op jit(solution)/shard_map/ppermute | solution.py:224
  254.0 91.2 %collective-permute-start.25 = (bf16[256,768]{1,0:T(8,128)(2,1)}, bf16[256,768]{1,0:T(8,128)(2,1)}, u32[]{:S(2)}, u32[]{:S(2)}) collective-permute-start(bf16[256,768]{1,0:T(8,128)(2,1)} %add_convert_fusion.6), channel_id=1, source_target_pairs={{0,16},{4,20},{8,24},{12,28},{16,0},{20,4},{24,8},{28,12},{1,17},{... | collective-permute-start | bytes 1179656 | tf_op jit(solution)/shard_map/ppermute | solution.py:224
  270.1 31.0 %collective-permute-start.32 = (bf16[768,768]{1,0:T(8,128)(2,1)}, bf16[768,768]{1,0:T(8,128)(2,1)}, u32[]{:S(2)}, u32[]{:S(2)}) collective-permute-start(bf16[768,768]{1,0:T(8,128)(2,1)} %get-tuple-element.113), channel_id=1, source_target_pairs={{0,2},{1,3},{2,0},{3,1},{4,6},{5,7},{6,4},{7,5},{8,10},{9,11},{10,... | collective-permute-start | bytes 3538952 | tf_op jit(solution)/shard_map/ppermute | solution.py:224
  284.8 60.4 %collective-permute-start.34 = (bf16[256,768]{1,0:T(8,128)(2,1)}, bf16[256,768]{1,0:T(8,128)(2,1)}, u32[]{:S(2)}, u32[]{:S(2)}) collective-permute-start(bf16[256,768]{1,0:T(8,128)(2,1)} %add_convert_fusion.5), channel_id=1, source_target_pairs={{0,24},{4,28},{8,16},{12,20},{16,8},{20,12},{24,0},{28,4},{1,25},{... | collective-permute-start | bytes 1179656 | tf_op jit(solution)/shard_map/ppermute | solution.py:224
  288.2 82.5 %collective-permute-start.49 = (bf16[2,768,768]{2,1,0:T(8,128)(2,1)}, bf16[2,768,768]{2,1,0:T(8,128)(2,1)}, u32[]{:S(2)}, u32[]{:S(2)}) collective-permute-start(bf16[2,768,768]{2,1,0:T(8,128)(2,1)} %get-tuple-element.100), channel_id=1, source_target_pairs={{0,1},{1,0},{2,3},{3,2},{4,5},{5,4},{6,7},{7,6},{8,9},{9,8},{10,11... | collective-permute-start | bytes 7077896 | tf_op jit(solution)/shard_map/ppermute | solution.py:224
  293.7 30.9 %collective-permute-start.48 = (bf16[768,768]{1,0:T(8,128)(2,1)}, bf16[768,768]{1,0:T(8,128)(2,1)S(1)}, u32[]{:S(2)}, u32[]{:S(2)}) collective-permute-start(bf16[768,768]{1,0:T(8,128)(2,1)} %tie.56), channel_id=1, source_target_pairs={{0,2},{1,3},{2,0},{3,1},{4,6},{5,7},{6,4},{7,5},{8,10},{9,11},{10,... | collective-permute-start | bytes 3538952 | tf_op jit(solution)/shard_map/ppermute | solution.py:224
  325.6 31.2 %all-to-all-start = ((bf16[8,96,768]{2,1,0:T(8,128)(2,1)}), bf16[8,96,768]{2,1,0:T(8,128)(2,1)S(1)}, u32[]{:S(2)}, u32[]{:S(2)}) async-start(bf16[8,96,768]{2,1,0:T(8,128)(2,1)} %bitcast.67), calls=%async_computation | async-start | bytes 2359296 | tf_op jit(solution)/shard_map/all_to_all | solution.py:268
  361.0 49.3 %all-to-all-start.1 = ((bf16[8,96,768]{2,1,0:T(8,128)(2,1)}), bf16[8,96,768]{2,1,0:T(8,128)(2,1)S(1)}, u32[]{:S(2)}, u32[]{:S(2)}) async-start(bf16[8,96,768]{2,1,0:T(8,128)(2,1)} %broadcast_in_dim.102), calls=%async_computation.1 | async-start | bytes 2359296 | tf_op jit(solution)/shard_map/all_to_all | solution.py:271
  370.8 30.4 %collective-permute-start.35 = (bf16[256,768]{1,0:T(8,128)(2,1)}, bf16[256,768]{1,0:T(8,128)(2,1)}, u32[]{:S(2)}, u32[]{:S(2)}) collective-permute-start(bf16[256,768]{1,0:T(8,128)(2,1)} %fusion.26.refs_0_), channel_id=1, source_target_pairs={{0,1},{1,0},{2,3},{3,2},{4,5},{5,4},{6,7},{7,6},{8,9},{9,8},{10,11... | collective-permute-start | bytes 1179656 | tf_op jit(solution)/shard_map/ppermute | solution.py:224
  370.8 30.3 %collective-permute-start.37 = (bf16[256,768]{1,0:T(8,128)(2,1)}, bf16[256,768]{1,0:T(8,128)(2,1)}, u32[]{:S(2)}, u32[]{:S(2)}) collective-permute-start(bf16[256,768]{1,0:T(8,128)(2,1)} %collective-permute-done.36.refs_2_), channel_id=1, source_target_pairs={{0,1},{1,0},{2,3},{3,2},{4,5},{5,4},{6,7},{7,6},{8,9},{9,8},{10,11... | collective-permute-start | bytes 1179656 | tf_op jit(solution)/shard_map/ppermute | solution.py:224
  (101 other events, 839.2 us)
Sparse Core Ops, SparseCore 0:
  14.7 67.0 all-gather.1

commit v4 on v3

--- a/solution.py
+++ b/solution.py
@@ -599,8 +599,7 @@
         back_near, arrived = backs[chunk]
         return (back_near.astype(WIDE) + tie(arrived, token).astype(WIDE)).astype(LOW)
 
-    chunk_step(0, [])
-    near[2] = tie(near[2], counts[0])
+    chunk_step(0, [far[1], near[2]])
     far.append(side_swap(near[2]))
     near.append(plane_swap(3, tie(payload, near[2])))
     chunk_step(1, [counts[0]])

time: 424 us -> 430 us (1.014)
  starting transfers between devices: 59.4 us -> 69.4 us
  Pallas kernels: 182 us -> 175 us
    all_to_all x2, starting transfers between devices: 7.51 us -> 16.3 us  [sum_expert(): lax.all_to_all(parts, 'expert', split_axis=0, concat_axis=0, tiled=True)]
    pallas_call x4, Pallas kernels: 86.7 us -> 81.1 us  [expert_chunk(): pl.pallas_call(functools.partial(expert_kernel, blocks, chunk, experts, l...]
    pallas_call x30 -> x29, Pallas kernels: 10.1 us -> 9.34 us  [tie(): pl.pallas_call(kernel, out_shape=jax.ShapeDtypeStruct(values.shape, value...]
  transfers between devices with their start and end apart: 53 -> 53, of which waited for: 13 -> 11; matrix products, arithmetic and copies ran while one was open for 16% -> 17% of each run, Pallas kernels for 38% -> 41%
where the time goes in v4:
time: 430 us; the launch traced here: 426 us
  Pallas kernels  175 us (41%)
  waiting for transfers between devices  74.9 us (17%)
  starting transfers between devices  69.4 us (16%)
  local copies, waits for them, and re-layouts  40.8 us (9%)
  other arithmetic  40.2 us (9%)
  between operations  15.6 us (4%)
  matrix products  9.96 us (2%)
    pallas_call x4, Pallas kernels, expert_chunk(): pl.pallas_call(functools.partial(expert_kernel, blocks, chunk, experts, l...  81.1 us
    ppermute x50, waiting for transfers between devices, swap(): return lax.ppermute(values, axis_name, [(i, i ^ bit) for i in range(size)])  70.4 us
    ppermute x50, starting transfers between devices, swap(): return lax.ppermute(values, axis_name, [(i, i ^ bit) for i in range(size)])  53 us
    pallas_call x4, Pallas kernels, weight_grads(): pl.pallas_call(functools.partial(weight_grad_kernel, chunks, block, len(t...  46.8 us
    unnamed x151, local copies, waits for them, and re-layouts  20.9 us
    pallas_call x1, Pallas kernels, attend_back(): pl.pallas_call(functools.partial(attend_back_kernel, heads, head_size, ro...  16.9 us
    all_to_all x2, starting transfers between devices, sum_expert(): lax.all_to_all(parts, 'expert', split_axis=0, concat_axis=0, tiled=True)  16.3 us
    pallas_call x1, Pallas kernels, attend(): pl.pallas_call(functools.partial(attend_kernel, heads, head_size, rows),...  13.6 us
  transfers between devices with their start and end apart: 53, of which 11 were waited for; matrix products, arithmetic and copies ran while one was open for 17% of the time, Pallas kernels for 41%

profile of v4, /device:TPU:0, one launch (start us, length us, event | category | flops | bytes accessed | tf_op | source)
XLA Modules:
  0.0 426.4 jit_solution(12035068519923167249)
XLA Ops:
  9.8 2.9 collective-permute-start.2
  23.1 13.6 %attend.1 = (bf16[1024,192]{1,0:T(8,128)(2,1)}, f32[1024,3]{1,0:T(8,128)}) custom-call(bf16[3,1024,192]{2,1,0:T(8,128)(2,1)} %bitcast.71, f32[3,1280]{1,0:T(4,128)} %fusion.7.lines_ref, s32[1024,1]{1,0:T(8,128)} %copy.69.ids_col, s32[1,1024]{1,0:T(1,128)} %bitcast.76), custom_call_target="tpu_custom_call" | custom-call | flops 40265318400 | bytes 4194304 | tf_op jit(solution)/shard_map/attend/pallas_call | solution.py:159
  40.5 4.6 %collective-permute-done.refs_0_ = bf16[768,768]{1,0:T(8,128)(2,1)} collective-permute-done((bf16[768,768]{1,0:T(8,128)(2,1)}, bf16[768,768]{1,0:T(8,128)(2,1)}, u32[]{:S(2)}, u32[]{:S(2)}) %collective-permute-start) | collective-permute-done | bytes 1179680 | tf_op jit(solution)/shard_map/ppermute | solution.py:224
  48.1 4.7 %collective-permute-done.1 = bf16[512,192]{1,0:T(8,128)(2,1)S(1)} collective-permute-done((bf16[512,192]{1,0:T(8,128)(2,1)}, bf16[512,192]{1,0:T(8,128)(2,1)S(1)}, u32[]{:S(2)}, u32[]{:S(2)}) %collective-permute-start.1) | collective-permute-done | bytes 196640 | tf_op jit(solution)/shard_map/ppermute | solution.py:224
  63.4 19.0 %collective-permute-done.11.refs_0_ = bf16[272,768]{1,0:T(8,128)(2,1)S(1)} collective-permute-done((bf16[272,768]{1,0:T(8,128)(2,1)S(1)}, bf16[272,768]{1,0:T(8,128)(2,1)S(1)}, u32[]{:S(2)}, u32[]{:S(2)}) %collective-permute-start.11) | collective-permute-done | bytes 417824 | tf_op jit(solution)/shard_map/ppermute | solution.py:224
  89.9 16.4 %collective-permute-done.15.refs_9_.near.refs_1_ = bf16[272,768]{1,0:T(8,128)(2,1)} collective-permute-done((bf16[272,768]{1,0:T(8,128)(2,1)}, bf16[272,768]{1,0:T(8,128)(2,1)}, u32[]{:S(2)}, u32[]{:S(2)}) %collective-permute-start.15) | collective-permute-done | bytes 417824 | tf_op jit(solution)/shard_map/ppermute | solution.py:224
  108.4 14.8 %expert_chunk.4 = (bf16[512,768]{1,0:T(8,128)(2,1)}, bf16[512,768]{1,0:T(8,128)(2,1)}, s32[1]{0:T(128)}, bf16[4,512,768]{2,1,0:T(8,128)(2,1)}, bf16[4,512,768]{2...) custom-call(s32[1]{0:T(128)} %bitcast.9.meta, bf16[272,768]{1,0:T(8,128)(2,1)} %copy-done.10, ...), custom_call_target="tpu_custom_call" | custom-call | flops 135895449600 | bytes 16777216 | tf_op jit(solution)/shard_map/expert_chunk/pallas_call | solution.py:432
  126.3 21.2 %expert_chunk.5 = (bf16[512,768]{1,0:T(8,128)(2,1)}, bf16[512,768]{1,0:T(8,128)(2,1)}, s32[1]{0:T(128)}, bf16[4,512,768]{2,1,0:T(8,128)(2,1)}, bf16[4,512,768]{2...) custom-call(s32[1]{0:T(128)} %bitcast.9.meta, bf16[272,768]{1,0:T(8,128)(2,1)} %tie.32.refs_1_.near, ...), custom_call_target="tpu_custom_call" | custom-call | flops 135895449600 | bytes 16777216 | tf_op jit(solution)/shard_map/expert_chunk/pallas_call | solution.py:432
  154.2 21.1 %expert_chunk.6 = (bf16[512,768]{1,0:T(8,128)(2,1)}, bf16[512,768]{1,0:T(8,128)(2,1)}, s32[1]{0:T(128)}, bf16[4,512,768]{2,1,0:T(8,128)(2,1)}, bf16[4,512,768]{2...) custom-call(s32[1]{0:T(128)} %bitcast.9.meta, ...), custom_call_target="tpu_custom_call" | custom-call | flops 135895449600 | bytes 16777216 | tf_op jit(solution)/shard_map/expert_chunk/pallas_call | solution.py:432
  180.7 23.9 %expert_chunk.7 = (bf16[512,768]{1,0:T(8,128)(2,1)}, bf16[512,768]{1,0:T(8,128)(2,1)}, s32[1]{0:T(128)}, bf16[4,512,768]{2,1,0:T(8,128)(2,1)}, bf16[4,512,768]{2...) custom-call(s32[1]{0:T(128)} %bitcast.9.meta, ...), custom_call_target="tpu_custom_call" | custom-call | flops 135895449600 | bytes 16777216 | tf_op jit(solution)/shard_map/expert_chunk/pallas_call | solution.py:432
  211.2 11.2 %weight_grads.4 = (s32[1]{0:T(128)}, bf16[2,768,768]{2,1,0:T(8,128)(2,1)}) custom-call(s32[1]{0:T(128)} %get-tuple-element.60.refs_8_.refs_0_, s32[1]{0:T(128)} %get-tuple-element.61.refs_1_.refs_8_, s32[1]{0:T(128)} %get-tuple-element.64.refs_1_.refs_8_.refs_2_, s32[1]{0:T(128)} %get-tuple-element.65.refs_1_.refs_3_, ...), custom_call_target="tpu_custom_call" | custom-call | flops 81537269760 | bytes 8388608 | tf_op jit(solution)/shard_map/weight_grads/pallas_call | solution.py:532
  227.1 12.3 %weight_grads.5 = (s32[1]{0:T(128)}, bf16[2,768,768]{2,1,0:T(8,128)(2,1)}) custom-call(s32[1]{0:T(128)} %get-tuple-element.60.refs_8_.refs_0_, s32[1]{0:T(128)} %get-tuple-element.61.refs_1_.refs_8_, s32[1]{0:T(128)} %get-tuple-element.64.refs_1_.refs_8_.refs_2_, s32[1]{0:T(128)} %get-tuple-element.65.refs_1_.refs_3_, ...), custom_call_target="tpu_custom_call" | custom-call | flops 81537269760 | bytes 8388608 | tf_op jit(solution)/shard_map/weight_grads/pallas_call | solution.py:532
  247.7 6.0 %collective-permute-done.33.refs_0_ = bf16[256,768]{1,0:T(8,128)(2,1)S(1)} collective-permute-done((bf16[256,768]{1,0:T(8,128)(2,1)}, bf16[256,768]{1,0:T(8,128)(2,1)S(1)}, u32[]{:S(2)}, u32[]{:S(2)}) %collective-permute-start.33) | collective-permute-done | bytes 393248 | tf_op jit(solution)/shard_map/ppermute | solution.py:224
  268.4 11.3 %weight_grads.6 = (s32[1]{0:T(128)}, bf16[2,768,768]{2,1,0:T(8,128)(2,1)}) custom-call(s32[1]{0:T(128)} %get-tuple-element.60.refs_8_.refs_0_, s32[1]{0:T(128)} %get-tuple-element.61.refs_1_.refs_8_, s32[1]{0:T(128)} %get-tuple-element.64.refs_1_.refs_8_.refs_2_, s32[1]{0:T(128)} %get-tuple-element.65.refs_1_.refs_3_, ...), custom_call_target="tpu_custom_call" | custom-call | flops 81537269760 | bytes 8388608 | tf_op jit(solution)/shard_map/weight_grads/pallas_call | solution.py:532
  292.6 6.2 %collective-permute-done.32.refs_1_ = bf16[768,768]{1,0:T(8,128)(2,1)} collective-permute-done((bf16[768,768]{1,0:T(8,128)(2,1)}, bf16[768,768]{1,0:T(8,128)(2,1)}, u32[]{:S(2)}, u32[]{:S(2)}) %collective-permute-start.32) | collective-permute-done | bytes 1179680 | tf_op jit(solution)/shard_map/ppermute | solution.py:224
  298.9 16.9 %attend_back.1 = (bf16[768,768]{1,0:T(8,128)(2,1)}, bf16[1024,768]{1,0:T(8,128)(2,1)}, f32[3,1280]{1,0:T(4,128)}) custom-call(bf16[3,1024,192]{2,1,0:T(8,128)(2,1)} %bitcast.72, bf16[1024,192]{1,0:T(8,128)(2,1)} %get-tuple-element.56.mixed_ref, bf16[1024,768]{1,0:T(8,128)(2,1)} %place.3.grad_ref, bf16[1024,768]{1,0:T(8,128)(2,1)} %copy-done.22, ...), custom_call_target="tpu_custom_call" | custom-call | flops 40265318400 | bytes 4194304 | tf_op jit(solution)/shard_map/attend_back/pallas_call | solution.py:181
  315.8 7.0 %collective-permute-done.48.refs_1_ = bf16[768,768]{1,0:T(8,128)(2,1)S(1)} collective-permute-done((bf16[768,768]{1,0:T(8,128)(2,1)}, bf16[768,768]{1,0:T(8,128)(2,1)S(1)}, u32[]{:S(2)}, u32[]{:S(2)}) %collective-permute-start.48) | collective-permute-done | bytes 1179680 | tf_op jit(solution)/shard_map/ppermute | solution.py:224
  323.8 12.4 %all-to-all-start = ((bf16[8,96,768]{2,1,0:T(8,128)(2,1)}), bf16[8,96,768]{2,1,0:T(8,128)(2,1)S(1)}, u32[]{:S(2)}, u32[]{:S(2)}) async-start(bf16[8,96,768]{2,1,0:T(8,128)(2,1)} %bitcast.67), calls=%async_computation | async-start | bytes 2359296 | tf_op jit(solution)/shard_map/all_to_all | solution.py:268
  339.4 12.0 %weight_grads.7 = (s32[1]{0:T(128)}, f32[768,768]{1,0:T(8,128)}, f32[768,768]{1,0:T(8,128)}) custom-call(s32[1]{0:T(128)} %get-tuple-element.60.refs_8_.refs_0_, s32[1]{0:T(128)} %get-tuple-element.61.refs_1_.refs_8_, s32[1]{0:T(128)} %get-tuple-element.64.refs_1_.refs_8_.refs_2_, s32[1]{0:T(128)} %get-tuple-element.65.refs_1_.refs_3_, ...), custom_call_target="tpu_custom_call" | custom-call | flops 81537269760 | bytes 8388608 | tf_op jit(solution)/shard_map/weight_grads/pallas_call | solution.py:532
  359.1 4.4 %all-to-all-done.refs_0_ = bf16[8,96,768]{2,1,0:T(8,128)(2,1)S(1)} async-done(((bf16[8,96,768]{2,1,0:T(8,128)(2,1)}), bf16[8,96,768]{2,1,0:T(8,128)(2,1)S(1)}, u32[]{:S(2)}, u32[]{:S(2)}) %all-to-all-start) | async-done | bytes 1179680 | tf_op jit(solution)/shard_map/all_to_all | solution.py:268
  367.8 3.9 all-to-all-start.1
  386.8 4.4 %collective-permute-start.46 = (f32[22,768]{1,0:T(8,128)S(1)}, f32[22,768]{1,0:T(8,128)S(1)}, u32[]{:S(2)}, u32[]{:S(2)}) collective-permute-start(f32[22,768]{1,0:T(8,128)S(1)} %add.202), channel_id=1, source_target_pairs={{0,8},{4,12},{8,0},{12,4},{16,24},{20,28},{24,16},{28,20},{1,9},{5... | collective-permute-start | bytes 202760 | tf_op jit(solution)/shard_map/ppermute | solution.py:224
  395.1 6.5 %collective-permute-start.47 = (f32[22,768]{1,0:T(8,128)S(1)}, f32[22,768]{1,0:T(8,128)S(1)}, u32[]{:S(2)}, u32[]{:S(2)}) collective-permute-start(f32[22,768]{1,0:T(8,128)S(1)} %add.203), channel_id=1, source_target_pairs={{0,16},{4,20},{8,24},{12,28},{16,0},{20,4},{24,8},{28,12},{1,17},{... | collective-permute-start | bytes 202760 | tf_op jit(solution)/shard_map/ppermute | solution.py:224
  401.6 6.2 %fusion.4 = (f32[1,768,768]{2,1,0:T(8,128)}, f32[1,768,768]{2,1,0:T(8,128)}) fusion(f32[768,768]{1,0:T(8,128)} %get-tuple-element.101, bf16[768,768]{1,0:T(8,128)(2,1)S(1)} %copy-done.8, bf16[2,768,768]{2,1,0:T(8,128)(2,1)} %tie.57, bf16[768,768]{1,0:T(8,128)(2,1)} %collective-permute-done.32.refs_1_, f32[768,768]{1,0:T(8,128)} %get-tuple-element.99), kind=kLoop, calls=%fused_computation.8 | loop fusion | flops 4718592 | bytes 14155776 | tf_op jit(solution)/shard_map/broadcast_in_dim | solution.py:655
  (362 shorter events, 147.6 us)
Async XLA Ops:
  7.2 100.5 %all-gather.2.cloned.1.call-start = ((), (), s32[]{:S(2)}) async-start(), calls=%async_computation.2 | async-start | bytes 3538944 | tf_op jit(solution)/shard_map/all_gather | solution.py:831
  9.8 38.2 %collective-permute-start.2 = (bf16[192,768]{1,0:T(8,128)(2,1)S(1)}, bf16[192,768]{1,0:T(8,128)(2,1)}, u32[]{:S(2)}, u32[]{:S(2)}) collective-permute-start(bf16[192,768]{1,0:T(8,128)(2,1)S(1)} %copy-done.42), channel_id=1, source_target_pairs={{0,2},{1,3},{2,0},{3,1},{4,6},{5,7},{6,4},{7,5},{8,10},{9,11},{10,... | collective-permute-start | bytes 884744 | tf_op jit(solution)/shard_map/ppermute | solution.py:224
  12.7 43.5 %collective-permute-start.4 = (bf16[192,768]{1,0:T(8,128)(2,1)S(1)}, bf16[192,768]{1,0:T(8,128)(2,1)}, u32[]{:S(2)}, u32[]{:S(2)}) collective-permute-start(bf16[192,768]{1,0:T(8,128)(2,1)S(1)} %copy-done.42), channel_id=1, source_target_pairs={{0,1},{1,0},{2,3},{3,2},{4,5},{5,4},{6,7},{7,6},{8,9},{9,8},{10,11... | collective-permute-start | bytes 884744 | tf_op jit(solution)/shard_map/ppermute | solution.py:224
  12.7 32.4 %collective-permute-start = (bf16[768,768]{1,0:T(8,128)(2,1)}, bf16[768,768]{1,0:T(8,128)(2,1)}, u32[]{:S(2)}, u32[]{:S(2)}) collective-permute-start(bf16[768,768]{1,0:T(8,128)(2,1)} %bitcast.8.refs_0_), channel_id=1, source_target_pairs={{0,2},{1,3},{2,0},{3,1},{4,6},{5,7},{6,4},{7,5},{8,10},{9,11},{10,... | collective-permute-start | bytes 3538952 | tf_op jit(solution)/shard_map/ppermute | solution.py:224
  53.5 29.7 %collective-permute-start.10 = (bf16[768,768]{1,0:T(8,128)(2,1)}, bf16[768,768]{1,0:T(8,128)(2,1)}, u32[]{:S(2)}, u32[]{:S(2)}) collective-permute-start(bf16[768,768]{1,0:T(8,128)(2,1)} %tie.31.refs_1_), channel_id=1, source_target_pairs={{0,2},{1,3},{2,0},{3,1},{4,6},{5,7},{6,4},{7,5},{8,10},{9,11},{10,... | collective-permute-start | bytes 3538952 | tf_op jit(solution)/shard_map/ppermute | solution.py:224
  63.2 44.5 %collective-permute-start.12 = (bf16[768,768]{1,0:T(8,128)(2,1)}, bf16[768,768]{1,0:T(8,128)(2,1)}, u32[]{:S(2)}, u32[]{:S(2)}) collective-permute-start(bf16[768,768]{1,0:T(8,128)(2,1)} %tie.29.refs_1_.refs_4_), channel_id=1, source_target_pairs={{0,1},{1,0},{2,3},{3,2},{4,5},{5,4},{6,7},{7,6},{8,9},{9,8},{10,11... | collective-permute-start | bytes 3538952 | tf_op jit(solution)/shard_map/ppermute | solution.py:224
  82.4 25.2 %collective-permute-start.9 = (bf16[768,768]{1,0:T(8,128)(2,1)}, bf16[768,768]{1,0:T(8,128)(2,1)}, u32[]{:S(2)}, u32[]{:S(2)}) collective-permute-start(bf16[768,768]{1,0:T(8,128)(2,1)} %tie.31.refs_1_), channel_id=1, source_target_pairs={{0,1},{1,0},{2,3},{3,2},{4,5},{5,4},{6,7},{7,6},{8,9},{9,8},{10,11... | collective-permute-start | bytes 3538952 | tf_op jit(solution)/shard_map/ppermute | solution.py:224
  106.3 47.9 %collective-permute-start.18 = (bf16[272,768]{1,0:T(8,128)(2,1)}, bf16[272,768]{1,0:T(8,128)(2,1)}, u32[]{:S(2)}, u32[]{:S(2)}) collective-permute-start(bf16[272,768]{1,0:T(8,128)(2,1)} %collective-permute-done.15.refs_9_.near.refs_1_), channel_id=1, source_target_pairs={{0,4},{4,0},{8,12},{12,8},{16,20},{20,16},{24,28},{28,24},{1,5},{5... | collective-permute-start | bytes 1253384 | tf_op jit(solution)/shard_map/ppermute | solution.py:224
  123.3 25.9 %collective-permute-start.20 = (bf16[272,768]{1,0:T(8,128)(2,1)}, bf16[272,768]{1,0:T(8,128)(2,1)}, u32[]{:S(2)}, u32[]{:S(2)}) collective-permute-start(bf16[272,768]{1,0:T(8,128)(2,1)} %tie.37), channel_id=1, source_target_pairs={{0,24},{4,28},{8,16},{12,20},{16,8},{20,12},{24,0},{28,4},{1,25},{... | collective-permute-start | bytes 1253384 | tf_op jit(solution)/shard_map/ppermute | solution.py:224
  125.8 24.6 %collective-permute-start.16 = (bf16[528,768]{1,0:T(8,128)(2,1)}, bf16[528,768]{1,0:T(8,128)(2,1)S(1)}, u32[]{:S(2)}, u32[]{:S(2)}) collective-permute-start(bf16[528,768]{1,0:T(8,128)(2,1)} %get-tuple-element.59), channel_id=1, source_target_pairs={{0,4},{4,0},{8,12},{12,8},{16,20},{20,16},{24,28},{28,24},{1,5},{5... | collective-permute-start | bytes 2433032 | tf_op jit(solution)/shard_map/ppermute | solution.py:224
  147.6 29.3 %collective-permute-start.17 = (bf16[528,768]{1,0:T(8,128)(2,1)}, bf16[528,768]{1,0:T(8,128)(2,1)S(1)}, u32[]{:S(2)}, u32[]{:S(2)}) collective-permute-start(bf16[528,768]{1,0:T(8,128)(2,1)} %get-tuple-element.63), channel_id=1, source_target_pairs={{0,4},{4,0},{8,12},{12,8},{16,20},{20,16},{24,28},{28,24},{1,5},{5... | collective-permute-start | bytes 2433032 | tf_op jit(solution)/shard_map/ppermute | solution.py:224
  149.8 30.9 %collective-permute-start.21 = (bf16[272,768]{1,0:T(8,128)(2,1)}, bf16[272,768]{1,0:T(8,128)(2,1)}, u32[]{:S(2)}, u32[]{:S(2)}) collective-permute-start(bf16[272,768]{1,0:T(8,128)(2,1)} %tie.38.near), channel_id=1, source_target_pairs={{0,4},{4,0},{8,12},{12,8},{16,20},{20,16},{24,28},{28,24},{1,5},{5... | collective-permute-start | bytes 1253384 | tf_op jit(solution)/shard_map/ppermute | solution.py:224
  175.3 29.9 %collective-permute-start.23 = (bf16[272,768]{1,0:T(8,128)(2,1)}, bf16[272,768]{1,0:T(8,128)(2,1)}, u32[]{:S(2)}, u32[]{:S(2)}) collective-permute-start(bf16[272,768]{1,0:T(8,128)(2,1)} %get-tuple-element.87), channel_id=1, source_target_pairs={{0,4},{4,0},{8,12},{12,8},{16,20},{20,16},{24,28},{28,24},{1,5},{5... | collective-permute-start | bytes 1253384 | tf_op jit(solution)/shard_map/ppermute | solution.py:224
  180.7 29.0 %collective-permute-start.19 = (bf16[528,768]{1,0:T(8,128)(2,1)}, bf16[528,768]{1,0:T(8,128)(2,1)S(1)}, u32[]{:S(2)}, u32[]{:S(2)}) collective-permute-start(bf16[528,768]{1,0:T(8,128)(2,1)} %add_convert_fusion.1.refs_9_), channel_id=1, source_target_pairs={{0,8},{4,12},{8,0},{12,4},{16,24},{20,28},{24,16},{28,20},{1,9},{5... | collective-permute-start | bytes 2433032 | tf_op jit(solution)/shard_map/ppermute | solution.py:224
  207.7 36.1 %collective-permute-start.26 = (bf16[272,768]{1,0:T(8,128)(2,1)}, bf16[272,768]{1,0:T(8,128)(2,1)}, u32[]{:S(2)}, u32[]{:S(2)}) collective-permute-start(bf16[272,768]{1,0:T(8,128)(2,1)} %add_convert_fusion.4.refs_21_), channel_id=1, source_target_pairs={{0,16},{4,20},{8,24},{12,28},{16,0},{20,4},{24,8},{28,12},{1,17},{... | collective-permute-start | bytes 1253384 | tf_op jit(solution)/shard_map/ppermute | solution.py:224
  247.7 104.5 %collective-permute-start.25 = (bf16[256,768]{1,0:T(8,128)(2,1)}, bf16[256,768]{1,0:T(8,128)(2,1)}, u32[]{:S(2)}, u32[]{:S(2)}) collective-permute-start(bf16[256,768]{1,0:T(8,128)(2,1)} %add_convert_fusion.6), channel_id=1, source_target_pairs={{0,16},{4,20},{8,24},{12,28},{16,0},{20,4},{24,8},{28,12},{1,17},{... | collective-permute-start | bytes 1179656 | tf_op jit(solution)/shard_map/ppermute | solution.py:224
  267.8 31.0 %collective-permute-start.32 = (bf16[768,768]{1,0:T(8,128)(2,1)}, bf16[768,768]{1,0:T(8,128)(2,1)}, u32[]{:S(2)}, u32[]{:S(2)}) collective-permute-start(bf16[768,768]{1,0:T(8,128)(2,1)} %get-tuple-element.113), channel_id=1, source_target_pairs={{0,2},{1,3},{2,0},{3,1},{4,6},{5,7},{6,4},{7,5},{8,10},{9,11},{10,... | collective-permute-start | bytes 3538952 | tf_op jit(solution)/shard_map/ppermute | solution.py:224
  282.6 69.6 %collective-permute-start.34 = (bf16[256,768]{1,0:T(8,128)(2,1)}, bf16[256,768]{1,0:T(8,128)(2,1)}, u32[]{:S(2)}, u32[]{:S(2)}) collective-permute-start(bf16[256,768]{1,0:T(8,128)(2,1)} %add_convert_fusion.5), channel_id=1, source_target_pairs={{0,24},{4,28},{8,16},{12,20},{16,8},{20,12},{24,0},{28,4},{1,25},{... | collective-permute-start | bytes 1179656 | tf_op jit(solution)/shard_map/ppermute | solution.py:224
  285.7 91.8 %collective-permute-start.49 = (bf16[2,768,768]{2,1,0:T(8,128)(2,1)}, bf16[2,768,768]{2,1,0:T(8,128)(2,1)}, u32[]{:S(2)}, u32[]{:S(2)}) collective-permute-start(bf16[2,768,768]{2,1,0:T(8,128)(2,1)} %get-tuple-element.100), channel_id=1, source_target_pairs={{0,1},{1,0},{2,3},{3,2},{4,5},{5,4},{6,7},{7,6},{8,9},{9,8},{10,11... | collective-permute-start | bytes 7077896 | tf_op jit(solution)/shard_map/ppermute | solution.py:224
  291.2 31.6 %collective-permute-start.48 = (bf16[768,768]{1,0:T(8,128)(2,1)}, bf16[768,768]{1,0:T(8,128)(2,1)S(1)}, u32[]{:S(2)}, u32[]{:S(2)}) collective-permute-start(bf16[768,768]{1,0:T(8,128)(2,1)} %tie.54), channel_id=1, source_target_pairs={{0,2},{1,3},{2,0},{3,1},{4,6},{5,7},{6,4},{7,5},{8,10},{9,11},{10,... | collective-permute-start | bytes 3538952 | tf_op jit(solution)/shard_map/ppermute | solution.py:224
  323.8 39.7 %all-to-all-start = ((bf16[8,96,768]{2,1,0:T(8,128)(2,1)}), bf16[8,96,768]{2,1,0:T(8,128)(2,1)S(1)}, u32[]{:S(2)}, u32[]{:S(2)}) async-start(bf16[8,96,768]{2,1,0:T(8,128)(2,1)} %bitcast.67), calls=%async_computation | async-start | bytes 2359296 | tf_op jit(solution)/shard_map/all_to_all | solution.py:268
  367.8 49.3 %all-to-all-start.1 = ((bf16[8,96,768]{2,1,0:T(8,128)(2,1)}), bf16[8,96,768]{2,1,0:T(8,128)(2,1)S(1)}, u32[]{:S(2)}, u32[]{:S(2)}) async-start(bf16[8,96,768]{2,1,0:T(8,128)(2,1)} %broadcast_in_dim.102), calls=%async_computation.1 | async-start | bytes 2359296 | tf_op jit(solution)/shard_map/all_to_all | solution.py:271
  377.5 30.3 %collective-permute-start.35 = (bf16[256,768]{1,0:T(8,128)(2,1)}, bf16[256,768]{1,0:T(8,128)(2,1)}, u32[]{:S(2)}, u32[]{:S(2)}) collective-permute-start(bf16[256,768]{1,0:T(8,128)(2,1)} %fusion.26.refs_0_), channel_id=1, source_target_pairs={{0,1},{1,0},{2,3},{3,2},{4,5},{5,4},{6,7},{7,6},{8,9},{9,8},{10,11... | collective-permute-start | bytes 1179656 | tf_op jit(solution)/shard_map/ppermute | solution.py:224
  377.6 30.3 %collective-permute-start.37 = (bf16[256,768]{1,0:T(8,128)(2,1)}, bf16[256,768]{1,0:T(8,128)(2,1)}, u32[]{:S(2)}, u32[]{:S(2)}) collective-permute-start(bf16[256,768]{1,0:T(8,128)(2,1)} %collective-permute-done.36.refs_2_), channel_id=1, source_target_pairs={{0,1},{1,0},{2,3},{3,2},{4,5},{5,4},{6,7},{7,6},{8,9},{9,8},{10,11... | collective-permute-start | bytes 1179656 | tf_op jit(solution)/shard_map/ppermute | solution.py:224
  (101 other events, 895.7 us)
Sparse Core Ops, SparseCore 0:
  14.7 66.9 all-gather.1
